TPU v7x, 512 devices: a whole 4x4x16 slice. The times are simulated.
512 devices in a mesh: tile: 128 (over y, z, core), chan: 4 (over x).
Axes of the slice: x: 4, y: 4, z: 16, core: 2. Of those that a mesh axis runs over, the one named last changes fastest.
Arguments:
- spectra: float32 [16384, 4096], P('tile', 'chan'), as said below
- feed_ids: int32 [16384], P('tile'), may hold values from 0 to 18
- feed_gain: float32 [19, 4096], P(None, 'chan'), may hold values from 0.1 to 1.9
- send_list: int32 [1024, 64], P('tile'), may hold values from 0 to 127, as said below
- send_count: int32 [1024], P('tile'), may hold values from 0 to 64, as said below
- kernel_weight: float32 [65536, 64], P('tile'), may hold values from 0 to 1.5
- pixel_block: int32 [65536], P('tile'), may hold values from 0 to 3
- beam_width: float32 [4096], P(('chan', 'tile')), may hold values from 1.5 to 12
Outputs:
- smoothed: float32 [4096, 256, 128], P(('chan', 'tile'))
Inputs may be any that keep to these rules, and one draw needn't show every extreme that they name: `send_count`: entry s * 8 + o is the number of samples that slab s sends to tile (s + o - 4) mod 128; in every draw some tile receives 64 from each of the 8 slabs that send to it. `send_list`: the 64 entries of a row are distinct. Positive spectra.
All inputs are finite; a program needn't handle non-finite values.
Results may differ from a plain program's by a relative error of at most 0.0003.
Values sent between devices are 32-bit elements; how exact they have to be, the bound alone decides.
No kernel may reach another device: no remote copies, remote signals or barrier semaphores. Data moves between devices by JAX's collectives and lax.ppermute only.
A program may use at most 64 MiB of HBM per device.

v0:
```python
import math

import jax
import jax.numpy as jnp
from jax import lax
from jax.sharding import PartitionSpec as P

CH = 4096
TY = 2
TX = 128


highest = lax.Precision.HIGHEST


def from_behind(array, axis, by):
    peers = lax.axis_size(axis)
    return lax.ppermute(array, axis, [(i, (i + by) % peers) for i in range(peers)])


def circular_response(beam_sigma, length):
    frequency = jnp.arange(length, dtype=jnp.int32)
    folded = jnp.minimum(frequency, length - frequency).astype(jnp.float32) / length
    return jnp.exp(-2.0 * math.pi**2 * beam_sigma[:, None] ** 2 * folded[None, :] ** 2)


def wave_tables(length):
    frequency = jnp.arange(length, dtype=jnp.int32)
    phases = (frequency[:, None] * frequency[None, :] % length).astype(jnp.float32) * (
        2.0 * math.pi / length
    )
    return (jnp.cos(phases), jnp.sin(phases))


def kernel_rows(response, length):
    cosines, sines = wave_tables(length)
    return jnp.dot(response, cosines, precision=highest) / length


def offset_table(length):
    frequency = jnp.arange(length, dtype=jnp.int32)
    return (frequency[:, None] - frequency[None, :]) % length


def local(
    spectra, feed_ids, feed_gain, send_list, send_count, kernel_weight, pixel_block, beam_width
):
    tile_count = lax.axis_size("tile")
    chan_width = spectra.shape[1]
    band_size = send_list.shape[0]
    capacity = send_list.shape[1]
    half_band = band_size // 2
    onehot = (feed_ids[:, None] == jnp.arange(feed_gain.shape[0], dtype=jnp.int32)[None, :]).astype(
        jnp.float32
    )
    gain_rows = jnp.dot(onehot, feed_gain, precision=highest)
    band_total = lax.psum(jnp.sum(spectra, axis=1), "chan")
    calibrated = gain_rows * spectra / (band_total / CH)[:, None]
    packed = calibrated[send_list.reshape(-1)].reshape(band_size, capacity, chan_width)
    counts_column = send_count.astype(jnp.float32).reshape(band_size, 1)
    blocks_in = []
    tallies_in = []
    for offset in range(band_size):
        shift_by = offset - half_band
        if shift_by == 0:
            block_here, tally_here = (packed[offset], counts_column[offset])
        else:
            block_here, tally_here = from_behind(
                (packed[offset], counts_column[offset]), "tile", shift_by
            )
        blocks_in.append(block_here)
        tallies_in.append(tally_here)
    arrived = jnp.stack(blocks_in)
    arrived_counts = jnp.stack(tallies_in)
    slot_number = band_size * capacity
    live_mask = (
        (jnp.arange(capacity, dtype=jnp.float32)[None, :] < arrived_counts)
        .reshape(-1)
        .astype(jnp.float32)
    )
    weights = kernel_weight * live_mask[:, None]
    block_width = kernel_weight.shape[1]
    pixels = TY * TX
    block_number = pixels // block_width
    selector = (pixel_block[None, :] == jnp.arange(block_number, dtype=jnp.int32)[:, None]).astype(
        jnp.float32
    )
    dense_weights = (selector[:, None, :] * weights.T[None, :, :]).reshape(pixels, slot_number)
    slot_rows = arrived.reshape(slot_number, chan_width)
    numerator = lax.dot_general(
        slot_rows, dense_weights, (((0,), (1,)), ((), ())), precision=highest
    )
    weight_sum = jnp.sum(dense_weights, axis=1)
    gridded = numerator / jnp.maximum(weight_sum, 1.0)[None, :]
    slab_width = chan_width // tile_count
    relaid = lax.all_to_all(
        gridded.reshape(tile_count, slab_width, pixels),
        "tile",
        split_axis=0,
        concat_axis=2,
        tiled=True,
    )
    row_length = tile_count * TY
    sky_image = relaid.reshape(slab_width, row_length, TX)
    row_gain = circular_response(beam_width, row_length)
    cosines, sines = wave_tables(row_length)
    real_part = (
        jnp.einsum("fi,cix->cfx", cosines, sky_image, precision=highest) * row_gain[:, :, None]
    )
    imag_part = (
        jnp.einsum("fi,cix->cfx", sines, sky_image, precision=highest) * row_gain[:, :, None]
    )
    along_rows = (
        jnp.einsum("fi,cfx->cix", cosines, real_part, precision=highest)
        + jnp.einsum("fi,cfx->cix", sines, imag_part, precision=highest)
    ) / row_length
    column_kernel = kernel_rows(circular_response(beam_width, TX), TX)
    column_matrix = column_kernel[:, offset_table(TX)]
    return jnp.einsum("cix,cxy->ciy", along_rows, column_matrix, precision=highest)


def solution(mesh):
    in_specs = (
        P("tile", "chan"),
        P("tile"),
        P(None, "chan"),
        P("tile", None),
        P("tile"),
        P("tile", None),
        P("tile"),
        P(("chan", "tile")),
    )
    out_specs = P(("chan", "tile"), None, None)
    return jax.shard_map(local, mesh=mesh, in_specs=in_specs, out_specs=out_specs, check_vma=False)
```

profile of v0, /device:TPU:1, one launch (start us, length us, event | category | flops | bytes accessed | tf_op | source)
XLA Modules:
  0.0 189.0 jit_solution(5555645520651449281)
XLA Ops:
  0.0 0.7 convert_element_type.48
  0.7 0.7 fusion.79
  1.4 6.3 %collective-permute-start.13 = (f32[1]{0:T(128)}, f32[1]{0:T(128)}, u32[]{:S(2)}, u32[]{:S(2)}) collective-permute-start(f32[1]{0:T(128)} %get-tuple-element.14), channel_id=1, source_target_pairs={{0,12},{4,16},{8,20},{12,24},{16,28},{20,32},{24,36},{28,40},{32,4... | collective-permute-start | bytes 20 | tf_op jit(solution)/shard_map/ppermute | solution.py:18
  7.6 3.5 %collective-permute-start.12 = (f32[1]{0:T(128)}, f32[1]{0:T(128)}, u32[]{:S(2)}, u32[]{:S(2)}) collective-permute-start(f32[1]{0:T(128)} %get-tuple-element.15), channel_id=1, source_target_pairs={{0,8},{4,12},{8,16},{12,20},{16,24},{20,28},{24,32},{28,36},{32,40... | collective-permute-start | bytes 20 | tf_op jit(solution)/shard_map/ppermute | solution.py:18
  11.2 2.2 %collective-permute-start.11 = (f32[1]{0:T(128)}, f32[1]{0:T(128)}, u32[]{:S(2)}, u32[]{:S(2)}) collective-permute-start(f32[1]{0:T(128)} %get-tuple-element.16), channel_id=1, source_target_pairs={{0,4},{4,8},{8,12},{12,16},{16,20},{20,24},{24,28},{28,32},{32,36}... | collective-permute-start | bytes 20 | tf_op jit(solution)/shard_map/ppermute | solution.py:18
  13.4 2.5 %collective-permute-start.10 = (f32[1]{0:T(128)}, f32[1]{0:T(128)}, u32[]{:S(2)}, u32[]{:S(2)}) collective-permute-start(f32[1]{0:T(128)} %get-tuple-element.18), channel_id=1, source_target_pairs={{0,508},{4,0},{8,4},{12,8},{16,12},{20,16},{24,20},{28,24},{32,28}... | collective-permute-start | bytes 20 | tf_op jit(solution)/shard_map/ppermute | solution.py:18
  15.9 8.2 %collective-permute-start.9 = (f32[1]{0:T(128)}, f32[1]{0:T(128)}, u32[]{:S(2)}, u32[]{:S(2)}) collective-permute-start(f32[1]{0:T(128)} %get-tuple-element.19), channel_id=1, source_target_pairs={{0,504},{4,508},{8,0},{12,4},{16,8},{20,12},{24,16},{28,20},{32,24... | collective-permute-start | bytes 20 | tf_op jit(solution)/shard_map/ppermute | solution.py:18
  24.1 1.2 reduce_sum.18
  25.3 8.5 %psum.7 = f32[128]{0:T(128)S(1)} all-reduce(f32[128]{0:T(128)S(1)} %reduce_sum.18), channel_id=1, replica_groups=mesh['tile'=128,'chan'=4] {'chan'}, use_global_device_ids=true, to_apply=%region_1.0 | all-reduce | flops 128 | bytes 1024 | tf_op jit(solution)/shard_map/psum | solution.py:57
  33.8 0.8 reshape.241
  34.5 0.7 fusion.46
  35.2 1.5 fusion.4
  36.7 1.9 %gather_fusion = f32[512,1024]{1,0:T(8,128)S(1)} fusion(f32[128,1024]{1,0:T(8,128)S(1)} %fusion.4, s32[1024]{0:T(1024)S(1)} %pad_clamp_fusion), kind=kCustom, calls=%fused_computation | custom fusion | bytes 4196352 | tf_op jit(solution)/shard_map/gather | solution.py:59
  38.7 1.0 fusion.78
  39.7 7.5 %collective-permute-start.8 = (f32[1]{0:T(128)}, f32[1]{0:T(128)}, u32[]{:S(2)}, u32[]{:S(2)}) collective-permute-start(f32[1]{0:T(128)} %get-tuple-element.20), channel_id=1, source_target_pairs={{0,500},{4,504},{8,508},{12,0},{16,4},{20,8},{24,12},{28,16},{32,2... | collective-permute-start | bytes 20 | tf_op jit(solution)/shard_map/ppermute | solution.py:18
  47.3 4.7 %collective-permute-start.7 = (f32[1]{0:T(128)}, f32[1]{0:T(128)}, u32[]{:S(2)}, u32[]{:S(2)}) collective-permute-start(f32[1]{0:T(128)} %get-tuple-element.21), channel_id=1, source_target_pairs={{0,496},{4,500},{8,504},{12,508},{16,0},{20,4},{24,8},{28,12},{32,... | collective-permute-start | bytes 20 | tf_op jit(solution)/shard_map/ppermute | solution.py:18
  52.0 1.9 %collective-permute-start.6 = (f32[64,1024]{1,0:T(8,128)S(1)}, f32[64,1024]{1,0:T(8,128)}, u32[]{:S(2)}, u32[]{:S(2)}) collective-permute-start(f32[64,1024]{1,0:T(8,128)S(1)} %get-tuple-element.5), channel_id=1, source_target_pairs={{0,12},{4,16},{8,20},{12,24},{16,28},{20,32},{24,36},{28,40},{32,4... | collective-permute-start | bytes 786440 | tf_op jit(solution)/shard_map/ppermute | solution.py:18
  54.0 1.9 %collective-permute-start.5 = (f32[64,1024]{1,0:T(8,128)S(1)}, f32[64,1024]{1,0:T(8,128)}, u32[]{:S(2)}, u32[]{:S(2)}) collective-permute-start(f32[64,1024]{1,0:T(8,128)S(1)} %get-tuple-element.6), channel_id=1, source_target_pairs={{0,8},{4,12},{8,16},{12,20},{16,24},{20,28},{24,32},{28,36},{32,40... | collective-permute-start | bytes 786440 | tf_op jit(solution)/shard_map/ppermute | solution.py:18
  55.9 2.0 %collective-permute-start.4 = (f32[64,1024]{1,0:T(8,128)S(1)}, f32[64,1024]{1,0:T(8,128)}, u32[]{:S(2)}, u32[]{:S(2)}) collective-permute-start(f32[64,1024]{1,0:T(8,128)S(1)} %get-tuple-element.7), channel_id=1, source_target_pairs={{0,4},{4,8},{8,12},{12,16},{16,20},{20,24},{24,28},{28,32},{32,36}... | collective-permute-start | bytes 786440 | tf_op jit(solution)/shard_map/ppermute | solution.py:18
  58.0 7.0 %collective-permute-start.1 = (f32[64,1024]{1,0:T(8,128)}, f32[64,1024]{1,0:T(8,128)}, u32[]{:S(2)}, u32[]{:S(2)}) collective-permute-start(f32[64,1024]{1,0:T(8,128)} %get-tuple-element.10), channel_id=1, source_target_pairs={{0,500},{4,504},{8,508},{12,0},{16,4},{20,8},{24,12},{28,16},{32,2... | collective-permute-start | bytes 786440 | tf_op jit(solution)/shard_map/ppermute | solution.py:18
  64.9 3.0 %collective-permute-start = (f32[64,1024]{1,0:T(8,128)}, f32[64,1024]{1,0:T(8,128)}, u32[]{:S(2)}, u32[]{:S(2)}) collective-permute-start(f32[64,1024]{1,0:T(8,128)} %get-tuple-element.11), channel_id=1, source_target_pairs={{0,496},{4,500},{8,504},{12,508},{16,0},{20,4},{24,8},{28,12},{32,... | collective-permute-start | bytes 786440 | tf_op jit(solution)/shard_map/ppermute | solution.py:18
  67.9 5.0 %stack.63 = f32[8,1]{0,1:T(1,128)S(1)} concatenate(f32[1,1]{0,1:T(1,128)} %bitcast.10, f32[1,1]{0,1:T(1,128)} %bitcast.11, f32[1,1]{0,1:T(1,128)} %bitcast.12, f32[1,1]{0,1:T(1,128)} %bitcast.13, f32[1,1]{0,1:T(1,128)} %bitcast.14, f32[1,1]{0,1:T(1,128)} %bitcast.15, f32[1,1]{0,1:T(1,128)} %bitcast.16, f32[1,1]{0,1:T(1,128)} %bitcast.17), dimensions={0} | concatenate | bytes 64 | tf_op jit(solution)/shard_map/stack | solution.py:74
  72.9 0.1 fusion.49
  73.0 0.1 reshape.245
  73.1 0.1 fusion.25
  73.2 0.1 max.15
  73.3 10.3 %collective-permute-done = f32[64,1024]{1,0:T(8,128)} collective-permute-done((f32[64,1024]{1,0:T(8,128)}, f32[64,1024]{1,0:T(8,128)}, u32[]{:S(2)}, u32[]{:S(2)}) %collective-permute-start) | collective-permute-done | bytes 262176 | tf_op jit(solution)/shard_map/ppermute | solution.py:18
  83.6 5.3 %collective-permute-start.2 = (f32[64,1024]{1,0:T(8,128)}, f32[64,1024]{1,0:T(8,128)S(1)}, u32[]{:S(2)}, u32[]{:S(2)}) collective-permute-start(f32[64,1024]{1,0:T(8,128)} %get-tuple-element.9), channel_id=1, source_target_pairs={{0,504},{4,508},{8,0},{12,4},{16,8},{20,12},{24,16},{28,20},{32,24... | collective-permute-start | bytes 786440 | tf_op jit(solution)/shard_map/ppermute | solution.py:18
  88.9 1.0 bitcast_dynamic-update-slice_fusion.6
  89.9 3.9 %collective-permute-start.3 = (f32[64,1024]{1,0:T(8,128)}, f32[64,1024]{1,0:T(8,128)S(1)}, u32[]{:S(2)}, u32[]{:S(2)}) collective-permute-start(f32[64,1024]{1,0:T(8,128)} %get-tuple-element.8), channel_id=1, source_target_pairs={{0,508},{4,0},{8,4},{12,8},{16,12},{20,16},{24,20},{28,24},{32,28}... | collective-permute-start | bytes 786440 | tf_op jit(solution)/shard_map/ppermute | solution.py:18
  93.8 1.0 bitcast_dynamic-update-slice_fusion.5
  94.8 3.0 %collective-permute-done.3 = f32[64,1024]{1,0:T(8,128)S(1)} collective-permute-done((f32[64,1024]{1,0:T(8,128)}, f32[64,1024]{1,0:T(8,128)S(1)}, u32[]{:S(2)}, u32[]{:S(2)}) %collective-permute-start.3) | collective-permute-done | bytes 262176 | tf_op jit(solution)/shard_map/ppermute | solution.py:18
  97.8 1.0 bitcast_dynamic-update-slice_fusion.2
  98.8 1.0 bitcast_dynamic-update-slice_fusion.1
  99.8 1.0 bitcast_dynamic-update-slice_fusion
  100.8 4.4 %fusion.3 = f32[128,8,256]{2,1,0:T(8,128)} fusion(f32[512,1024]{1,0:T(8,128)S(1)} %bitcast.72, f32[256,512]{1,0:T(8,128)S(1)} %bitcast.71, f32[256]{0:T(256)S(1)} %max.15), kind=kOutput, calls=%fused_computation.9 | convolution fusion | flops 1610874880 | bytes 3671040 | tf_op jit(solution)/shard_map/dot_general | solution.py:90
  105.2 10.8 %all-to-all-start = ((f32[128,8,256]{2,1,0:T(8,128)}), f32[128,8,256]{2,1,0:T(8,128)S(1)}, u32[]{:S(2)}, u32[]{:S(2)}) async-start(f32[128,8,256]{2,1,0:T(8,128)} %fusion.3), calls=%async_computation | async-start | bytes 2097152 | tf_op jit(solution)/shard_map/all_to_all | solution.py:96
  116.0 0.4 convolution_multiply_fusion.3
  116.4 0.1 copy.23
  116.6 54.4 %gather_fusion.1 = f32[16384,8]{1,0:T(8,128)} fusion(f32[8,128]{0,1:T(8,128)S(1)} %copy.23, s32[16384]{0:T(1024)S(1)} %fusion.33), kind=kCustom, calls=%fused_computation.1 | custom fusion | bytes 1114112 | tf_op jit(solution)/shard_map/gather | solution.py:118
  171.0 5.3 %copy.24 = f32[128,128,8]{1,0,2:T(8,128)S(1)} copy(f32[128,128,8]{2,1,0:T(8,128)} %bitcast.69) | data formatting | bytes 1048576 | tf_op jit(solution)/shard_map/gather | solution.py:118
  176.4 0.1 multiply_exponential_fusion
  176.5 0.3 copy.20
  176.9 2.6 %fusion.1 = f32[8,256,128]{1,2,0:T(8,128)S(1)} fusion(f32[8,256,128]{2,1,0:T(8,128)S(1)} %reshape.244, f32[8,256]{1,0:T(8,128)S(1)} %multiply_exponential_fusion), kind=kOutput, calls=%fused_computation.5 | convolution fusion | flops 806486016 | bytes 2105344 | tf_op jit(solution)/shard_map/fi,cix->cfx/dot_general | solution.py:111
  179.5 2.6 %fusion.2 = f32[8,256,128]{1,2,0:T(8,128)S(1)} fusion(f32[8,256,128]{2,1,0:T(8,128)S(1)} %reshape.244, f32[8,256]{1,0:T(8,128)S(1)} %multiply_exponential_fusion), kind=kOutput, calls=%fused_computation.7 | convolution fusion | flops 806486016 | bytes 2105344 | tf_op jit(solution)/shard_map/fi,cix->cfx/dot_general | solution.py:108
  182.1 2.0 %fusion.13 = f32[8,128,256]{2,1,0:T(8,128)S(1)} fusion(f32[8,256,128]{1,2,0:T(8,128)S(1)} %fusion.2), kind=kOutput, calls=%fused_computation.25 | convolution fusion | flops 806223872 | bytes 2097152 | tf_op jit(solution)/shard_map/fi,cfx->cix/dot_general | solution.py:114
  184.1 2.0 %fusion = f32[8,128,256]{2,1,0:T(8,128)S(1)} fusion(f32[8,128,256]{2,1,0:T(8,128)S(1)} %fusion.13, f32[8,256,128]{1,2,0:T(8,128)S(1)} %fusion.1), kind=kOutput, calls=%fused_computation.3 | convolution fusion | flops 806748160 | bytes 3145728 | tf_op jit(solution)/shard_map/fi,cfx->cix/dot_general | solution.py:115
  186.1 2.9 %fusion.5 = f32[8,256,128]{2,1,0:T(8,128)} fusion(f32[8,128,256]{2,1,0:T(8,128)S(1)} %fusion, f32[128,128,8]{1,0,2:T(8,128)S(1)} %copy.24), kind=kOutput, calls=%fused_computation.13 | convolution fusion | flops 402653184 | bytes 2621440 | tf_op jit(solution)/shard_map/cix,cxy->ciy/dot_general | solution.py:119
  (32 shorter events, 0.3 us)
Async XLA Ops:
  0.0 35.2 %copy-start = (f32[19,1024]{1,0:T(8,128)S(1)}, f32[19,1024]{1,0:T(8,128)}, u32[]{:S(2)}) copy-start(f32[19,1024]{1,0:T(8,128)} %param.10) | copy-start | bytes 233476
  1.4 38.4 %collective-permute-start.13 = (f32[1]{0:T(128)}, f32[1]{0:T(128)}, u32[]{:S(2)}, u32[]{:S(2)}) collective-permute-start(f32[1]{0:T(128)} %get-tuple-element.14), channel_id=1, source_target_pairs={{0,12},{4,16},{8,20},{12,24},{16,28},{20,32},{24,36},{28,40},{32,4... | collective-permute-start | bytes 20 | tf_op jit(solution)/shard_map/ppermute | solution.py:18
  7.6 39.6 %collective-permute-start.12 = (f32[1]{0:T(128)}, f32[1]{0:T(128)}, u32[]{:S(2)}, u32[]{:S(2)}) collective-permute-start(f32[1]{0:T(128)} %get-tuple-element.15), channel_id=1, source_target_pairs={{0,8},{4,12},{8,16},{12,20},{16,24},{20,28},{24,32},{28,36},{32,40... | collective-permute-start | bytes 20 | tf_op jit(solution)/shard_map/ppermute | solution.py:18
  11.2 40.8 %collective-permute-start.11 = (f32[1]{0:T(128)}, f32[1]{0:T(128)}, u32[]{:S(2)}, u32[]{:S(2)}) collective-permute-start(f32[1]{0:T(128)} %get-tuple-element.16), channel_id=1, source_target_pairs={{0,4},{4,8},{8,12},{12,16},{16,20},{20,24},{24,28},{28,32},{32,36}... | collective-permute-start | bytes 20 | tf_op jit(solution)/shard_map/ppermute | solution.py:18
  13.4 40.6 %collective-permute-start.10 = (f32[1]{0:T(128)}, f32[1]{0:T(128)}, u32[]{:S(2)}, u32[]{:S(2)}) collective-permute-start(f32[1]{0:T(128)} %get-tuple-element.18), channel_id=1, source_target_pairs={{0,508},{4,0},{8,4},{12,8},{16,12},{20,16},{24,20},{28,24},{32,28}... | collective-permute-start | bytes 20 | tf_op jit(solution)/shard_map/ppermute | solution.py:18
  15.9 40.0 %collective-permute-start.9 = (f32[1]{0:T(128)}, f32[1]{0:T(128)}, u32[]{:S(2)}, u32[]{:S(2)}) collective-permute-start(f32[1]{0:T(128)} %get-tuple-element.19), channel_id=1, source_target_pairs={{0,504},{4,508},{8,0},{12,4},{16,8},{20,12},{24,16},{28,20},{32,24... | collective-permute-start | bytes 20 | tf_op jit(solution)/shard_map/ppermute | solution.py:18
  38.6 34.4 %copy-start.1 = (f32[512,64]{0,1:T(8,128)S(1)}, f32[512,64]{0,1:T(8,128)}, u32[]{:S(2)}) copy-start(f32[512,64]{0,1:T(8,128)} %param.13) | copy-start | bytes 393220
  39.7 18.2 %collective-permute-start.8 = (f32[1]{0:T(128)}, f32[1]{0:T(128)}, u32[]{:S(2)}, u32[]{:S(2)}) collective-permute-start(f32[1]{0:T(128)} %get-tuple-element.20), channel_id=1, source_target_pairs={{0,500},{4,504},{8,508},{12,0},{16,4},{20,8},{24,12},{28,16},{32,2... | collective-permute-start | bytes 20 | tf_op jit(solution)/shard_map/ppermute | solution.py:18
  47.3 17.7 %collective-permute-start.7 = (f32[1]{0:T(128)}, f32[1]{0:T(128)}, u32[]{:S(2)}, u32[]{:S(2)}) collective-permute-start(f32[1]{0:T(128)} %get-tuple-element.21), channel_id=1, source_target_pairs={{0,496},{4,500},{8,504},{12,508},{16,0},{20,4},{24,8},{28,12},{32,... | collective-permute-start | bytes 20 | tf_op jit(solution)/shard_map/ppermute | solution.py:18
  52.0 47.8 %collective-permute-start.6 = (f32[64,1024]{1,0:T(8,128)S(1)}, f32[64,1024]{1,0:T(8,128)}, u32[]{:S(2)}, u32[]{:S(2)}) collective-permute-start(f32[64,1024]{1,0:T(8,128)S(1)} %get-tuple-element.5), channel_id=1, source_target_pairs={{0,12},{4,16},{8,20},{12,24},{16,28},{20,32},{24,36},{28,40},{32,4... | collective-permute-start | bytes 786440 | tf_op jit(solution)/shard_map/ppermute | solution.py:18
  54.0 44.8 %collective-permute-start.5 = (f32[64,1024]{1,0:T(8,128)S(1)}, f32[64,1024]{1,0:T(8,128)}, u32[]{:S(2)}, u32[]{:S(2)}) collective-permute-start(f32[64,1024]{1,0:T(8,128)S(1)} %get-tuple-element.6), channel_id=1, source_target_pairs={{0,8},{4,12},{8,16},{12,20},{16,24},{20,28},{24,32},{28,36},{32,40... | collective-permute-start | bytes 786440 | tf_op jit(solution)/shard_map/ppermute | solution.py:18
  55.9 41.9 %collective-permute-start.4 = (f32[64,1024]{1,0:T(8,128)S(1)}, f32[64,1024]{1,0:T(8,128)}, u32[]{:S(2)}, u32[]{:S(2)}) collective-permute-start(f32[64,1024]{1,0:T(8,128)S(1)} %get-tuple-element.7), channel_id=1, source_target_pairs={{0,4},{4,8},{8,12},{12,16},{16,20},{20,24},{24,28},{28,32},{32,36}... | collective-permute-start | bytes 786440 | tf_op jit(solution)/shard_map/ppermute | solution.py:18
  58.0 31.9 %collective-permute-start.1 = (f32[64,1024]{1,0:T(8,128)}, f32[64,1024]{1,0:T(8,128)}, u32[]{:S(2)}, u32[]{:S(2)}) collective-permute-start(f32[64,1024]{1,0:T(8,128)} %get-tuple-element.10), channel_id=1, source_target_pairs={{0,500},{4,504},{8,508},{12,0},{16,4},{20,8},{24,12},{28,16},{32,2... | collective-permute-start | bytes 786440 | tf_op jit(solution)/shard_map/ppermute | solution.py:18
  64.9 18.7 %collective-permute-start = (f32[64,1024]{1,0:T(8,128)}, f32[64,1024]{1,0:T(8,128)}, u32[]{:S(2)}, u32[]{:S(2)}) collective-permute-start(f32[64,1024]{1,0:T(8,128)} %get-tuple-element.11), channel_id=1, source_target_pairs={{0,496},{4,500},{8,504},{12,508},{16,0},{20,4},{24,8},{28,12},{32,... | collective-permute-start | bytes 786440 | tf_op jit(solution)/shard_map/ppermute | solution.py:18
  83.6 11.2 %collective-permute-start.2 = (f32[64,1024]{1,0:T(8,128)}, f32[64,1024]{1,0:T(8,128)S(1)}, u32[]{:S(2)}, u32[]{:S(2)}) collective-permute-start(f32[64,1024]{1,0:T(8,128)} %get-tuple-element.9), channel_id=1, source_target_pairs={{0,504},{4,508},{8,0},{12,4},{16,8},{20,12},{24,16},{28,20},{32,24... | collective-permute-start | bytes 786440 | tf_op jit(solution)/shard_map/ppermute | solution.py:18
  89.9 7.9 %collective-permute-start.3 = (f32[64,1024]{1,0:T(8,128)}, f32[64,1024]{1,0:T(8,128)S(1)}, u32[]{:S(2)}, u32[]{:S(2)}) collective-permute-start(f32[64,1024]{1,0:T(8,128)} %get-tuple-element.8), channel_id=1, source_target_pairs={{0,508},{4,0},{8,4},{12,8},{16,12},{20,16},{24,20},{28,24},{32,28}... | collective-permute-start | bytes 786440 | tf_op jit(solution)/shard_map/ppermute | solution.py:18
  105.2 10.8 %copy-start.2 = (f32[8]{0:T(128)S(1)}, f32[8]{0:T(128)}, u32[]{:S(2)}) copy-start(f32[8]{0:T(128)} %param.15) | copy-start | bytes 100
  105.2 71.3 %all-to-all-start = ((f32[128,8,256]{2,1,0:T(8,128)}), f32[128,8,256]{2,1,0:T(8,128)S(1)}, u32[]{:S(2)}, u32[]{:S(2)}) async-start(f32[128,8,256]{2,1,0:T(8,128)} %fusion.3), calls=%async_computation | async-start | bytes 2097152 | tf_op jit(solution)/shard_map/all_to_all | solution.py:96
where the time goes:
time: 190 us; the launch traced here: 189 us
  local copies, waits for them, and re-layouts  74.7 us (39%)
  starting transfers between devices  70.8 us (37%)
  matrix products  18.3 us (10%)
  waiting for transfers between devices  13.3 us (7%)
  blocking collectives  8.47 us (4%)
  other arithmetic  2.92 us (2%)
    ppermute x14, starting transfers between devices, from_behind(): lax.ppermute(array, axis, [(i, (i + by) % peers) for i in range(peers)])  60 us
    gather x2, local copies, waits for them, and re-layouts, local(): column_matrix = column_kernel[:, offset_table(TX)]  59.8 us
    ppermute x14, waiting for transfers between devices, from_behind(): lax.ppermute(array, axis, [(i, (i + by) % peers) for i in range(peers)])  13.3 us
    all_to_all x1, starting transfers between devices, local(): lax.all_to_all(gridded.reshape(tile_count, slab_width, pixels), 'tile', s...  10.8 us
    psum x1, blocking collectives, local(): band_total = lax.psum(jnp.sum(spectra, axis=1), 'chan')  8.47 us
    another operation x1, local copies, waits for them, and re-layouts, local(): arrived_counts = jnp.stack(tallies_in)  5 us
    dot_general x1, matrix products, local(): lax.dot_general(slot_rows, dense_weights, (((0,), (1,)), ((), ())), preci...  4.4 us
    unnamed x13, local copies, waits for them, and re-layouts  3.95 us
  transfers between devices with their start and end apart: 15, of which 2 were waited for; matrix products, arithmetic and copies ran while one was open for 41% of the time, Pallas kernels for 0%

commit v1 on v0

v1 whole, which is shorter than its diff:
```python
import math

import jax
import jax.numpy as jnp
from jax import lax
from jax.experimental import pallas as pl
from jax.experimental.pallas import tpu as pltpu
from jax.sharding import Mesh
from jax.sharding import PartitionSpec as P

CH = 4096
TY = 2
TX = 128
CORES = 2
ROWS_Z = 16
SLAB = 128
BAND = 8
CAP = 64
KB = 64
HALF_CH = 512
META = 8
UNIT = HALF_CH + META
REACH = 9
PIX = TY * TX

f32 = jnp.float32
bf16 = jnp.bfloat16
highest = lax.Precision.HIGHEST
VMEM = pltpu.VMEM


def whole(memory_space=VMEM):
    return pl.BlockSpec(memory_space=memory_space)


def split(value):
    high = value.astype(bf16)
    return high, (value - high.astype(f32)).astype(bf16)


def prepare_kernel(
    spectra, feed_ids, feed_gain, send_list, counts, weights, blocks, unit, packed, gains
):
    feeds = feed_gain.shape[0]
    gains[...] = jnp.zeros_like(gains)
    gains[0:feeds, :] = feed_gain[...]
    onehot = (
        lax.broadcasted_iota(jnp.int32, (gains.shape[0], SLAB), 0) == feed_ids[...]
    ).astype(f32)
    gain_rows = lax.dot_general(
        gains[...], onehot, (((0,), (0,)), ((), ())), precision=highest, preferred_element_type=f32
    )
    raw = spectra[...].T
    band_sum = jnp.sum(raw, axis=0, keepdims=True)
    scaled = (raw * gain_rows).reshape(HALF_CH // 8, CORES, 8, SLAB)
    lane = lax.broadcasted_iota(jnp.int32, (1, CAP), 1)
    rows = []
    for row in range(BAND):
        rows.append(
            jnp.where(lane < counts[row], send_list[row : row + 1, :], -1).astype(f32)
        )
    rows = [jnp.concatenate(rows[2 * m : 2 * m + 2], axis=1) for m in range(BAND // 2)]
    meta = jnp.concatenate(rows + [band_sum, jnp.zeros((META - BAND // 2 - 1, SLAB), f32)], axis=0)
    for core in range(CORES):
        unit[core, 0:HALF_CH, :] = scaled[:, core].reshape(HALF_CH, SLAB)
        unit[core, HALF_CH:UNIT, :] = meta
    wide = jnp.concatenate([weights[...], jnp.zeros((BAND * CAP, KB), f32)], axis=1)
    packed[0:KB, :] = wide.T[0:KB, :]
    packed[KB : KB + 8, :] = jnp.broadcast_to(blocks[...].astype(f32), (8, BAND * CAP))


def prepare(spectra, feed_ids, feed_gain, send_list, send_count, kernel_weight, pixel_block):
    slots = BAND * CAP
    return pl.pallas_call(
        prepare_kernel,
        out_shape=(
            jax.ShapeDtypeStruct((CORES, UNIT, SLAB), f32),
            jax.ShapeDtypeStruct((KB + 8, slots), f32),
        ),
        in_specs=[
            whole(),
            whole(),
            whole(),
            whole(),
            whole(pltpu.SMEM),
            whole(),
            whole(),
        ],
        out_specs=(whole(), whole()),
        scratch_shapes=[VMEM((24, spectra.shape[1]), f32)],
        compiler_params=pltpu.CompilerParams(vmem_limit_bytes=24 << 20),
        name="prepare",
    )(
        spectra,
        feed_ids.reshape(1, SLAB),
        feed_gain,
        send_list,
        send_count,
        kernel_weight,
        pixel_block.reshape(1, slots),
    )


def grid_kernel(
    core, below2, below1, here, above1, above2, sum_b2, sum_b1, sum_h, sum_a1, sum_a2,
    packed_own, packed_other, out, left, right, dense,
):
    me = core[0]
    for tile in range(CORES):
        pack = jnp.where(me == tile, packed_own[...], packed_other[...])
        weight = pack[0:KB, :]
        block = pack[KB : KB + 1, :]
        for number in range(PIX // KB):
            high, low = split(jnp.where(block == number, weight, 0.0))
            dense[tile, number * KB : (number + 1) * KB, :] = high
            dense[tile, PIX + number * KB : PIX + (number + 1) * KB, :] = low
    slabs = [
        (below2, None, sum_b2, 0),
        (below1, 0, sum_b1, 0),
        (below1, 1, sum_b1, 1),
        (here, 0, sum_h, 0),
        (here, 1, sum_h, 1),
        (above1, 0, sum_a1, 0),
        (above1, 1, sum_a1, 1),
        (above2, 0, sum_a2, 0),
        (above2, 1, sum_a2, 1),
    ]
    depth = REACH * SLAB
    totals = [jnp.zeros((1, PIX), f32) for _ in range(CORES)]
    sample = lax.broadcasted_iota(jnp.int32, (SLAB, SLAB), 0).astype(f32)
    lane = lax.broadcasted_iota(jnp.int32, (SLAB, SLAB), 1)
    for index, (ref, part, sums, row) in enumerate(slabs):
        unit = ref if part is None else ref.at[part]
        scale = CH / sums[row : row + 1, :]
        high, low = split(unit[0:HALF_CH, :] * scale)
        at = index * SLAB
        left[:, at : at + SLAB] = high
        left[:, depth + at : depth + at + SLAB] = low
        left[:, 2 * depth + at : 2 * depth + at + SLAB] = high
        for tile in range(CORES):
            offset = tile + BAND - 1 - index
            columns = slice(tile * PIX, (tile + 1) * PIX)
            if not 0 <= offset < BAND:
                for copy in range(3):
                    start = copy * depth + at
                    right[start : start + SLAB, columns] = jnp.zeros((SLAB, PIX), bf16)
                continue
            pair = offset // 2
            chosen = unit[HALF_CH + pair : HALF_CH + pair + 1, :]
            hot = ((sample == chosen) & ((lane // CAP) == offset % 2)).astype(f32).astype(bf16)
            picked = lax.dot_general(
                hot,
                dense[tile, :, pair * SLAB : (pair + 1) * SLAB],
                (((1,), (1,)), ((), ())),
                preferred_element_type=f32,
            )
            top, rest = picked[:, 0:PIX], picked[:, PIX:]
            totals[tile] = totals[tile] + jnp.sum(top + rest, axis=0, keepdims=True)
            top, rest = top.astype(bf16), rest.astype(bf16)
            right[at : at + SLAB, columns] = top
            right[depth + at : depth + at + SLAB, columns] = top
            right[2 * depth + at : 2 * depth + at + SLAB, columns] = rest
    total = jnp.maximum(jnp.concatenate(totals, axis=1), 1.0)
    tiles = jnp.dot(left[...], right[...], preferred_element_type=f32) / total
    for row in range(CORES * TY):
        out[:, row] = tiles[:, row * TX : (row + 1) * TX].reshape(HALF_CH // 8, 8, TX)


def grid_tiles(core, units, sums, packed_own, packed_other):
    slots = BAND * CAP
    depth = REACH * SLAB
    return pl.pallas_call(
        grid_kernel,
        out_shape=jax.ShapeDtypeStruct((HALF_CH // 8, CORES * TY, 8, TX), f32),
        in_specs=[whole(pltpu.SMEM)] + [whole()] * 12,
        out_specs=whole(),
        scratch_shapes=[
            VMEM((HALF_CH, 3 * depth), bf16),
            VMEM((3 * depth, CORES * PIX), bf16),
            VMEM((CORES, 2 * PIX, slots), bf16),
        ],
        compiler_params=pltpu.CompilerParams(vmem_limit_bytes=32 << 20),
        name="grid_tiles",
    )(core, *units, *sums, packed_own, packed_other)


def waves(length):
    frequency = jnp.arange(length, dtype=jnp.int32)
    phases = (frequency[:, None] * frequency[None, :] % length).astype(f32) * (
        2.0 * math.pi / length
    )
    return jnp.concatenate([jnp.cos(phases), jnp.sin(phases)], axis=1)


def response(sigma, length):
    frequency = lax.broadcasted_iota(jnp.int32, (1, 2 * length), 1) % length
    folded = jnp.minimum(frequency, length - frequency).astype(f32) / length
    return jnp.exp(-2.0 * math.pi**2 * sigma**2 * folded**2)


def circulant(sigma, basis):
    length = basis.shape[0]
    return (
        lax.dot_general(
            basis * response(sigma, length),
            basis,
            (((1,), (1,)), ((), ())),
            precision=highest,
            preferred_element_type=f32,
        )
        / length
    )


def tables_kernel(sigma, row_waves, column_waves, rows_out, columns_out):
    width = sigma[pl.program_id(0)]
    high, low = split(circulant(width, row_waves[...]))
    size = high.shape[0]
    rows_out[0, :, 0:size] = high
    rows_out[0, :, size : 2 * size] = high
    rows_out[0, :, 2 * size : 3 * size] = low
    high, low = split(circulant(width, column_waves[...]))
    columns_out[0, 0:TX, :] = high
    columns_out[0, TX : 2 * TX, :] = high
    columns_out[0, 2 * TX : 3 * TX, :] = low


def make_tables(sigma, length):
    channels = sigma.shape[0]
    waves_rows = waves(length)
    fixed = lambda shape: pl.BlockSpec(shape, lambda c: (0, 0))
    return pl.pallas_call(
        tables_kernel,
        grid=(channels,),
        out_shape=(
            jax.ShapeDtypeStruct((channels, length, 3 * length), bf16),
            jax.ShapeDtypeStruct((channels, 3 * TX, TX), bf16),
        ),
        in_specs=[
            whole(pltpu.SMEM),
            fixed((length, 2 * length)),
            fixed((TX, 2 * TX)),
        ],
        out_specs=(
            pl.BlockSpec((1, length, 3 * length), lambda c: (c, 0, 0)),
            pl.BlockSpec((1, 3 * TX, TX), lambda c: (c, 0, 0)),
        ),
        compiler_params=pltpu.CompilerParams(vmem_limit_bytes=16 << 20),
        cost_estimate=pl.CostEstimate(
            flops=2 * channels * 6 * 2 * length**3, bytes_accessed=6 << 20, transcendentals=0
        ),
        name="smoothing_tables",
    )(sigma, waves_rows, waves(TX))


def smooth_kernel(field, rows_table, columns_table, out):
    channel = pl.program_id(0)
    high, low = split(field[pl.ds(channel, field.shape[0] // 8, stride=8), :])
    across = jnp.dot(
        jnp.concatenate([high, low, high], axis=1), columns_table[0], preferred_element_type=f32
    )
    high, low = split(across)
    out[0] = jnp.dot(
        rows_table[0], jnp.concatenate([high, low, high], axis=0), preferred_element_type=f32
    )


def smooth(field, rows_table, columns_table):
    channels, length, _ = rows_table.shape
    return pl.pallas_call(
        smooth_kernel,
        grid=(channels,),
        out_shape=jax.ShapeDtypeStruct((channels, length, TX), f32),
        in_specs=[
            pl.BlockSpec(field.shape, lambda c: (0, 0)),
            pl.BlockSpec((1, length, 3 * length), lambda c: (c, 0, 0)),
            pl.BlockSpec((1, 3 * TX, TX), lambda c: (c, 0, 0)),
        ],
        out_specs=pl.BlockSpec((1, length, TX), lambda c: (c, 0, 0)),
        compiler_params=pltpu.CompilerParams(vmem_limit_bytes=16 << 20),
        name="smooth",
    )(field, rows_table, columns_table)


def local(
    spectra, feed_ids, feed_gain, send_list, send_count, kernel_weight, pixel_block, beam_width
):
    chips = lax.axis_size(("y", "z"))

    def shift(array, by):
        return lax.ppermute(array, ("y", "z"), [(i, (i + by) % chips) for i in range(chips)])

    unit, packed = prepare(
        spectra, feed_ids, feed_gain, send_list, send_count, kernel_weight, pixel_block
    )
    here = lax.all_to_all(unit, "core", split_axis=0, concat_axis=0, tiled=True)
    packed_other = lax.ppermute(packed, "core", [(0, 1), (1, 0)])
    above1 = shift(here, -1)
    below1 = shift(here, 1)
    above2 = shift(above1, -1)
    below2 = shift(below1[1], 1)
    sums = lax.psum(here[:, HALF_CH + BAND // 2, :], "chan")
    sum_a1, sum_b1 = shift(sums, -1), shift(sums, 1)
    sum_a2, sum_b2 = shift(sums, -2), shift(sums[1:2], 2)
    core = lax.axis_index("core").astype(jnp.int32).reshape(1)
    gridded = grid_tiles(
        core,
        (below2, below1, here, above1, above2),
        (sum_b2, sum_b1, sums, sum_a1, sum_a2),
        packed,
        packed_other,
    )
    gridded, beam_width = lax.optimization_barrier((gridded, beam_width))
    relaid = lax.all_to_all(gridded, ("y", "z"), split_axis=0, concat_axis=0, tiled=True)
    rows_table, columns_table = make_tables(beam_width, chips * CORES * TY)
    return smooth(relaid.reshape(chips * CORES * TY * 8, TX), rows_table, columns_table)


def solution(mesh):
    tiles, channels = mesh.devices.shape
    chips = tiles // CORES
    grid = Mesh(
        mesh.devices.reshape(chips // ROWS_Z, ROWS_Z, CORES, channels), ("y", "z", "core", "chan")
    )
    tile = ("y", "z", "core")
    in_specs = (
        P(tile, "chan"),
        P(tile),
        P(None, "chan"),
        P(tile, None),
        P(tile),
        P(tile, None),
        P(tile),
        P(("chan",) + tile),
    )
    out_specs = P(("chan",) + tile, None, None)
    return jax.shard_map(local, mesh=grid, in_specs=in_specs, out_specs=out_specs, check_vma=False)
```

time: 190 us -> 152 us (0.80)
  the two profiles are of different devices: /device:TPU:1 before, /device:TPU:32 now
where the time goes in v1:
time: 152 us; the launch traced here: 151 us
  waiting for transfers between devices  60.2 us (40%)
  starting transfers between devices  49.1 us (32%)
  Pallas kernels  16.6 us (11%)
  blocking collectives  14.6 us (10%)
  local copies, waits for them, and re-layouts  9.2 us (6%)
    all_to_all x1, waiting for transfers between devices, local(): lax.all_to_all(gridded, ('y', 'z'), split_axis=0, concat_axis=0, tiled=True)  40.7 us
    ppermute x8, starting transfers between devices, shift(): lax.ppermute(array, ('y', 'z'), [(i, (i + by) % chips) for i in range(chi...  39.4 us
    ppermute x8, waiting for transfers between devices, shift(): lax.ppermute(array, ('y', 'z'), [(i, (i + by) % chips) for i in range(chi...  19.4 us
    psum x1, blocking collectives, local(): sums = lax.psum(here[:, HALF_CH + BAND // 2, :], 'chan')  10.5 us
    unnamed x19, local copies, waits for them, and re-layouts  9.17 us
    all_to_all x1, starting transfers between devices, local(): lax.all_to_all(gridded, ('y', 'z'), split_axis=0, concat_axis=0, tiled=True)  7.74 us
    pallas_call x1, Pallas kernels, make_tables(): pl.pallas_call(tables_kernel, grid=(channels,), out_shape=(jax.ShapeDtype...  6.63 us
    pallas_call x1, Pallas kernels, smooth(): pl.pallas_call(smooth_kernel, grid=(channels,), out_shape=jax.ShapeDtypeS...  5.14 us
  transfers between devices with their start and end apart: 10, of which 5 were waited for; matrix products, arithmetic and copies ran while one was open for 1% of the time, Pallas kernels for 4%

profile of v1, /device:TPU:32, one launch (start us, length us, event | category | flops | bytes accessed | tf_op | source)
XLA Modules:
  0.0 151.3 jit_solution(17013482996382870539)
XLA Ops:
  0.0 1.0 copy.15.weights
  1.0 0.0 copy-start.2
  1.0 1.0 copy-done.2
  2.1 0.0 copy-start.3
  2.1 0.9 copy-done.3
  3.0 0.0 copy-start.4
  3.0 0.7 copy-done.4
  3.7 0.0 copy-start.5
  3.7 0.7 copy-done.5
  4.3 0.0 copy-start.6
  4.3 0.7 copy-done.6
  5.0 0.0 copy-start.7
  5.0 0.7 copy-done.7
  5.7 1.2 prepare.1
  6.8 4.1 %all_to_all.10.here = f32[2,520,128]{2,1,0:T(8,128)S(1)} all-to-all(f32[2,520,128]{2,1,0:T(8,128)S(1)} %get-tuple-element.11), channel_id=1, replica_groups=mesh['y'=4,'z'=16,'core'=2,'chan'=4] {'core'}, dimensions={0} | all-to-all | bytes 1064960 | tf_op jit(solution)/shard_map/all_to_all | solution.py:296
  11.0 7.4 %collective-permute-start.2 = (f32[2,520,128]{2,1,0:T(8,128)S(1)}, f32[2,520,128]{2,1,0:T(8,128)S(1)}, u32[]{:S(2)}, u32[]{:S(2)}) collective-permute-start(f32[2,520,128]{2,1,0:T(8,128)S(1)} %all_to_all.10.here), channel_id=1, source_target_pairs={{0,504},{8,0},{16,8},{24,16},{32,24},{40,32},{48,40},{56,48},{64,5... | collective-permute-start | bytes 1597448 | tf_op jit(solution)/shard_map/ppermute | solution.py:291
  18.3 1.9 %collective-permute-start = (f32[2,520,128]{2,1,0:T(8,128)S(1)}, f32[2,520,128]{2,1,0:T(8,128)S(1)}, u32[]{:S(2)}, u32[]{:S(2)}) collective-permute-start(f32[2,520,128]{2,1,0:T(8,128)S(1)} %all_to_all.10.here), channel_id=1, source_target_pairs={{0,8},{8,16},{16,24},{24,32},{32,40},{40,48},{48,56},{56,64},{64,7... | collective-permute-start | bytes 1597448 | tf_op jit(solution)/shard_map/ppermute | solution.py:291
  20.3 9.7 %collective-permute-done.2.above1 = f32[2,520,128]{2,1,0:T(8,128)S(1)} collective-permute-done((f32[2,520,128]{2,1,0:T(8,128)S(1)}, f32[2,520,128]{2,1,0:T(8,128)S(1)}, u32[]{:S(2)}, u32[]{:S(2)}) %collective-permute-start.2) | collective-permute-done | bytes 532512 | tf_op jit(solution)/shard_map/ppermute | solution.py:291
  30.0 8.5 %collective-permute-start.3 = (f32[2,520,128]{2,1,0:T(8,128)S(1)}, f32[2,520,128]{2,1,0:T(8,128)S(1)}, u32[]{:S(2)}, u32[]{:S(2)}) collective-permute-start(f32[2,520,128]{2,1,0:T(8,128)S(1)} %collective-permute-done.2.above1), channel_id=1, source_target_pairs={{0,504},{8,0},{16,8},{24,16},{32,24},{40,32},{48,40},{56,48},{64,5... | collective-permute-start | bytes 1597448 | tf_op jit(solution)/shard_map/ppermute | solution.py:291
  38.5 0.5 collective-permute-done.below1
  39.0 1.9 %collective-permute-start.1 = (f32[520,128]{1,0:T(8,128)S(1)}, f32[520,128]{1,0:T(8,128)S(1)}, u32[]{:S(2)}, u32[]{:S(2)}) collective-permute-start(f32[520,128]{1,0:T(8,128)S(1)} %slice_bitcast_fusion), channel_id=1, source_target_pairs={{0,8},{8,16},{16,24},{24,32},{32,40},{40,48},{48,56},{56,64},{64,7... | collective-permute-start | bytes 798728 | tf_op jit(solution)/shard_map/ppermute | solution.py:291
  40.9 1.9 %collective-permute-start.8 = (f32[72,512]{1,0:T(8,128)S(1)}, f32[72,512]{1,0:T(8,128)S(1)}, u32[]{:S(2)}, u32[]{:S(2)}) collective-permute-start(f32[72,512]{1,0:T(8,128)S(1)} %get-tuple-element.12.packed_own), channel_id=1, source_target_pairs={{0,4},{4,0},{1,5},{5,1},{2,6},{6,2},{3,7},{7,3},{8,12},{12,8},{9,1... | collective-permute-start | bytes 442376 | tf_op jit(solution)/shard_map/ppermute | solution.py:297
  42.8 10.5 %psum.7.sum_h = f32[2,128]{1,0:T(2,128)S(1)} all-reduce(f32[2,128]{1,0:T(2,128)S(1)} %bitcast.12), channel_id=1, replica_groups=mesh['y'=4,'z'=16,'core'=2,'chan'=4] {'chan'}, use_global_device_ids=true, to_apply=%region_0.0 | all-reduce | flops 256 | bytes 2048 | tf_op jit(solution)/shard_map/psum | solution.py:302
  53.3 12.0 %collective-permute-start.7 = (f32[2,128]{1,0:T(2,128)S(1)}, f32[2,128]{1,0:T(2,128)S(1)}, u32[]{:S(2)}, u32[]{:S(2)}) collective-permute-start(f32[2,128]{1,0:T(2,128)S(1)} %psum.7.sum_h), channel_id=1, source_target_pairs={{0,496},{8,504},{16,0},{24,8},{32,16},{40,24},{48,32},{56,40},{64,... | collective-permute-start | bytes 3080 | tf_op jit(solution)/shard_map/ppermute | solution.py:291
  65.3 1.9 %collective-permute-start.4 = (f32[1,128]{1,0:T(1,128)S(1)}, f32[1,128]{1,0:T(1,128)S(1)}, u32[]{:S(2)}, u32[]{:S(2)}) collective-permute-start(f32[1,128]{1,0:T(1,128)S(1)} %slice.11), channel_id=1, source_target_pairs={{0,16},{8,24},{16,32},{24,40},{32,48},{40,56},{48,64},{56,72},{64,... | collective-permute-start | bytes 1544 | tf_op jit(solution)/shard_map/ppermute | solution.py:291
  67.3 7.7 %collective-permute-done.4.sum_b2 = f32[1,128]{1,0:T(1,128)S(1)} collective-permute-done((f32[1,128]{1,0:T(1,128)S(1)}, f32[1,128]{1,0:T(1,128)S(1)}, u32[]{:S(2)}, u32[]{:S(2)}) %collective-permute-start.4) | collective-permute-done | bytes 544 | tf_op jit(solution)/shard_map/ppermute | solution.py:291
  75.0 1.9 %collective-permute-start.6 = (f32[2,128]{1,0:T(2,128)S(1)}, f32[2,128]{1,0:T(2,128)S(1)}, u32[]{:S(2)}, u32[]{:S(2)}) collective-permute-start(f32[2,128]{1,0:T(2,128)S(1)} %psum.7.sum_h), channel_id=1, source_target_pairs={{0,504},{8,0},{16,8},{24,16},{32,24},{40,32},{48,40},{56,48},{64,5... | collective-permute-start | bytes 3080 | tf_op jit(solution)/shard_map/ppermute | solution.py:291
  76.9 0.0 collective-permute-done.7.sum_a2
  76.9 3.9 %collective-permute-start.5 = (f32[2,128]{1,0:T(2,128)S(1)}, f32[2,128]{1,0:T(2,128)S(1)}, u32[]{:S(2)}, u32[]{:S(2)}) collective-permute-start(f32[2,128]{1,0:T(2,128)S(1)} %psum.7.sum_h), channel_id=1, source_target_pairs={{0,8},{8,16},{16,24},{24,32},{32,40},{40,48},{48,56},{56,64},{64,7... | collective-permute-start | bytes 3080 | tf_op jit(solution)/shard_map/ppermute | solution.py:291
  80.9 0.0 collective-permute-done.6.sum_a1
  80.9 1.5 %collective-permute-done.5.sum_b1 = f32[2,128]{1,0:T(2,128)S(1)} collective-permute-done((f32[2,128]{1,0:T(2,128)S(1)}, f32[2,128]{1,0:T(2,128)S(1)}, u32[]{:S(2)}, u32[]{:S(2)}) %collective-permute-start.5) | collective-permute-done | bytes 1056 | tf_op jit(solution)/shard_map/ppermute | solution.py:291
  82.4 0.0 collective-permute-done.8.packed_other
  82.4 0.0 collective-permute-done.1.below2
  82.4 0.0 collective-permute-done.3.above2
  82.4 0.0 copy-start.8
  82.4 3.7 %grid_tiles.1 = f32[64,4,8,128]{3,2,1,0:T(8,128)} custom-call(s32[1]{0:T(128)} %bitcast.core, f32[520,128]{1,0:T(8,128)S(1)} %collective-permute-done.1.below2, f32[2,520,128]{2,1,0:T(8,128)S(1)} %collective-permute-done.below1, f32[2,520,128]{2,1,0:T(8,128)S(1)} %all_to_all.10.here, f32[2,520,128]{2,1,0:T(8,128)S(1)} %collective-permute-done.2.above1, ...), custom_call_target="tpu_custom_call" | custom-call | tf_op jit(solution)/shard_map/grid_tiles/pallas_call | solution.py:172
  86.1 7.7 %all-to-all-start.1 = ((f32[64,4,8,128]{3,2,1,0:T(8,128)}), f32[64,4,8,128]{3,2,1,0:T(8,128)S(1)}, u32[]{:S(2)}, u32[]{:S(2)}) async-start(f32[64,4,8,128]{3,2,1,0:T(8,128)} %grid_tiles.1), calls=%async_computation.1 | async-start | bytes 2097152 | tf_op jit(solution)/shard_map/all_to_all | solution.py:314
  93.9 0.3 fusion.14
  94.2 1.0 fusion.6
  95.2 0.1 pad_maximum_fusion.row_waves
  95.3 0.0 copy-done.8
  95.3 6.6 %smoothing_tables.1 = (bf16[8,256,768]{2,1,0:T(8,128)(2,1)S(1)}, bf16[8,384,128]{2,1,0:T(8,128)(2,1)S(1)}) custom-call(f32[8]{0:T(128)S(1)} %copy-done.8, f32[256,512]{1,0:T(8,128)S(1)} %pad_maximum_fusion.row_waves, f32[128,256]{1,0:T(8,128)S(1)} %pad_maximum_fusion.1.column_waves), custom_call_target="tpu_custom_call" | custom-call | flops 3221225472 | bytes 6291456 | tf_op jit(solution)/shard_map/smoothing_tables/pallas_call | solution.py:232
  101.9 0.0 copy-start
  101.9 1.6 %copy-done = bf16[8,256,768]{2,1,0:T(8,128)(2,1)} copy-done((bf16[8,256,768]{2,1,0:T(8,128)(2,1)}, bf16[8,256,768]{2,1,0:T(8,128)(2,1)S(1)}, u32[]{:S(2)}) %copy-start) | copy-done | bytes 3145752
  103.6 40.7 %all-to-all-done.1 = f32[64,4,8,128]{3,2,1,0:T(8,128)S(1)} async-done(((f32[64,4,8,128]{3,2,1,0:T(8,128)}), f32[64,4,8,128]{3,2,1,0:T(8,128)S(1)}, u32[]{:S(2)}, u32[]{:S(2)}) %all-to-all-start.1) | async-done | bytes 1048608 | tf_op jit(solution)/shard_map/all_to_all | solution.py:314
  144.3 0.0 copy-start.1
  144.3 1.9 %copy-done.1 = bf16[8,256,768]{2,1,0:T(8,128)(2,1)S(1)} copy-done((bf16[8,256,768]{2,1,0:T(8,128)(2,1)S(1)}, bf16[8,256,768]{2,1,0:T(8,128)(2,1)}, u32[]{:S(2)}) %copy-start.1) | copy-done | bytes 3145752
  146.2 5.1 %smooth.1 = f32[8,256,128]{2,1,0:T(8,128)} custom-call(f32[2048,128]{1,0:T(8,128)S(1)} %bitcast.9, bf16[8,256,768]{2,1,0:T(8,128)(2,1)S(1)} %copy-done.1, bf16[8,384,128]{2,1,0:T(8,128)(2,1)S(1)} %get-tuple-element.16.columns_table), custom_call_target="tpu_custom_call" | custom-call | tf_op jit(solution)/shard_map/smooth/pallas_call | solution.py:270
  (4 shorter events, 0.0 us)
Async XLA Ops:
  1.0 1.0 copy-start.2
  2.1 0.9 copy-start.3
  3.0 0.7 copy-start.4
  3.7 0.7 copy-start.5
  4.3 0.7 copy-start.6
  5.0 0.7 copy-start.7
  11.0 19.0 %collective-permute-start.2 = (f32[2,520,128]{2,1,0:T(8,128)S(1)}, f32[2,520,128]{2,1,0:T(8,128)S(1)}, u32[]{:S(2)}, u32[]{:S(2)}) collective-permute-start(f32[2,520,128]{2,1,0:T(8,128)S(1)} %all_to_all.10.here), channel_id=1, source_target_pairs={{0,504},{8,0},{16,8},{24,16},{32,24},{40,32},{48,40},{56,48},{64,5... | collective-permute-start | bytes 1597448 | tf_op jit(solution)/shard_map/ppermute | solution.py:291
  18.3 20.6 %collective-permute-start = (f32[2,520,128]{2,1,0:T(8,128)S(1)}, f32[2,520,128]{2,1,0:T(8,128)S(1)}, u32[]{:S(2)}, u32[]{:S(2)}) collective-permute-start(f32[2,520,128]{2,1,0:T(8,128)S(1)} %all_to_all.10.here), channel_id=1, source_target_pairs={{0,8},{8,16},{16,24},{24,32},{32,40},{40,48},{48,56},{56,64},{64,7... | collective-permute-start | bytes 1597448 | tf_op jit(solution)/shard_map/ppermute | solution.py:291
  30.0 52.4 %collective-permute-start.3 = (f32[2,520,128]{2,1,0:T(8,128)S(1)}, f32[2,520,128]{2,1,0:T(8,128)S(1)}, u32[]{:S(2)}, u32[]{:S(2)}) collective-permute-start(f32[2,520,128]{2,1,0:T(8,128)S(1)} %collective-permute-done.2.above1), channel_id=1, source_target_pairs={{0,504},{8,0},{16,8},{24,16},{32,24},{40,32},{48,40},{56,48},{64,5... | collective-permute-start | bytes 1597448 | tf_op jit(solution)/shard_map/ppermute | solution.py:291
  39.0 43.4 %collective-permute-start.1 = (f32[520,128]{1,0:T(8,128)S(1)}, f32[520,128]{1,0:T(8,128)S(1)}, u32[]{:S(2)}, u32[]{:S(2)}) collective-permute-start(f32[520,128]{1,0:T(8,128)S(1)} %slice_bitcast_fusion), channel_id=1, source_target_pairs={{0,8},{8,16},{16,24},{24,32},{32,40},{40,48},{48,56},{56,64},{64,7... | collective-permute-start | bytes 798728 | tf_op jit(solution)/shard_map/ppermute | solution.py:291
  40.9 41.5 %collective-permute-start.8 = (f32[72,512]{1,0:T(8,128)S(1)}, f32[72,512]{1,0:T(8,128)S(1)}, u32[]{:S(2)}, u32[]{:S(2)}) collective-permute-start(f32[72,512]{1,0:T(8,128)S(1)} %get-tuple-element.12.packed_own), channel_id=1, source_target_pairs={{0,4},{4,0},{1,5},{5,1},{2,6},{6,2},{3,7},{7,3},{8,12},{12,8},{9,1... | collective-permute-start | bytes 442376 | tf_op jit(solution)/shard_map/ppermute | solution.py:297
  53.3 23.6 %collective-permute-start.7 = (f32[2,128]{1,0:T(2,128)S(1)}, f32[2,128]{1,0:T(2,128)S(1)}, u32[]{:S(2)}, u32[]{:S(2)}) collective-permute-start(f32[2,128]{1,0:T(2,128)S(1)} %psum.7.sum_h), channel_id=1, source_target_pairs={{0,496},{8,504},{16,0},{24,8},{32,16},{40,24},{48,32},{56,40},{64,... | collective-permute-start | bytes 3080 | tf_op jit(solution)/shard_map/ppermute | solution.py:291
  65.3 9.7 %collective-permute-start.4 = (f32[1,128]{1,0:T(1,128)S(1)}, f32[1,128]{1,0:T(1,128)S(1)}, u32[]{:S(2)}, u32[]{:S(2)}) collective-permute-start(f32[1,128]{1,0:T(1,128)S(1)} %slice.11), channel_id=1, source_target_pairs={{0,16},{8,24},{16,32},{24,40},{32,48},{40,56},{48,64},{56,72},{64,... | collective-permute-start | bytes 1544 | tf_op jit(solution)/shard_map/ppermute | solution.py:291
  75.0 5.9 %collective-permute-start.6 = (f32[2,128]{1,0:T(2,128)S(1)}, f32[2,128]{1,0:T(2,128)S(1)}, u32[]{:S(2)}, u32[]{:S(2)}) collective-permute-start(f32[2,128]{1,0:T(2,128)S(1)} %psum.7.sum_h), channel_id=1, source_target_pairs={{0,504},{8,0},{16,8},{24,16},{32,24},{40,32},{48,40},{56,48},{64,5... | collective-permute-start | bytes 3080 | tf_op jit(solution)/shard_map/ppermute | solution.py:291
  76.9 5.5 %collective-permute-start.5 = (f32[2,128]{1,0:T(2,128)S(1)}, f32[2,128]{1,0:T(2,128)S(1)}, u32[]{:S(2)}, u32[]{:S(2)}) collective-permute-start(f32[2,128]{1,0:T(2,128)S(1)} %psum.7.sum_h), channel_id=1, source_target_pairs={{0,8},{8,16},{16,24},{24,32},{32,40},{40,48},{48,56},{56,64},{64,7... | collective-permute-start | bytes 3080 | tf_op jit(solution)/shard_map/ppermute | solution.py:291
  82.4 12.9 %copy-start.8 = (f32[8]{0:T(128)S(1)}, f32[8]{0:T(128)}, u32[]{:S(2)}) copy-start(f32[8]{0:T(128)} %sigma) | copy-start | bytes 100
  86.1 58.2 %all-to-all-start.1 = ((f32[64,4,8,128]{3,2,1,0:T(8,128)}), f32[64,4,8,128]{3,2,1,0:T(8,128)S(1)}, u32[]{:S(2)}, u32[]{:S(2)}) async-start(f32[64,4,8,128]{3,2,1,0:T(8,128)} %grid_tiles.1), calls=%async_computation.1 | async-start | bytes 2097152 | tf_op jit(solution)/shard_map/all_to_all | solution.py:314
  101.9 1.7 %copy-start = (bf16[8,256,768]{2,1,0:T(8,128)(2,1)}, bf16[8,256,768]{2,1,0:T(8,128)(2,1)S(1)}, u32[]{:S(2)}) copy-start(bf16[8,256,768]{2,1,0:T(8,128)(2,1)S(1)} %get-tuple-element.15.rows_table) | copy-start | bytes 9437188
  144.3 1.9 %copy-start.1 = (bf16[8,256,768]{2,1,0:T(8,128)(2,1)S(1)}, bf16[8,256,768]{2,1,0:T(8,128)(2,1)}, u32[]{:S(2)}) copy-start(bf16[8,256,768]{2,1,0:T(8,128)(2,1)} %copy-done) | copy-start | bytes 9437188

commit v2 on v1

--- a/solution.py
+++ b/solution.py
@@ -20,7 +20,11 @@
 HALF_CH = 512
 META = 8
 UNIT = HALF_CH + META
+TOTALS = HALF_CH + BAND // 2 + 1
 REACH = 9
+GROUPS = 4
+VMEM_SMOOTH = 52
+VMEM_PREPARE = 56
 PIX = TY * TX
 
 f32 = jnp.float32
@@ -39,71 +43,101 @@
 
 
 def prepare_kernel(
-    spectra, feed_ids, feed_gain, send_list, counts, weights, blocks, unit, packed, gains
+    counts,
+    spectra_in,
+    feed_ids_in,
+    feed_gain_in,
+    send_list_in,
+    weights_in,
+    blocks_in,
+    unit,
+    packed,
+    spectra,
+    feed_ids,
+    feed_gain,
+    gains,
+    send_list,
+    blocks,
+    arrived,
 ):
-    feeds = feed_gain.shape[0]
+    feeds = feed_gain_in.shape[0]
+    copies = []
+    for source, target in (
+        (feed_ids_in, feed_ids),
+        (feed_gain_in, feed_gain),
+        (spectra_in, spectra),
+        (send_list_in, send_list),
+        (blocks_in, blocks),
+        (weights_in, packed.at[0:KB]),
+    ):
+        copies.append(pltpu.make_async_copy(source, target, arrived.at[len(copies)]))
+        copies[-1].start()
     gains[...] = jnp.zeros_like(gains)
+    copies[0].wait()
+    copies[1].wait()
     gains[0:feeds, :] = feed_gain[...]
-    onehot = (
-        lax.broadcasted_iota(jnp.int32, (gains.shape[0], SLAB), 0) == feed_ids[...]
-    ).astype(f32)
+    onehot = (lax.broadcasted_iota(jnp.int32, (gains.shape[0], SLAB), 0) == feed_ids[...]).astype(
+        f32
+    )
     gain_rows = lax.dot_general(
         gains[...], onehot, (((0,), (0,)), ((), ())), precision=highest, preferred_element_type=f32
     )
+    copies[2].wait()
     raw = spectra[...].T
     band_sum = jnp.sum(raw, axis=0, keepdims=True)
     scaled = (raw * gain_rows).reshape(HALF_CH // 8, CORES, 8, SLAB)
+    copies[3].wait()
     lane = lax.broadcasted_iota(jnp.int32, (1, CAP), 1)
-    rows = []
-    for row in range(BAND):
-        rows.append(
-            jnp.where(lane < counts[row], send_list[row : row + 1, :], -1).astype(f32)
-        )
+    rows = [
+        jnp.where(lane < counts[row], send_list[row : row + 1, :], -1).astype(f32)
+        for row in range(BAND)
+    ]
     rows = [jnp.concatenate(rows[2 * m : 2 * m + 2], axis=1) for m in range(BAND // 2)]
     meta = jnp.concatenate(rows + [band_sum, jnp.zeros((META - BAND // 2 - 1, SLAB), f32)], axis=0)
     for core in range(CORES):
         unit[core, 0:HALF_CH, :] = scaled[:, core].reshape(HALF_CH, SLAB)
         unit[core, HALF_CH:UNIT, :] = meta
-    wide = jnp.concatenate([weights[...], jnp.zeros((BAND * CAP, KB), f32)], axis=1)
-    packed[0:KB, :] = wide.T[0:KB, :]
+    copies[4].wait()
     packed[KB : KB + 8, :] = jnp.broadcast_to(blocks[...].astype(f32), (8, BAND * CAP))
+    copies[5].wait()
 
 
 def prepare(spectra, feed_ids, feed_gain, send_list, send_count, kernel_weight, pixel_block):
     slots = BAND * CAP
+    channels = spectra.shape[1]
     return pl.pallas_call(
         prepare_kernel,
         out_shape=(
             jax.ShapeDtypeStruct((CORES, UNIT, SLAB), f32),
             jax.ShapeDtypeStruct((KB + 8, slots), f32),
         ),
-        in_specs=[
-            whole(),
-            whole(),
-            whole(),
-            whole(),
-            whole(pltpu.SMEM),
-            whole(),
-            whole(),
+        in_specs=[whole(pltpu.SMEM)] + [whole(pltpu.HBM)] * 6,
+        out_specs=(whole(), whole()),
+        scratch_shapes=[
+            VMEM((SLAB, channels), f32),
+            VMEM((1, SLAB), jnp.int32),
+            VMEM(feed_gain.shape, f32),
+            VMEM((24, channels), f32),
+            VMEM((BAND, CAP), jnp.int32),
+            VMEM((1, slots), jnp.int32),
+            pltpu.SemaphoreType.DMA((6,)),
         ],
-        out_specs=(whole(), whole()),
-        scratch_shapes=[VMEM((24, spectra.shape[1]), f32)],
-        compiler_params=pltpu.CompilerParams(vmem_limit_bytes=24 << 20),
+        compiler_params=pltpu.CompilerParams(vmem_limit_bytes=VMEM_PREPARE << 20),
         name="prepare",
     )(
+        send_count,
         spectra,
         feed_ids.reshape(1, SLAB),
         feed_gain,
         send_list,
-        send_count,
-        kernel_weight,
+        kernel_weight.T,
         pixel_block.reshape(1, slots),
     )
 
 
 def grid_kernel(
-    core, below2, below1, here, above1, above2, sum_b2, sum_b1, sum_h, sum_a1, sum_a2,
-    packed_own, packed_other, out, left, right, dense,
+    core, below2, below1, here, above1, above2, sum_b2, sum_h, sum_a2, packed_own, packed_other, out,
+    left, right, dense,
 ):
     me = core[0]
     for tile in range(CORES):
@@ -115,23 +149,22 @@
             dense[tile, number * KB : (number + 1) * KB, :] = high
             dense[tile, PIX + number * KB : PIX + (number + 1) * KB, :] = low
     slabs = [
-        (below2, None, sum_b2, 0),
-        (below1, 0, sum_b1, 0),
-        (below1, 1, sum_b1, 1),
-        (here, 0, sum_h, 0),
-        (here, 1, sum_h, 1),
-        (above1, 0, sum_a1, 0),
-        (above1, 1, sum_a1, 1),
-        (above2, 0, sum_a2, 0),
-        (above2, 1, sum_a2, 1),
+        (below2, sum_b2[0:1, :]),
+        (below1.at[0], below2[TOTALS : TOTALS + 1, :]),
+        (below1.at[1], below2[TOTALS + 1 : TOTALS + 2, :]),
+        (here.at[0], sum_h[0:1, :]),
+        (here.at[1], sum_h[1:2, :]),
+        (above1.at[0], above2[0, TOTALS : TOTALS + 1, :]),
+        (above1.at[1], above2[1, TOTALS : TOTALS + 1, :]),
+        (above2.at[0], sum_a2[0:1, :]),
+        (above2.at[1], sum_a2[1:2, :]),
     ]
     depth = REACH * SLAB
     totals = [jnp.zeros((1, PIX), f32) for _ in range(CORES)]
     sample = lax.broadcasted_iota(jnp.int32, (SLAB, SLAB), 0).astype(f32)
     lane = lax.broadcasted_iota(jnp.int32, (SLAB, SLAB), 1)
-    for index, (ref, part, sums, row) in enumerate(slabs):
-        unit = ref if part is None else ref.at[part]
-        scale = CH / sums[row : row + 1, :]
+    for index, (unit, band_sum) in enumerate(slabs):
+        scale = CH / band_sum
         high, low = split(unit[0:HALF_CH, :] * scale)
         at = index * SLAB
         left[:, at : at + SLAB] = high
@@ -172,7 +205,7 @@
     return pl.pallas_call(
         grid_kernel,
         out_shape=jax.ShapeDtypeStruct((HALF_CH // 8, CORES * TY, 8, TX), f32),
-        in_specs=[whole(pltpu.SMEM)] + [whole()] * 12,
+        in_specs=[whole(pltpu.SMEM)] + [whole()] * 10,
         out_specs=whole(),
         scratch_shapes=[
             VMEM((HALF_CH, 3 * depth), bf16),
@@ -215,14 +248,13 @@
 def tables_kernel(sigma, row_waves, column_waves, rows_out, columns_out):
     width = sigma[pl.program_id(0)]
     high, low = split(circulant(width, row_waves[...]))
-    size = high.shape[0]
-    rows_out[0, :, 0:size] = high
-    rows_out[0, :, size : 2 * size] = high
-    rows_out[0, :, 2 * size : 3 * size] = low
+    rows_out[0, 0] = high
+    rows_out[0, 1] = low
     high, low = split(circulant(width, column_waves[...]))
-    columns_out[0, 0:TX, :] = high
-    columns_out[0, TX : 2 * TX, :] = high
-    columns_out[0, 2 * TX : 3 * TX, :] = low
+    columns_out[0, 0:TX, 0:TX] = high
+    columns_out[0, 0:TX, TX:] = low
+    columns_out[0, TX:, 0:TX] = high
+    columns_out[0, TX:, TX:] = jnp.zeros_like(low)
 
 
 def make_tables(sigma, length):
@@ -233,8 +265,8 @@
         tables_kernel,
         grid=(channels,),
         out_shape=(
-            jax.ShapeDtypeStruct((channels, length, 3 * length), bf16),
-            jax.ShapeDtypeStruct((channels, 3 * TX, TX), bf16),
+            jax.ShapeDtypeStruct((channels, 2, length, length), bf16),
+            jax.ShapeDtypeStruct((channels, 2 * TX, 2 * TX), bf16),
         ),
         in_specs=[
             whole(pltpu.SMEM),
@@ -242,10 +274,10 @@
             fixed((TX, 2 * TX)),
         ],
         out_specs=(
-            pl.BlockSpec((1, length, 3 * length), lambda c: (c, 0, 0)),
-            pl.BlockSpec((1, 3 * TX, TX), lambda c: (c, 0, 0)),
+            pl.BlockSpec((1, 2, length, length), lambda c: (c, 0, 0, 0)),
+            pl.BlockSpec((1, 2 * TX, 2 * TX), lambda c: (c, 0, 0)),
         ),
-        compiler_params=pltpu.CompilerParams(vmem_limit_bytes=16 << 20),
+        compiler_params=pltpu.CompilerParams(vmem_limit_bytes=60 << 20),
         cost_estimate=pl.CostEstimate(
             flops=2 * channels * 6 * 2 * length**3, bytes_accessed=6 << 20, transcendentals=0
         ),
@@ -253,31 +285,54 @@
     )(sigma, waves_rows, waves(TX))
 
 
-def smooth_kernel(field, rows_table, columns_table, out):
-    channel = pl.program_id(0)
-    high, low = split(field[pl.ds(channel, field.shape[0] // 8, stride=8), :])
-    across = jnp.dot(
-        jnp.concatenate([high, low, high], axis=1), columns_table[0], preferred_element_type=f32
-    )
-    high, low = split(across)
-    out[0] = jnp.dot(
-        rows_table[0], jnp.concatenate([high, low, high], axis=0), preferred_element_type=f32
-    )
+def smooth_kernel(
+    field, rows_in, columns_in, out, rows_table, columns_table, across, smoothed, here, done
+):
+    channels, length, _ = smoothed.shape
+    columns_copy = pltpu.make_async_copy(columns_in, columns_table, here.at[0])
+    rows_copy = pltpu.make_async_copy(rows_in, rows_table, here.at[1])
+    columns_copy.start()
+    rows_copy.start()
+    columns_copy.wait()
+    for c in range(channels):
+        high, low = split(field[pl.ds(c, length, stride=channels), :])
+        both = jnp.dot(
+            jnp.concatenate([high, low], axis=1), columns_table[c], preferred_element_type=f32
+        )
+        high, low = split(both[:, 0:TX] + both[:, TX:])
+        across[c, :, 0:TX] = high
+        across[c, :, TX:] = low
+    rows_copy.wait()
+    group = channels // GROUPS
+    copies = []
+    for number in range(GROUPS):
+        for c in range(number * group, (number + 1) * group):
+            both = jnp.dot(rows_table[c, 0], across[c], preferred_element_type=f32)
+            rest = jnp.dot(rows_table[c, 1], across[c, :, 0:TX], preferred_element_type=f32)
+            smoothed[c] = both[:, 0:TX] + both[:, TX:] + rest
+        part = pl.ds(number * group, group)
+        copies.append(pltpu.make_async_copy(smoothed.at[part], out.at[part], done.at[number]))
+        copies[-1].start()
+    for copy in copies:
+        copy.wait()
 
 
 def smooth(field, rows_table, columns_table):
-    channels, length, _ = rows_table.shape
+    channels, _, length, _ = rows_table.shape
     return pl.pallas_call(
         smooth_kernel,
-        grid=(channels,),
         out_shape=jax.ShapeDtypeStruct((channels, length, TX), f32),
-        in_specs=[
-            pl.BlockSpec(field.shape, lambda c: (0, 0)),
-            pl.BlockSpec((1, length, 3 * length), lambda c: (c, 0, 0)),
-            pl.BlockSpec((1, 3 * TX, TX), lambda c: (c, 0, 0)),
+        in_specs=[whole(), whole(pltpu.HBM), whole(pltpu.HBM)],
+        out_specs=whole(pltpu.HBM),
+        scratch_shapes=[
+            VMEM(rows_table.shape, bf16),
+            VMEM(columns_table.shape, bf16),
+            VMEM((channels, length, 2 * TX), bf16),
+            VMEM((channels, length, TX), f32),
+            pltpu.SemaphoreType.DMA((2,)),
+            pltpu.SemaphoreType.DMA((GROUPS,)),
         ],
-        out_specs=pl.BlockSpec((1, length, TX), lambda c: (c, 0, 0)),
-        compiler_params=pltpu.CompilerParams(vmem_limit_bytes=16 << 20),
+        compiler_params=pltpu.CompilerParams(vmem_limit_bytes=VMEM_SMOOTH << 20),
         name="smooth",
     )(field, rows_table, columns_table)
 
@@ -297,16 +352,16 @@
     packed_other = lax.ppermute(packed, "core", [(0, 1), (1, 0)])
     above1 = shift(here, -1)
     below1 = shift(here, 1)
+    sums = lax.psum(here[:, TOTALS - 1, :], "chan")
+    sum_a2, sum_b2 = shift(sums, -2), shift(sums[1:2], 2)
+    above1 = above1.at[:, TOTALS, :].set(sums)
     above2 = shift(above1, -1)
-    below2 = shift(below1[1], 1)
-    sums = lax.psum(here[:, HALF_CH + BAND // 2, :], "chan")
-    sum_a1, sum_b1 = shift(sums, -1), shift(sums, 1)
-    sum_a2, sum_b2 = shift(sums, -2), shift(sums[1:2], 2)
+    below2 = shift(below1[1].at[TOTALS : TOTALS + CORES, :].set(sums), 1)
     core = lax.axis_index("core").astype(jnp.int32).reshape(1)
     gridded = grid_tiles(
         core,
         (below2, below1, here, above1, above2),
-        (sum_b2, sum_b1, sums, sum_a1, sum_a2),
+        (sum_b2, sums, sum_a2),
         packed,
         packed_other,
     )

time: 152 us -> 128 us (0.84)
  the two profiles are of different devices: /device:TPU:32 before, /device:TPU:4 now
where the time goes in v2:
time: 128 us
  waiting for transfers between devices  50.2 us (39%)
  starting transfers between devices  41.7 us (33%)
  Pallas kernels  18.3 us (14%)
  blocking collectives  13.6 us (11%)
  other arithmetic  2.85 us (2%)
    all_to_all x1, waiting for transfers between devices, local(): lax.all_to_all(gridded, ('y', 'z'), split_axis=0, concat_axis=0, tiled=True)  42.6 us
    ppermute x6, starting transfers between devices, shift(): lax.ppermute(array, ('y', 'z'), [(i, (i + by) % chips) for i in range(chi...  32.1 us
    psum x1, blocking collectives, local(): sums = lax.psum(here[:, TOTALS - 1, :], 'chan')  8.32 us
    pallas_call x1, Pallas kernels, make_tables(): pl.pallas_call(tables_kernel, grid=(channels,), out_shape=(jax.ShapeDtype...  7.87 us
    ppermute x6, waiting for transfers between devices, shift(): lax.ppermute(array, ('y', 'z'), [(i, (i + by) % chips) for i in range(chi...  7.66 us
    all_to_all x1, starting transfers between devices, local(): lax.all_to_all(gridded, ('y', 'z'), split_axis=0, concat_axis=0, tiled=True)  7.61 us
    all_to_all x1, blocking collectives, local(): here = lax.all_to_all(unit, 'core', split_axis=0, concat_axis=0, tiled=True)  5.24 us
    pallas_call x1, Pallas kernels, grid_tiles(): pl.pallas_call(grid_kernel, out_shape=jax.ShapeDtypeStruct((HALF_CH // 8,...  3.7 us
  transfers between devices with their start and end apart: 8, of which 3 were waited for; matrix products, arithmetic and copies ran while one was open for 2% of the time, Pallas kernels for 6%

profile of v2, /device:TPU:4, one launch (start us, length us, event | category | flops | bytes accessed | tf_op | source)
XLA Modules:
  0.0 127.9 jit_solution(11972108372760630950)
XLA Ops:
  0.0 3.4 %prepare.1 = (f32[2,520,128]{2,1,0:T(8,128)}, f32[72,512]{1,0:T(8,128)}) custom-call(s32[8]{0:T(128)} %counts.1, f32[128,1024]{1,0:T(8,128)} %spectra_in.1, s32[1,128]{1,0:T(1,128)} %bitcast.18, f32[19,1024]{1,0:T(8,128)} %feed_gain_in.1, s32[8,64]{1,0:T(8,128)} %send_list_in.1, f32[64,512]{1,0:T(8,128)} %bitcast.15, s32[1,512]{1,0:T(1,128)} %bitcast.17), custom_call_target="tpu_custom_call" | custom-call | tf_op jit(solution)/shard_map/prepare/pallas_call | solution.py:108
  3.4 5.2 %all_to_all.10.here = f32[2,520,128]{2,1,0:T(8,128)S(1)} all-to-all(f32[2,520,128]{2,1,0:T(8,128)} %get-tuple-element.35), channel_id=1, replica_groups=mesh['y'=4,'z'=16,'core'=2,'chan'=4] {'core'}, dimensions={0} | all-to-all | bytes 1064960 | tf_op jit(solution)/shard_map/all_to_all | solution.py:351
  8.7 13.8 %collective-permute-start.2 = (f32[2,520,128]{2,1,0:T(8,128)S(1)}, f32[2,520,128]{2,1,0:T(8,128)S(1)}, u32[]{:S(2)}, u32[]{:S(2)}) collective-permute-start(f32[2,520,128]{2,1,0:T(8,128)S(1)} %all_to_all.10.here), channel_id=1, source_target_pairs={{0,504},{8,0},{16,8},{24,16},{32,24},{40,32},{48,40},{56,48},{64,5... | collective-permute-start | bytes 1597448 | tf_op jit(solution)/shard_map/ppermute | solution.py:346
  22.5 1.9 %collective-permute-start = (f32[2,520,128]{2,1,0:T(8,128)S(1)}, f32[2,520,128]{2,1,0:T(8,128)S(1)}, u32[]{:S(2)}, u32[]{:S(2)}) collective-permute-start(f32[2,520,128]{2,1,0:T(8,128)S(1)} %all_to_all.10.here), channel_id=1, source_target_pairs={{0,8},{8,16},{16,24},{24,32},{32,40},{40,48},{48,56},{56,64},{64,7... | collective-permute-start | bytes 1597448 | tf_op jit(solution)/shard_map/ppermute | solution.py:346
  24.4 8.3 %psum.7.sum_h = f32[2,128]{1,0:T(2,128)S(1)} all-reduce(f32[2,128]{1,0:T(2,128)S(1)} %bitcast.16), channel_id=1, replica_groups=mesh['y'=4,'z'=16,'core'=2,'chan'=4] {'chan'}, use_global_device_ids=true, to_apply=%region_0.0 | all-reduce | flops 256 | bytes 2048 | tf_op jit(solution)/shard_map/psum | solution.py:355
  32.8 1.4 %collective-permute-done.2 = f32[2,520,128]{2,1,0:T(8,128)S(1)} collective-permute-done((f32[2,520,128]{2,1,0:T(8,128)S(1)}, f32[2,520,128]{2,1,0:T(8,128)S(1)}, u32[]{:S(2)}, u32[]{:S(2)}) %collective-permute-start.2) | collective-permute-done | bytes 532512 | tf_op jit(solution)/shard_map/ppermute | solution.py:346
  34.2 7.7 %collective-permute-start.3 = (f32[2,520,128]{2,1,0:T(8,128)S(1)}, f32[2,520,128]{2,1,0:T(8,128)S(1)}, u32[]{:S(2)}, u32[]{:S(2)}) collective-permute-start(f32[2,520,128]{2,1,0:T(8,128)S(1)} %scatter.9.above1), channel_id=1, source_target_pairs={{0,504},{8,0},{16,8},{24,16},{32,24},{40,32},{48,40},{56,48},{64,5... | collective-permute-start | bytes 1597448 | tf_op jit(solution)/shard_map/ppermute | solution.py:346
  41.9 0.0 collective-permute-done.below1
  41.9 0.1 scatter.6
  42.0 1.9 %collective-permute-start.1 = (f32[520,128]{1,0:T(8,128)S(1)}, f32[520,128]{1,0:T(8,128)S(1)}, u32[]{:S(2)}, u32[]{:S(2)}) collective-permute-start(f32[520,128]{1,0:T(8,128)S(1)} %scatter.6), channel_id=1, source_target_pairs={{0,8},{8,16},{16,24},{24,32},{32,40},{40,48},{48,56},{56,64},{64,7... | collective-permute-start | bytes 798728 | tf_op jit(solution)/shard_map/ppermute | solution.py:346
  44.0 1.9 %collective-permute-start.6 = (f32[72,512]{1,0:T(8,128)}, f32[72,512]{1,0:T(8,128)S(1)}, u32[]{:S(2)}, u32[]{:S(2)}) collective-permute-start(f32[72,512]{1,0:T(8,128)} %get-tuple-element.36.packed_own), channel_id=1, source_target_pairs={{0,4},{4,0},{1,5},{5,1},{2,6},{6,2},{3,7},{7,3},{8,12},{12,8},{9,1... | collective-permute-start | bytes 442376 | tf_op jit(solution)/shard_map/ppermute | solution.py:352
  45.9 3.4 %collective-permute-start.5 = (f32[2,128]{1,0:T(2,128)S(1)}, f32[2,128]{1,0:T(2,128)S(1)}, u32[]{:S(2)}, u32[]{:S(2)}) collective-permute-start(f32[2,128]{1,0:T(2,128)S(1)} %psum.7.sum_h), channel_id=1, source_target_pairs={{0,496},{8,504},{16,0},{24,8},{32,16},{40,24},{48,32},{56,40},{64,... | collective-permute-start | bytes 3080 | tf_op jit(solution)/shard_map/ppermute | solution.py:346
  49.3 3.4 %collective-permute-start.4 = (f32[1,128]{1,0:T(1,128)S(1)}, f32[1,128]{1,0:T(1,128)S(1)}, u32[]{:S(2)}, u32[]{:S(2)}) collective-permute-start(f32[1,128]{1,0:T(1,128)S(1)} %slice.48), channel_id=1, source_target_pairs={{0,16},{8,24},{16,32},{24,40},{32,48},{40,56},{48,64},{56,72},{64,... | collective-permute-start | bytes 1544 | tf_op jit(solution)/shard_map/ppermute | solution.py:346
  52.7 6.3 %collective-permute-done.4.sum_b2 = f32[1,128]{1,0:T(1,128)S(1)} collective-permute-done((f32[1,128]{1,0:T(1,128)S(1)}, f32[1,128]{1,0:T(1,128)S(1)}, u32[]{:S(2)}, u32[]{:S(2)}) %collective-permute-start.4) | collective-permute-done | bytes 544 | tf_op jit(solution)/shard_map/ppermute | solution.py:346
  58.9 0.0 collective-permute-done.5.sum_a2
  58.9 0.0 collective-permute-done.6.packed_other
  59.0 0.0 collective-permute-done.1.below2
  59.0 0.0 collective-permute-done.3.above2
  59.0 0.0 copy-start
  59.0 0.9 copy-done
  59.9 3.7 %grid_tiles.1 = f32[64,4,8,128]{3,2,1,0:T(8,128)} custom-call(s32[1]{0:T(128)} %bitcast.core, f32[520,128]{1,0:T(8,128)S(1)} %collective-permute-done.1.below2, f32[2,520,128]{2,1,0:T(8,128)S(1)} %collective-permute-done.below1, f32[2,520,128]{2,1,0:T(8,128)S(1)} %all_to_all.10.here, f32[2,520,128]{2,1,0:T(8,128)S(1)} %scatter.9.above1, ...), custom_call_target="tpu_custom_call" | custom-call | tf_op jit(solution)/shard_map/grid_tiles/pallas_call | solution.py:205
  63.6 7.6 %all-to-all-start.1 = ((f32[64,4,8,128]{3,2,1,0:T(8,128)}), f32[64,4,8,128]{3,2,1,0:T(8,128)S(1)}, u32[]{:S(2)}, u32[]{:S(2)}) async-start(f32[64,4,8,128]{3,2,1,0:T(8,128)} %grid_tiles.1), calls=%async_computation.1 | async-start | bytes 2097152 | tf_op jit(solution)/shard_map/all_to_all | solution.py:369
  71.2 0.3 fusion.14
  71.5 0.7 pad_maximum_fusion.1.column_waves
  72.1 1.0 fusion.6
  73.2 0.9 pad_maximum_fusion.row_waves
  74.1 7.9 %smoothing_tables.1 = (bf16[8,2,256,256]{3,2,1,0:T(8,128)(2,1)}, bf16[8,256,256]{2,1,0:T(8,128)(2,1)}) custom-call(f32[8]{0:T(128)} %sigma, f32[256,512]{1,0:T(8,128)} %pad_maximum_fusion.row_waves, f32[128,256]{1,0:T(8,128)} %pad_maximum_fusion.1.column_waves), custom_call_target="tpu_custom_call" | custom-call | flops 3221225472 | bytes 6291456 | tf_op jit(solution)/shard_map/smoothing_tables/pallas_call | solution.py:264
  81.9 42.6 %all-to-all-done.1 = f32[64,4,8,128]{3,2,1,0:T(8,128)S(1)} async-done(((f32[64,4,8,128]{3,2,1,0:T(8,128)}), f32[64,4,8,128]{3,2,1,0:T(8,128)S(1)}, u32[]{:S(2)}, u32[]{:S(2)}) %all-to-all-start.1) | async-done | bytes 1048608 | tf_op jit(solution)/shard_map/all_to_all | solution.py:369
  124.5 3.4 %smooth.1 = f32[8,256,128]{2,1,0:T(8,128)} custom-call(f32[2048,128]{1,0:T(8,128)S(1)} %bitcast.13, bf16[8,2,256,256]{3,2,1,0:T(8,128)(2,1)} %get-tuple-element.39.rows_in, bf16[8,256,256]{2,1,0:T(8,128)(2,1)} %get-tuple-element.40.columns_in), custom_call_target="tpu_custom_call" | custom-call | tf_op jit(solution)/shard_map/smooth/pallas_call | solution.py:322
  (4 shorter events, 0.0 us)
Async XLA Ops:
  8.7 25.5 %collective-permute-start.2 = (f32[2,520,128]{2,1,0:T(8,128)S(1)}, f32[2,520,128]{2,1,0:T(8,128)S(1)}, u32[]{:S(2)}, u32[]{:S(2)}) collective-permute-start(f32[2,520,128]{2,1,0:T(8,128)S(1)} %all_to_all.10.here), channel_id=1, source_target_pairs={{0,504},{8,0},{16,8},{24,16},{32,24},{40,32},{48,40},{56,48},{64,5... | collective-permute-start | bytes 1597448 | tf_op jit(solution)/shard_map/ppermute | solution.py:346
  22.5 19.4 %collective-permute-start = (f32[2,520,128]{2,1,0:T(8,128)S(1)}, f32[2,520,128]{2,1,0:T(8,128)S(1)}, u32[]{:S(2)}, u32[]{:S(2)}) collective-permute-start(f32[2,520,128]{2,1,0:T(8,128)S(1)} %all_to_all.10.here), channel_id=1, source_target_pairs={{0,8},{8,16},{16,24},{24,32},{32,40},{40,48},{48,56},{56,64},{64,7... | collective-permute-start | bytes 1597448 | tf_op jit(solution)/shard_map/ppermute | solution.py:346
  34.2 24.8 %collective-permute-start.3 = (f32[2,520,128]{2,1,0:T(8,128)S(1)}, f32[2,520,128]{2,1,0:T(8,128)S(1)}, u32[]{:S(2)}, u32[]{:S(2)}) collective-permute-start(f32[2,520,128]{2,1,0:T(8,128)S(1)} %scatter.9.above1), channel_id=1, source_target_pairs={{0,504},{8,0},{16,8},{24,16},{32,24},{40,32},{48,40},{56,48},{64,5... | collective-permute-start | bytes 1597448 | tf_op jit(solution)/shard_map/ppermute | solution.py:346
  42.0 16.9 %collective-permute-start.1 = (f32[520,128]{1,0:T(8,128)S(1)}, f32[520,128]{1,0:T(8,128)S(1)}, u32[]{:S(2)}, u32[]{:S(2)}) collective-permute-start(f32[520,128]{1,0:T(8,128)S(1)} %scatter.6), channel_id=1, source_target_pairs={{0,8},{8,16},{16,24},{24,32},{32,40},{40,48},{48,56},{56,64},{64,7... | collective-permute-start | bytes 798728 | tf_op jit(solution)/shard_map/ppermute | solution.py:346
  44.0 15.0 %collective-permute-start.6 = (f32[72,512]{1,0:T(8,128)}, f32[72,512]{1,0:T(8,128)S(1)}, u32[]{:S(2)}, u32[]{:S(2)}) collective-permute-start(f32[72,512]{1,0:T(8,128)} %get-tuple-element.36.packed_own), channel_id=1, source_target_pairs={{0,4},{4,0},{1,5},{5,1},{2,6},{6,2},{3,7},{7,3},{8,12},{12,8},{9,1... | collective-permute-start | bytes 442376 | tf_op jit(solution)/shard_map/ppermute | solution.py:352
  45.9 13.1 %collective-permute-start.5 = (f32[2,128]{1,0:T(2,128)S(1)}, f32[2,128]{1,0:T(2,128)S(1)}, u32[]{:S(2)}, u32[]{:S(2)}) collective-permute-start(f32[2,128]{1,0:T(2,128)S(1)} %psum.7.sum_h), channel_id=1, source_target_pairs={{0,496},{8,504},{16,0},{24,8},{32,16},{40,24},{48,32},{56,40},{64,... | collective-permute-start | bytes 3080 | tf_op jit(solution)/shard_map/ppermute | solution.py:346
  49.3 9.7 %collective-permute-start.4 = (f32[1,128]{1,0:T(1,128)S(1)}, f32[1,128]{1,0:T(1,128)S(1)}, u32[]{:S(2)}, u32[]{:S(2)}) collective-permute-start(f32[1,128]{1,0:T(1,128)S(1)} %slice.48), channel_id=1, source_target_pairs={{0,16},{8,24},{16,32},{24,40},{32,48},{40,56},{48,64},{56,72},{64,... | collective-permute-start | bytes 1544 | tf_op jit(solution)/shard_map/ppermute | solution.py:346
  59.0 0.9 copy-start
  63.6 60.9 %all-to-all-start.1 = ((f32[64,4,8,128]{3,2,1,0:T(8,128)}), f32[64,4,8,128]{3,2,1,0:T(8,128)S(1)}, u32[]{:S(2)}, u32[]{:S(2)}) async-start(f32[64,4,8,128]{3,2,1,0:T(8,128)} %grid_tiles.1), calls=%async_computation.1 | async-start | bytes 2097152 | tf_op jit(solution)/shard_map/all_to_all | solution.py:369

commit v3 on v2

--- a/solution.py
+++ b/solution.py
@@ -20,7 +20,7 @@
 HALF_CH = 512
 META = 8
 UNIT = HALF_CH + META
-TOTALS = HALF_CH + BAND // 2 + 1
+SUM_ROW = HALF_CH + BAND // 2
 REACH = 9
 GROUPS = 4
 VMEM_SMOOTH = 52
@@ -136,12 +136,9 @@
 
 
 def grid_kernel(
-    core, below2, below1, here, above1, above2, sum_b2, sum_h, sum_a2, packed_own, packed_other, out,
-    left, right, dense,
+    below2, below1, here, above1, above2, sums, packed_even, packed_odd, out, left, right, dense
 ):
-    me = core[0]
-    for tile in range(CORES):
-        pack = jnp.where(me == tile, packed_own[...], packed_other[...])
+    for tile, pack in enumerate((packed_even, packed_odd)):
         weight = pack[0:KB, :]
         block = pack[KB : KB + 1, :]
         for number in range(PIX // KB):
@@ -149,22 +146,22 @@
             dense[tile, number * KB : (number + 1) * KB, :] = high
             dense[tile, PIX + number * KB : PIX + (number + 1) * KB, :] = low
     slabs = [
-        (below2, sum_b2[0:1, :]),
-        (below1.at[0], below2[TOTALS : TOTALS + 1, :]),
-        (below1.at[1], below2[TOTALS + 1 : TOTALS + 2, :]),
-        (here.at[0], sum_h[0:1, :]),
-        (here.at[1], sum_h[1:2, :]),
-        (above1.at[0], above2[0, TOTALS : TOTALS + 1, :]),
-        (above1.at[1], above2[1, TOTALS : TOTALS + 1, :]),
-        (above2.at[0], sum_a2[0:1, :]),
-        (above2.at[1], sum_a2[1:2, :]),
+        below2,
+        below1.at[0],
+        below1.at[1],
+        here.at[0],
+        here.at[1],
+        above1.at[0],
+        above1.at[1],
+        above2.at[0],
+        above2.at[1],
     ]
     depth = REACH * SLAB
     totals = [jnp.zeros((1, PIX), f32) for _ in range(CORES)]
     sample = lax.broadcasted_iota(jnp.int32, (SLAB, SLAB), 0).astype(f32)
     lane = lax.broadcasted_iota(jnp.int32, (SLAB, SLAB), 1)
-    for index, (unit, band_sum) in enumerate(slabs):
-        scale = CH / band_sum
+    for index, unit in enumerate(slabs):
+        scale = CH / sums[index : index + 1, :]
         high, low = split(unit[0:HALF_CH, :] * scale)
         at = index * SLAB
         left[:, at : at + SLAB] = high
@@ -199,13 +196,13 @@
         out[:, row] = tiles[:, row * TX : (row + 1) * TX].reshape(HALF_CH // 8, 8, TX)
 
 
-def grid_tiles(core, units, sums, packed_own, packed_other):
+def grid_tiles(units, sums, packed_even, packed_odd):
     slots = BAND * CAP
     depth = REACH * SLAB
     return pl.pallas_call(
         grid_kernel,
         out_shape=jax.ShapeDtypeStruct((HALF_CH // 8, CORES * TY, 8, TX), f32),
-        in_specs=[whole(pltpu.SMEM)] + [whole()] * 10,
+        in_specs=[whole()] * 8,
         out_specs=whole(),
         scratch_shapes=[
             VMEM((HALF_CH, 3 * depth), bf16),
@@ -214,7 +211,7 @@
         ],
         compiler_params=pltpu.CompilerParams(vmem_limit_bytes=32 << 20),
         name="grid_tiles",
-    )(core, *units, *sums, packed_own, packed_other)
+    )(*units, sums, packed_even, packed_odd)
 
 
 def waves(length):
@@ -350,20 +347,25 @@
     )
     here = lax.all_to_all(unit, "core", split_axis=0, concat_axis=0, tiled=True)
     packed_other = lax.ppermute(packed, "core", [(0, 1), (1, 0)])
-    above1 = shift(here, -1)
-    below1 = shift(here, 1)
-    sums = lax.psum(here[:, TOTALS - 1, :], "chan")
-    sum_a2, sum_b2 = shift(sums, -2), shift(sums[1:2], 2)
-    above1 = above1.at[:, TOTALS, :].set(sums)
+    part = here[:, SUM_ROW, :]
+    arrived = (
+        shift(here, -1),
+        shift(here, 1),
+        shift(part, -2),
+        shift(part[1:2], 2),
+        packed_other,
+    )
+    above1, below1, part_above2, part_below2, packed_other = lax.optimization_barrier(arrived)
     above2 = shift(above1, -1)
-    below2 = shift(below1[1].at[TOTALS : TOTALS + CORES, :].set(sums), 1)
-    core = lax.axis_index("core").astype(jnp.int32).reshape(1)
+    below2 = shift(below1[1], 1)
+    parts = [part_below2, below1[:, SUM_ROW, :], part, above1[:, SUM_ROW, :], part_above2]
+    sums = lax.psum(jnp.concatenate(parts, axis=0), "chan")
+    even = lax.axis_index("core") == 0
     gridded = grid_tiles(
-        core,
         (below2, below1, here, above1, above2),
-        (sum_b2, sums, sum_a2),
-        packed,
-        packed_other,
+        sums,
+        jnp.where(even, packed, packed_other),
+        jnp.where(even, packed_other, packed),
     )
     gridded, beam_width = lax.optimization_barrier((gridded, beam_width))
     relaid = lax.all_to_all(gridded, ("y", "z"), split_axis=0, concat_axis=0, tiled=True)

time: 128 us -> 124 us (0.969)
  the two profiles are of different devices: /device:TPU:4 before, /device:TPU:32 now
where the time goes in v3:
time: 124 us; the launch traced here: 123 us
  waiting for transfers between devices  47.8 us (39%)
  starting transfers between devices  37.1 us (30%)
  Pallas kernels  18.4 us (15%)
  blocking collectives  16 us (13%)
  other arithmetic  2.87 us (2%)
    all_to_all x1, waiting for transfers between devices, local(): lax.all_to_all(gridded, ('y', 'z'), split_axis=0, concat_axis=0, tiled=True)  40.1 us
    ppermute x6, starting transfers between devices, shift(): lax.ppermute(array, ('y', 'z'), [(i, (i + by) % chips) for i in range(chi...  27 us
    psum x1, blocking collectives, local(): sums = lax.psum(jnp.concatenate(parts, axis=0), 'chan')  10.6 us
    all_to_all x1, starting transfers between devices, local(): lax.all_to_all(gridded, ('y', 'z'), split_axis=0, concat_axis=0, tiled=True)  8.16 us
    pallas_call x1, Pallas kernels, make_tables(): pl.pallas_call(tables_kernel, grid=(channels,), out_shape=(jax.ShapeDtype...  7.87 us
    ppermute x6, waiting for transfers between devices, shift(): lax.ppermute(array, ('y', 'z'), [(i, (i + by) % chips) for i in range(chi...  7.74 us
    all_to_all x1, blocking collectives, local(): here = lax.all_to_all(unit, 'core', split_axis=0, concat_axis=0, tiled=True)  5.37 us
    pallas_call x1, Pallas kernels, grid_tiles(): pl.pallas_call(grid_kernel, out_shape=jax.ShapeDtypeStruct((HALF_CH // 8,...  3.7 us
  transfers between devices with their start and end apart: 8, of which 2 were waited for; matrix products, arithmetic and copies ran while one was open for 3% of the time, Pallas kernels for 6%

profile of v3, /device:TPU:32, one launch (start us, length us, event | category | flops | bytes accessed | tf_op | source)
XLA Modules:
  0.0 123.1 jit_solution(5145414760202988170)
XLA Ops:
  0.0 3.4 %prepare.1 = (f32[2,520,128]{2,1,0:T(8,128)}, f32[72,512]{1,0:T(8,128)}) custom-call(s32[8]{0:T(128)} %counts.1, f32[128,1024]{1,0:T(8,128)} %spectra_in.1, s32[1,128]{1,0:T(1,128)} %bitcast.17, f32[19,1024]{1,0:T(8,128)} %feed_gain_in.1, s32[8,64]{1,0:T(8,128)} %send_list_in.1, f32[64,512]{1,0:T(8,128)} %bitcast.15, s32[1,512]{1,0:T(1,128)} %bitcast.16), custom_call_target="tpu_custom_call" | custom-call | tf_op jit(solution)/shard_map/prepare/pallas_call | solution.py:108
  3.4 0.0 copy-start
  3.4 5.4 %all_to_all.10.here = f32[2,520,128]{2,1,0:T(8,128)S(1)} all-to-all(f32[2,520,128]{2,1,0:T(8,128)} %get-tuple-element.16), channel_id=1, replica_groups=mesh['y'=4,'z'=16,'core'=2,'chan'=4] {'core'}, dimensions={0} | all-to-all | bytes 1064960 | tf_op jit(solution)/shard_map/all_to_all | solution.py:348
  8.8 0.3 copy.14
  9.1 3.8 %collective-permute-start.1 = (f32[2,520,128]{2,0,1:T(2,128)S(1)}, f32[2,520,128]{2,0,1:T(2,128)S(1)}, u32[]{:S(2)}, u32[]{:S(2)}) collective-permute-start(f32[2,520,128]{2,0,1:T(2,128)S(1)} %copy.14), channel_id=1, source_target_pairs={{0,8},{8,16},{16,24},{24,32},{32,40},{40,48},{48,56},{56,64},{64,7... | collective-permute-start | bytes 1597448 | tf_op jit(solution)/shard_map/ppermute | solution.py:343
  12.9 5.5 %collective-permute-start = (f32[2,520,128]{2,0,1:T(2,128)S(1)}, f32[2,520,128]{2,0,1:T(2,128)S(1)}, u32[]{:S(2)}, u32[]{:S(2)}) collective-permute-start(f32[2,520,128]{2,0,1:T(2,128)S(1)} %copy.14), channel_id=1, source_target_pairs={{0,504},{8,0},{16,8},{24,16},{32,24},{40,32},{48,40},{56,48},{64,5... | collective-permute-start | bytes 1597448 | tf_op jit(solution)/shard_map/ppermute | solution.py:343
  18.4 0.0 copy-done
  18.4 1.9 %collective-permute-start.4 = (f32[72,512]{1,0:T(8,128)S(1)}, f32[72,512]{1,0:T(8,128)S(1)}, u32[]{:S(2)}, u32[]{:S(2)}) collective-permute-start(f32[72,512]{1,0:T(8,128)S(1)} %copy-done), channel_id=1, source_target_pairs={{0,4},{4,0},{1,5},{5,1},{2,6},{6,2},{3,7},{7,3},{8,12},{12,8},{9,1... | collective-permute-start | bytes 442376 | tf_op jit(solution)/shard_map/ppermute | solution.py:349
  20.4 9.9 %collective-permute-start.2 = (f32[2,128]{1,0:T(2,128)S(1)}, f32[2,128]{1,0:T(2,128)S(1)}, u32[]{:S(2)}, u32[]{:S(2)}) collective-permute-start(f32[2,128]{1,0:T(2,128)S(1)} %slice_bitcast_fusion), channel_id=1, source_target_pairs={{0,496},{8,504},{16,0},{24,8},{32,16},{40,24},{48,32},{56,40},{64,... | collective-permute-start | bytes 3080 | tf_op jit(solution)/shard_map/ppermute | solution.py:343
  30.3 1.9 %collective-permute-start.3 = (f32[1,128]{1,0:T(1,128)S(1)}, f32[1,128]{1,0:T(1,128)S(1)}, u32[]{:S(2)}, u32[]{:S(2)}) collective-permute-start(f32[1,128]{1,0:T(1,128)S(1)} %slice_bitcast_fusion.3), channel_id=1, source_target_pairs={{0,16},{8,24},{16,32},{24,40},{32,48},{40,56},{48,64},{56,72},{64,... | collective-permute-start | bytes 1544 | tf_op jit(solution)/shard_map/ppermute | solution.py:343
  32.2 7.7 %collective-permute-done.3 = f32[1,128]{1,0:T(1,128)S(1)} collective-permute-done((f32[1,128]{1,0:T(1,128)S(1)}, f32[1,128]{1,0:T(1,128)S(1)}, u32[]{:S(2)}, u32[]{:S(2)}) %collective-permute-start.3) | collective-permute-done | bytes 544 | tf_op jit(solution)/shard_map/ppermute | solution.py:343
  40.0 0.0 collective-permute-done.2
  40.0 0.0 collective-permute-done.4
  40.0 0.0 collective-permute-done.1
  40.0 0.0 collective-permute-done
  40.0 2.9 %collective-permute-start.6 = (f32[2,520,128]{2,0,1:T(2,128)S(1)}, f32[2,520,128]{2,0,1:T(2,128)S(1)}, u32[]{:S(2)}, u32[]{:S(2)}) collective-permute-start(f32[2,520,128]{2,0,1:T(2,128)S(1)} %collective-permute-done), channel_id=1, source_target_pairs={{0,504},{8,0},{16,8},{24,16},{32,24},{40,32},{48,40},{56,48},{64,5... | collective-permute-start | bytes 1597448 | tf_op jit(solution)/shard_map/ppermute | solution.py:343
  42.9 0.3 slice.22
  43.2 2.9 %collective-permute-start.5 = (f32[520,128]{1,0:T(8,128)S(1)}, f32[520,128]{1,0:T(8,128)S(1)}, u32[]{:S(2)}, u32[]{:S(2)}) collective-permute-start(f32[520,128]{1,0:T(8,128)S(1)} %bitcast.14), channel_id=1, source_target_pairs={{0,8},{8,16},{16,24},{24,32},{32,40},{40,48},{48,56},{56,64},{64,7... | collective-permute-start | bytes 798728 | tf_op jit(solution)/shard_map/ppermute | solution.py:343
  46.2 0.1 concatenate.9
  46.3 10.6 %psum.7.sums = f32[9,128]{1,0:T(8,128)S(1)} all-reduce(f32[9,128]{1,0:T(8,128)S(1)} %concatenate.9), channel_id=1, replica_groups=mesh['y'=4,'z'=16,'core'=2,'chan'=4] {'chan'}, use_global_device_ids=true, to_apply=%region_0.0 | all-reduce | flops 1152 | bytes 9216 | tf_op jit(solution)/shard_map/psum | solution.py:362
  57.0 0.0 collective-permute-done.6
  57.0 0.0 collective-permute-done.5.below2
  57.1 3.7 %grid_tiles.1 = f32[64,4,8,128]{3,2,1,0:T(8,128)} custom-call(f32[520,128]{1,0:T(8,128)S(1)} %collective-permute-done.5.below2, f32[2,520,128]{2,1,0:T(8,128)S(1)} %copy.17.below1, f32[2,520,128]{2,1,0:T(8,128)S(1)} %all_to_all.10.here, f32[2,520,128]{2,1,0:T(8,128)S(1)} %copy.18.above1, f32[2,520,128]{2,1,0:T(8,128)S(1)} %copy.19.above2, ...), custom_call_target="tpu_custom_call" | custom-call | tf_op jit(solution)/shard_map/grid_tiles/pallas_call | solution.py:202
  60.8 8.2 %all-to-all-start.1 = ((f32[64,4,8,128]{3,2,1,0:T(8,128)}), f32[64,4,8,128]{3,2,1,0:T(8,128)S(1)}, u32[]{:S(2)}, u32[]{:S(2)}) async-start(f32[64,4,8,128]{3,2,1,0:T(8,128)} %grid_tiles.1), calls=%async_computation.1 | async-start | bytes 2097152 | tf_op jit(solution)/shard_map/all_to_all | solution.py:371
  68.9 0.3 fusion.14
  69.2 0.7 pad_maximum_fusion.1.column_waves
  69.9 1.0 fusion.6
  70.9 0.9 pad_maximum_fusion.row_waves
  71.8 7.9 %smoothing_tables.1 = (bf16[8,2,256,256]{3,2,1,0:T(8,128)(2,1)}, bf16[8,256,256]{2,1,0:T(8,128)(2,1)}) custom-call(f32[8]{0:T(128)} %sigma, f32[256,512]{1,0:T(8,128)} %pad_maximum_fusion.row_waves, f32[128,256]{1,0:T(8,128)} %pad_maximum_fusion.1.column_waves), custom_call_target="tpu_custom_call" | custom-call | flops 3221225472 | bytes 6291456 | tf_op jit(solution)/shard_map/smoothing_tables/pallas_call | solution.py:261
  79.6 40.1 %all-to-all-done.1 = f32[64,4,8,128]{3,2,1,0:T(8,128)S(1)} async-done(((f32[64,4,8,128]{3,2,1,0:T(8,128)}), f32[64,4,8,128]{3,2,1,0:T(8,128)S(1)}, u32[]{:S(2)}, u32[]{:S(2)}) %all-to-all-start.1) | async-done | bytes 1048608 | tf_op jit(solution)/shard_map/all_to_all | solution.py:371
  119.7 3.4 %smooth.1 = f32[8,256,128]{2,1,0:T(8,128)} custom-call(f32[2048,128]{1,0:T(8,128)S(1)} %bitcast.13, bf16[8,2,256,256]{3,2,1,0:T(8,128)(2,1)} %get-tuple-element.25.rows_in, bf16[8,256,256]{2,1,0:T(8,128)(2,1)} %get-tuple-element.26.columns_in), custom_call_target="tpu_custom_call" | custom-call | tf_op jit(solution)/shard_map/smooth/pallas_call | solution.py:319
  (7 shorter events, 0.1 us)
Async XLA Ops:
  3.4 15.0 %copy-start = (f32[72,512]{1,0:T(8,128)S(1)}, f32[72,512]{1,0:T(8,128)}, u32[]{:S(2)}) copy-start(f32[72,512]{1,0:T(8,128)} %get-tuple-element.17) | copy-start | bytes 442372
  9.1 30.9 %collective-permute-start.1 = (f32[2,520,128]{2,0,1:T(2,128)S(1)}, f32[2,520,128]{2,0,1:T(2,128)S(1)}, u32[]{:S(2)}, u32[]{:S(2)}) collective-permute-start(f32[2,520,128]{2,0,1:T(2,128)S(1)} %copy.14), channel_id=1, source_target_pairs={{0,8},{8,16},{16,24},{24,32},{32,40},{40,48},{48,56},{56,64},{64,7... | collective-permute-start | bytes 1597448 | tf_op jit(solution)/shard_map/ppermute | solution.py:343
  12.9 27.1 %collective-permute-start = (f32[2,520,128]{2,0,1:T(2,128)S(1)}, f32[2,520,128]{2,0,1:T(2,128)S(1)}, u32[]{:S(2)}, u32[]{:S(2)}) collective-permute-start(f32[2,520,128]{2,0,1:T(2,128)S(1)} %copy.14), channel_id=1, source_target_pairs={{0,504},{8,0},{16,8},{24,16},{32,24},{40,32},{48,40},{56,48},{64,5... | collective-permute-start | bytes 1597448 | tf_op jit(solution)/shard_map/ppermute | solution.py:343
  18.4 21.5 %collective-permute-start.4 = (f32[72,512]{1,0:T(8,128)S(1)}, f32[72,512]{1,0:T(8,128)S(1)}, u32[]{:S(2)}, u32[]{:S(2)}) collective-permute-start(f32[72,512]{1,0:T(8,128)S(1)} %copy-done), channel_id=1, source_target_pairs={{0,4},{4,0},{1,5},{5,1},{2,6},{6,2},{3,7},{7,3},{8,12},{12,8},{9,1... | collective-permute-start | bytes 442376 | tf_op jit(solution)/shard_map/ppermute | solution.py:349
  20.4 19.6 %collective-permute-start.2 = (f32[2,128]{1,0:T(2,128)S(1)}, f32[2,128]{1,0:T(2,128)S(1)}, u32[]{:S(2)}, u32[]{:S(2)}) collective-permute-start(f32[2,128]{1,0:T(2,128)S(1)} %slice_bitcast_fusion), channel_id=1, source_target_pairs={{0,496},{8,504},{16,0},{24,8},{32,16},{40,24},{48,32},{56,40},{64,... | collective-permute-start | bytes 3080 | tf_op jit(solution)/shard_map/ppermute | solution.py:343
  30.3 9.7 %collective-permute-start.3 = (f32[1,128]{1,0:T(1,128)S(1)}, f32[1,128]{1,0:T(1,128)S(1)}, u32[]{:S(2)}, u32[]{:S(2)}) collective-permute-start(f32[1,128]{1,0:T(1,128)S(1)} %slice_bitcast_fusion.3), channel_id=1, source_target_pairs={{0,16},{8,24},{16,32},{24,40},{32,48},{40,56},{48,64},{56,72},{64,... | collective-permute-start | bytes 1544 | tf_op jit(solution)/shard_map/ppermute | solution.py:343
  40.0 17.0 %collective-permute-start.6 = (f32[2,520,128]{2,0,1:T(2,128)S(1)}, f32[2,520,128]{2,0,1:T(2,128)S(1)}, u32[]{:S(2)}, u32[]{:S(2)}) collective-permute-start(f32[2,520,128]{2,0,1:T(2,128)S(1)} %collective-permute-done), channel_id=1, source_target_pairs={{0,504},{8,0},{16,8},{24,16},{32,24},{40,32},{48,40},{56,48},{64,5... | collective-permute-start | bytes 1597448 | tf_op jit(solution)/shard_map/ppermute | solution.py:343
  43.2 13.9 %collective-permute-start.5 = (f32[520,128]{1,0:T(8,128)S(1)}, f32[520,128]{1,0:T(8,128)S(1)}, u32[]{:S(2)}, u32[]{:S(2)}) collective-permute-start(f32[520,128]{1,0:T(8,128)S(1)} %bitcast.14), channel_id=1, source_target_pairs={{0,8},{8,16},{16,24},{24,32},{32,40},{40,48},{48,56},{56,64},{64,7... | collective-permute-start | bytes 798728 | tf_op jit(solution)/shard_map/ppermute | solution.py:343
  60.8 59.0 %all-to-all-start.1 = ((f32[64,4,8,128]{3,2,1,0:T(8,128)}), f32[64,4,8,128]{3,2,1,0:T(8,128)S(1)}, u32[]{:S(2)}, u32[]{:S(2)}) async-start(f32[64,4,8,128]{3,2,1,0:T(8,128)} %grid_tiles.1), calls=%async_computation.1 | async-start | bytes 2097152 | tf_op jit(solution)/shard_map/all_to_all | solution.py:371

commit v4 on v3

--- a/solution.py
+++ b/solution.py
@@ -20,9 +20,9 @@
 HALF_CH = 512
 META = 8
 UNIT = HALF_CH + META
-SUM_ROW = HALF_CH + BAND // 2
 REACH = 9
-GROUPS = 4
+GROUPS = 8
+PARTS = 4
 VMEM_SMOOTH = 52
 VMEM_PREPARE = 56
 PIX = TY * TX
@@ -43,84 +43,123 @@
 
 
 def prepare_kernel(
-    counts,
+    counts_in,
     spectra_in,
     feed_ids_in,
     feed_gain_in,
     send_list_in,
     weights_in,
     blocks_in,
-    unit,
-    packed,
+    unit_out,
+    packed_out,
+    counts,
     spectra,
     feed_ids,
     feed_gain,
     gains,
     send_list,
     blocks,
+    unit,
+    packed,
     arrived,
+    left,
 ):
-    feeds = feed_gain_in.shape[0]
+    feeds, channels = feed_gain.shape
+    width = channels // PARTS
+    rows = HALF_CH // PARTS
+    room = gains.shape[0] // 3
     copies = []
-    for source, target in (
-        (feed_ids_in, feed_ids),
-        (feed_gain_in, feed_gain),
-        (spectra_in, spectra),
-        (send_list_in, send_list),
-        (blocks_in, blocks),
-        (weights_in, packed.at[0:KB]),
-    ):
+
+    def fetch(source, target):
         copies.append(pltpu.make_async_copy(source, target, arrived.at[len(copies)]))
         copies[-1].start()
+
+    fetch(feed_ids_in, feed_ids)
+    fetch(feed_gain_in, feed_gain)
+    for part in range(PARTS):
+        columns = pl.ds(part * width, width)
+        fetch(spectra_in.at[:, columns], spectra.at[part])
+    fetch(send_list_in, send_list)
+    fetch(blocks_in, blocks)
+    fetch(weights_in, packed.at[0:KB])
+    fetch(counts_in, counts)
     gains[...] = jnp.zeros_like(gains)
     copies[0].wait()
     copies[1].wait()
-    gains[0:feeds, :] = feed_gain[...]
-    onehot = (lax.broadcasted_iota(jnp.int32, (gains.shape[0], SLAB), 0) == feed_ids[...]).astype(
-        f32
-    )
-    gain_rows = lax.dot_general(
-        gains[...], onehot, (((0,), (0,)), ((), ())), precision=highest, preferred_element_type=f32
-    )
-    copies[2].wait()
-    raw = spectra[...].T
-    band_sum = jnp.sum(raw, axis=0, keepdims=True)
-    scaled = (raw * gain_rows).reshape(HALF_CH // 8, CORES, 8, SLAB)
-    copies[3].wait()
+    value = feed_gain[...]
+    for step in range(3):
+        piece = value.astype(bf16)
+        value = value - piece.astype(f32)
+        gains[step * room : step * room + feeds, :] = piece.astype(f32)
+    onehot = (
+        lax.broadcasted_iota(jnp.int32, (3 * room, SLAB), 0) % room == feed_ids[...]
+    ).astype(f32)
+    onehot = onehot.astype(bf16)
+    band_sum = jnp.zeros((1, SLAB), f32)
+    sends = []
+
+    def send(source, target):
+        sends.append(pltpu.make_async_copy(source, target, left.at[len(sends)]))
+        sends[-1].start()
+
+    for part in range(PARTS):
+        gain_rows = lax.dot_general(
+            gains[:, part * width : (part + 1) * width].astype(bf16),
+            onehot,
+            (((0,), (0,)), ((), ())),
+            preferred_element_type=f32,
+        )
+        copies[2 + part].wait()
+        raw = spectra[part].T
+        band_sum = band_sum + jnp.sum(raw, axis=0, keepdims=True)
+        scaled = (raw * gain_rows).reshape(rows // 8, CORES, 8, SLAB)
+        for core in range(CORES):
+            unit[core, part * rows : (part + 1) * rows, :] = scaled[:, core].reshape(rows, SLAB)
+        span = pl.ds(part * rows, rows)
+        send(unit.at[:, span], unit_out.at[:, span])
+    copies[2 + PARTS].wait()
+    copies[5 + PARTS].wait()
     lane = lax.broadcasted_iota(jnp.int32, (1, CAP), 1)
-    rows = [
+    lists = [
         jnp.where(lane < counts[row], send_list[row : row + 1, :], -1).astype(f32)
         for row in range(BAND)
     ]
-    rows = [jnp.concatenate(rows[2 * m : 2 * m + 2], axis=1) for m in range(BAND // 2)]
-    meta = jnp.concatenate(rows + [band_sum, jnp.zeros((META - BAND // 2 - 1, SLAB), f32)], axis=0)
+    lists = [jnp.concatenate(lists[2 * m : 2 * m + 2], axis=1) for m in range(BAND // 2)]
+    meta = jnp.concatenate(lists + [band_sum, jnp.zeros((META - BAND // 2 - 1, SLAB), f32)], axis=0)
     for core in range(CORES):
-        unit[core, 0:HALF_CH, :] = scaled[:, core].reshape(HALF_CH, SLAB)
         unit[core, HALF_CH:UNIT, :] = meta
-    copies[4].wait()
+    span = pl.ds(HALF_CH, META)
+    send(unit.at[:, span], unit_out.at[:, span])
+    copies[3 + PARTS].wait()
     packed[KB : KB + 8, :] = jnp.broadcast_to(blocks[...].astype(f32), (8, BAND * CAP))
-    copies[5].wait()
+    copies[4 + PARTS].wait()
+    send(packed, packed_out)
+    for copy in sends:
+        copy.wait()
 
 
 def prepare(spectra, feed_ids, feed_gain, send_list, send_count, kernel_weight, pixel_block):
     slots = BAND * CAP
     channels = spectra.shape[1]
+    unit = (CORES, UNIT, SLAB)
+    packed = (KB + 8, slots)
     return pl.pallas_call(
         prepare_kernel,
-        out_shape=(
-            jax.ShapeDtypeStruct((CORES, UNIT, SLAB), f32),
-            jax.ShapeDtypeStruct((KB + 8, slots), f32),
-        ),
-        in_specs=[whole(pltpu.SMEM)] + [whole(pltpu.HBM)] * 6,
-        out_specs=(whole(), whole()),
+        out_shape=(jax.ShapeDtypeStruct(unit, f32), jax.ShapeDtypeStruct(packed, f32)),
+        in_specs=[whole(pltpu.HBM)] * 7,
+        out_specs=(whole(pltpu.HBM), whole(pltpu.HBM)),
         scratch_shapes=[
-            VMEM((SLAB, channels), f32),
+            pltpu.SMEM(send_count.shape, jnp.int32),
+            VMEM((PARTS, SLAB, channels // PARTS), f32),
             VMEM((1, SLAB), jnp.int32),
             VMEM(feed_gain.shape, f32),
-            VMEM((24, channels), f32),
+            VMEM((3 * 32, channels), f32),
             VMEM((BAND, CAP), jnp.int32),
             VMEM((1, slots), jnp.int32),
-            pltpu.SemaphoreType.DMA((6,)),
+            VMEM(unit, f32),
+            VMEM(packed, f32),
+            pltpu.SemaphoreType.DMA((6 + PARTS,)),
+            pltpu.SemaphoreType.DMA((2 + PARTS,)),
         ],
         compiler_params=pltpu.CompilerParams(vmem_limit_bytes=VMEM_PREPARE << 20),
         name="prepare",
@@ -136,7 +175,8 @@
 
 
 def grid_kernel(
-    below2, below1, here, above1, above2, sums, packed_even, packed_odd, out, left, right, dense
+    below2, below1, here, above1, above2, sums, packed_even, packed_odd, out,
+    left_high, left_low, right, dense, tiles, done,
 ):
     for tile, pack in enumerate((packed_even, packed_odd)):
         weight = pack[0:KB, :]
@@ -145,35 +185,31 @@
             high, low = split(jnp.where(block == number, weight, 0.0))
             dense[tile, number * KB : (number + 1) * KB, :] = high
             dense[tile, PIX + number * KB : PIX + (number + 1) * KB, :] = low
+    first, second = pl.ds(0, UNIT), pl.ds(UNIT, UNIT)
     slabs = [
+        here.at[first],
+        here.at[second],
+        below1.at[first],
+        below1.at[second],
+        above1.at[first],
+        above1.at[second],
         below2,
-        below1.at[0],
-        below1.at[1],
-        here.at[0],
-        here.at[1],
-        above1.at[0],
-        above1.at[1],
-        above2.at[0],
-        above2.at[1],
+        above2.at[first],
+        above2.at[second],
     ]
-    depth = REACH * SLAB
+    places = [3, 4, 1, 2, 5, 6, 0, 7, 8]
     totals = [jnp.zeros((1, PIX), f32) for _ in range(CORES)]
     sample = lax.broadcasted_iota(jnp.int32, (SLAB, SLAB), 0).astype(f32)
     lane = lax.broadcasted_iota(jnp.int32, (SLAB, SLAB), 1)
-    for index, unit in enumerate(slabs):
+    for index, unit in zip(places, slabs):
         scale = CH / sums[index : index + 1, :]
         high, low = split(unit[0:HALF_CH, :] * scale)
         at = index * SLAB
-        left[:, at : at + SLAB] = high
-        left[:, depth + at : depth + at + SLAB] = low
-        left[:, 2 * depth + at : 2 * depth + at + SLAB] = high
+        left_high[:, at : at + SLAB] = high
+        left_low[:, at : at + SLAB] = low
         for tile in range(CORES):
             offset = tile + BAND - 1 - index
-            columns = slice(tile * PIX, (tile + 1) * PIX)
             if not 0 <= offset < BAND:
-                for copy in range(3):
-                    start = copy * depth + at
-                    right[start : start + SLAB, columns] = jnp.zeros((SLAB, PIX), bf16)
                 continue
             pair = offset // 2
             chosen = unit[HALF_CH + pair : HALF_CH + pair + 1, :]
@@ -184,16 +220,21 @@
                 (((1,), (1,)), ((), ())),
                 preferred_element_type=f32,
             )
-            top, rest = picked[:, 0:PIX], picked[:, PIX:]
-            totals[tile] = totals[tile] + jnp.sum(top + rest, axis=0, keepdims=True)
-            top, rest = top.astype(bf16), rest.astype(bf16)
-            right[at : at + SLAB, columns] = top
-            right[depth + at : depth + at + SLAB, columns] = top
-            right[2 * depth + at : 2 * depth + at + SLAB, columns] = rest
-    total = jnp.maximum(jnp.concatenate(totals, axis=1), 1.0)
-    tiles = jnp.dot(left[...], right[...], preferred_element_type=f32) / total
-    for row in range(CORES * TY):
-        out[:, row] = tiles[:, row * TX : (row + 1) * TX].reshape(HALF_CH // 8, 8, TX)
+            totals[tile] = totals[tile] + jnp.sum(
+                picked[:, 0:PIX] + picked[:, PIX:], axis=0, keepdims=True
+            )
+            start = (index - tile) * SLAB
+            right[tile, start : start + SLAB, :] = picked.astype(bf16)
+    copies = []
+    for tile in range(CORES):
+        span = slice(tile * SLAB, (tile + BAND) * SLAB)
+        both = jnp.dot(left_high[:, span], right[tile], preferred_element_type=f32)
+        rest = jnp.dot(left_low[:, span], right[tile, :, 0:PIX], preferred_element_type=f32)
+        gridded = (both[:, 0:PIX] + both[:, PIX:] + rest) / jnp.maximum(totals[tile], 1.0)
+        for row in range(TY):
+            out[:, tile * TY + row] = gridded[:, row * TX : (row + 1) * TX].reshape(
+                HALF_CH // 8, 8, TX
+            )
 
 
 def grid_tiles(units, sums, packed_even, packed_odd):
@@ -205,9 +246,12 @@
         in_specs=[whole()] * 8,
         out_specs=whole(),
         scratch_shapes=[
-            VMEM((HALF_CH, 3 * depth), bf16),
-            VMEM((3 * depth, CORES * PIX), bf16),
+            VMEM((HALF_CH, depth), bf16),
+            VMEM((HALF_CH, depth), bf16),
+            VMEM((CORES, BAND * SLAB, 2 * PIX), bf16),
             VMEM((CORES, 2 * PIX, slots), bf16),
+            VMEM((CORES, HALF_CH // 8, TY, 8, TX), f32),
+            pltpu.SemaphoreType.DMA((CORES,)),
         ],
         compiler_params=pltpu.CompilerParams(vmem_limit_bytes=32 << 20),
         name="grid_tiles",
@@ -334,6 +378,11 @@
     )(field, rows_table, columns_table)
 
 
+def sum_rows(block):
+    starts = range(HALF_CH + BAND // 2, block.shape[0], UNIT)
+    return jnp.concatenate([block[start : start + 1] for start in starts], axis=0)
+
+
 def local(
     spectra, feed_ids, feed_gain, send_list, send_count, kernel_weight, pixel_block, beam_width
 ):
@@ -345,20 +394,15 @@
     unit, packed = prepare(
         spectra, feed_ids, feed_gain, send_list, send_count, kernel_weight, pixel_block
     )
+    unit = unit.reshape(CORES * UNIT, SLAB)
     here = lax.all_to_all(unit, "core", split_axis=0, concat_axis=0, tiled=True)
     packed_other = lax.ppermute(packed, "core", [(0, 1), (1, 0)])
-    part = here[:, SUM_ROW, :]
-    arrived = (
-        shift(here, -1),
-        shift(here, 1),
-        shift(part, -2),
-        shift(part[1:2], 2),
-        packed_other,
-    )
-    above1, below1, part_above2, part_below2, packed_other = lax.optimization_barrier(arrived)
+    above1, below1 = shift(here, -1), shift(here, 1)
+    part_above2 = shift(sum_rows(here), -2)
+    part_below2 = shift(sum_rows(here)[1:], 2)
     above2 = shift(above1, -1)
-    below2 = shift(below1[1], 1)
-    parts = [part_below2, below1[:, SUM_ROW, :], part, above1[:, SUM_ROW, :], part_above2]
+    below2 = shift(below1[UNIT:], 1)
+    parts = [part_below2] + [sum_rows(block) for block in (below1, here, above1)] + [part_above2]
     sums = lax.psum(jnp.concatenate(parts, axis=0), "chan")
     even = lax.axis_index("core") == 0
     gridded = grid_tiles(

time: 124 us -> 121 us (0.976)
  waiting for transfers between devices: 47.8 us -> 40.5 us
  starting transfers between devices: 37.1 us -> 42.3 us
    ppermute x6, waiting for transfers between devices: 7.74 us -> 0.02 us  [shift(): lax.ppermute(array, ('y', 'z'), [(i, (i + by) % chips) for i in range(chi...]
    ppermute x6, starting transfers between devices: 27 us -> 30.3 us  [shift(): lax.ppermute(array, ('y', 'z'), [(i, (i + by) % chips) for i in range(chi...]
    all_to_all x1, starting transfers between devices: 8.16 us -> 10.1 us  [local(): lax.all_to_all(gridded, ('y', 'z'), split_axis=0, concat_axis=0, tiled=True)]
  transfers between devices with their start and end apart: 8 -> 8, of which waited for: 2 -> 1; matrix products, arithmetic and copies ran while one was open for 3% -> 3% of each run, Pallas kernels for 6% -> 7%
where the time goes in v4:
time: 121 us; the launch traced here: 120 us
  starting transfers between devices  42.3 us (35%)
  waiting for transfers between devices  40.5 us (33%)
  Pallas kernels  17.5 us (14%)
  blocking collectives  15.8 us (13%)
  other arithmetic  3.77 us (3%)
    all_to_all x1, waiting for transfers between devices, local(): lax.all_to_all(gridded, ('y', 'z'), split_axis=0, concat_axis=0, tiled=True)  40.5 us
    ppermute x6, starting transfers between devices, shift(): lax.ppermute(array, ('y', 'z'), [(i, (i + by) % chips) for i in range(chi...  30.3 us
    psum x1, blocking collectives, local(): sums = lax.psum(jnp.concatenate(parts, axis=0), 'chan')  10.6 us
    all_to_all x1, starting transfers between devices, local(): lax.all_to_all(gridded, ('y', 'z'), split_axis=0, concat_axis=0, tiled=True)  10.1 us
    pallas_call x1, Pallas kernels, make_tables(): pl.pallas_call(tables_kernel, grid=(channels,), out_shape=(jax.ShapeDtype...  7.87 us
    all_to_all x1, blocking collectives, local(): here = lax.all_to_all(unit, 'core', split_axis=0, concat_axis=0, tiled=True)  5.24 us
    pallas_call x1, Pallas kernels, grid_tiles(): pl.pallas_call(grid_kernel, out_shape=jax.ShapeDtypeStruct((HALF_CH // 8,...  3.5 us
    pallas_call x1, Pallas kernels, smooth(): pl.pallas_call(smooth_kernel, out_shape=jax.ShapeDtypeStruct((channels, l...  3.37 us
  transfers between devices with their start and end apart: 8, of which 1 were waited for; matrix products, arithmetic and copies ran while one was open for 3% of the time, Pallas kernels for 7%

profile of v4, /device:TPU:32, one launch (start us, length us, event | category | flops | bytes accessed | tf_op | source)
XLA Modules:
  0.0 120.3 jit_solution(3135410161832153882)
XLA Ops:
  0.0 2.8 %prepare.1 = (f32[2,520,128]{2,1,0:T(8,128)}, f32[72,512]{1,0:T(8,128)}) custom-call(s32[8]{0:T(128)} %counts_in.1, f32[128,1024]{1,0:T(8,128)} %spectra_in.1, s32[1,128]{1,0:T(1,128)} %bitcast.12, f32[19,1024]{1,0:T(8,128)} %feed_gain_in.1, s32[8,64]{1,0:T(8,128)} %send_list_in.1, f32[64,512]{1,0:T(8,128)} %bitcast.10, s32[1,512]{1,0:T(1,128)} %bitcast.11), custom_call_target="tpu_custom_call" | custom-call | tf_op jit(solution)/shard_map/prepare/pallas_call | solution.py:146
  2.8 5.2 %all_to_all.13 = f32[2,520,128]{2,1,0:T(8,128)S(1)} all-to-all(f32[2,520,128]{2,1,0:T(8,128)} %get-tuple-element.11), channel_id=1, replica_groups=mesh['y'=4,'z'=16,'core'=2,'chan'=4] {'core'}, dimensions={0} | all-to-all | bytes 1064960 | tf_op jit(solution)/shard_map/all_to_all | solution.py:398
  8.0 7.4 %collective-permute-start.2 = (f32[1040,128]{1,0:T(8,128)S(1)}, f32[1040,128]{1,0:T(8,128)S(1)}, u32[]{:S(2)}, u32[]{:S(2)}) collective-permute-start(f32[1040,128]{1,0:T(8,128)S(1)} %bitcast.6), channel_id=1, source_target_pairs={{0,504},{8,0},{16,8},{24,16},{32,24},{40,32},{48,40},{56,48},{64,5... | collective-permute-start | bytes 1597448 | tf_op jit(solution)/shard_map/ppermute | solution.py:392
  15.4 1.9 %collective-permute-start = (f32[1040,128]{1,0:T(8,128)S(1)}, f32[1040,128]{1,0:T(8,128)S(1)}, u32[]{:S(2)}, u32[]{:S(2)}) collective-permute-start(f32[1040,128]{1,0:T(8,128)S(1)} %bitcast.7), channel_id=1, source_target_pairs={{0,8},{8,16},{16,24},{24,32},{32,40},{40,48},{48,56},{56,64},{64,7... | collective-permute-start | bytes 1597448 | tf_op jit(solution)/shard_map/ppermute | solution.py:392
  17.3 1.9 %collective-permute-start.6 = (f32[72,512]{1,0:T(8,128)}, f32[72,512]{1,0:T(8,128)S(1)}, u32[]{:S(2)}, u32[]{:S(2)}) collective-permute-start(f32[72,512]{1,0:T(8,128)} %get-tuple-element.12), channel_id=1, source_target_pairs={{0,4},{4,0},{1,5},{5,1},{2,6},{6,2},{3,7},{7,3},{8,12},{12,8},{9,1... | collective-permute-start | bytes 442376 | tf_op jit(solution)/shard_map/ppermute | solution.py:399
  19.3 2.9 %collective-permute-start.4 = (f32[1,128]{1,0:T(1,128)S(1)}, f32[1,128]{1,0:T(1,128)S(1)}, u32[]{:S(2)}, u32[]{:S(2)}) collective-permute-start(f32[1,128]{1,0:T(1,128)S(1)} %get-tuple-element.20), channel_id=1, source_target_pairs={{0,16},{8,24},{16,32},{24,40},{32,48},{40,56},{48,64},{56,72},{64,... | collective-permute-start | bytes 1544 | tf_op jit(solution)/shard_map/ppermute | solution.py:392
  22.2 12.2 %collective-permute-start.5 = (f32[2,128]{1,0:T(2,128)S(1)}, f32[2,128]{1,0:T(2,128)S(1)}, u32[]{:S(2)}, u32[]{:S(2)}) collective-permute-start(f32[2,128]{1,0:T(2,128)S(1)} %pad_maximum_fusion.2), channel_id=1, source_target_pairs={{0,496},{8,504},{16,0},{24,8},{32,16},{40,24},{48,32},{56,40},{64,... | collective-permute-start | bytes 3080 | tf_op jit(solution)/shard_map/ppermute | solution.py:392
  34.5 0.0 collective-permute-done.2.above1
  34.5 3.4 %collective-permute-start.3 = (f32[1040,128]{1,0:T(8,128)S(1)}, f32[1040,128]{1,0:T(8,128)S(1)}, u32[]{:S(2)}, u32[]{:S(2)}) collective-permute-start(f32[1040,128]{1,0:T(8,128)S(1)} %collective-permute-done.2.above1), channel_id=1, source_target_pairs={{0,504},{8,0},{16,8},{24,16},{32,24},{40,32},{48,40},{56,48},{64,5... | collective-permute-start | bytes 1597448 | tf_op jit(solution)/shard_map/ppermute | solution.py:392
  37.9 0.0 collective-permute-done.6
  37.9 0.9 broadcast_select_fusion
  38.8 0.0 collective-permute-done.below1
  38.9 2.5 %collective-permute-start.1 = (f32[520,128]{1,0:T(8,128)S(1)}, f32[520,128]{1,0:T(8,128)S(1)}, u32[]{:S(2)}, u32[]{:S(2)}) collective-permute-start(f32[520,128]{1,0:T(8,128)S(1)} %slice.31), channel_id=1, source_target_pairs={{0,8},{8,16},{16,24},{24,32},{32,40},{40,48},{48,56},{56,64},{64,7... | collective-permute-start | bytes 798728 | tf_op jit(solution)/shard_map/ppermute | solution.py:392
  41.4 0.0 collective-permute-done.4
  41.4 0.0 collective-permute-done.5
  41.4 0.1 concatenate.13
  41.5 10.6 %psum.7.sums = f32[9,128]{1,0:T(8,128)S(1)} all-reduce(f32[9,128]{1,0:T(8,128)S(1)} %concatenate.13), channel_id=1, replica_groups=mesh['y'=4,'z'=16,'core'=2,'chan'=4] {'chan'}, use_global_device_ids=true, to_apply=%region_0.0 | all-reduce | flops 1152 | bytes 9216 | tf_op jit(solution)/shard_map/psum | solution.py:406
  52.1 0.0 collective-permute-done.1.below2
  52.1 0.0 collective-permute-done.3.above2
  52.1 3.5 %grid_tiles.1 = f32[64,4,8,128]{3,2,1,0:T(8,128)} custom-call(f32[520,128]{1,0:T(8,128)S(1)} %collective-permute-done.1.below2, f32[1040,128]{1,0:T(8,128)S(1)} %collective-permute-done.below1, f32[1040,128]{1,0:T(8,128)S(1)} %bitcast.9, f32[1040,128]{1,0:T(8,128)S(1)} %collective-permute-done.2.above1, f32[1040,128]{1,0:T(8,128)S(1)} %collective-permute-done.3.above2, ...), custom_call_target="tpu_custom_call" | custom-call | tf_op jit(solution)/shard_map/grid_tiles/pallas_call | solution.py:243
  55.7 10.1 %all-to-all-start.1 = ((f32[64,4,8,128]{3,2,1,0:T(8,128)}), f32[64,4,8,128]{3,2,1,0:T(8,128)S(1)}, u32[]{:S(2)}, u32[]{:S(2)}) async-start(f32[64,4,8,128]{3,2,1,0:T(8,128)} %grid_tiles.1), calls=%async_computation.1 | async-start | bytes 2097152 | tf_op jit(solution)/shard_map/all_to_all | solution.py:415
  65.7 0.3 fusion.14
  66.0 0.7 pad_maximum_fusion.1.column_waves
  66.7 1.0 fusion.6
  67.7 0.9 pad_maximum_fusion.row_waves
  68.6 7.9 %smoothing_tables.1 = (bf16[8,2,256,256]{3,2,1,0:T(8,128)(2,1)}, bf16[8,256,256]{2,1,0:T(8,128)(2,1)}) custom-call(f32[8]{0:T(128)} %sigma, f32[256,512]{1,0:T(8,128)} %pad_maximum_fusion.row_waves, f32[128,256]{1,0:T(8,128)} %pad_maximum_fusion.1.column_waves), custom_call_target="tpu_custom_call" | custom-call | flops 3221225472 | bytes 6291456 | tf_op jit(solution)/shard_map/smoothing_tables/pallas_call | solution.py:305
  76.5 40.5 %all-to-all-done.1 = f32[64,4,8,128]{3,2,1,0:T(8,128)S(1)} async-done(((f32[64,4,8,128]{3,2,1,0:T(8,128)}), f32[64,4,8,128]{3,2,1,0:T(8,128)S(1)}, u32[]{:S(2)}, u32[]{:S(2)}) %all-to-all-start.1) | async-done | bytes 1048608 | tf_op jit(solution)/shard_map/all_to_all | solution.py:415
  116.9 3.4 %smooth.1 = f32[8,256,128]{2,1,0:T(8,128)} custom-call(f32[2048,128]{1,0:T(8,128)S(1)} %bitcast.5, bf16[8,2,256,256]{3,2,1,0:T(8,128)(2,1)} %get-tuple-element.15.rows_in, bf16[8,256,256]{2,1,0:T(8,128)(2,1)} %get-tuple-element.16.columns_in), custom_call_target="tpu_custom_call" | custom-call | tf_op jit(solution)/shard_map/smooth/pallas_call | solution.py:363
  (5 shorter events, 0.0 us)
Async XLA Ops:
  8.0 26.5 %collective-permute-start.2 = (f32[1040,128]{1,0:T(8,128)S(1)}, f32[1040,128]{1,0:T(8,128)S(1)}, u32[]{:S(2)}, u32[]{:S(2)}) collective-permute-start(f32[1040,128]{1,0:T(8,128)S(1)} %bitcast.6), channel_id=1, source_target_pairs={{0,504},{8,0},{16,8},{24,16},{32,24},{40,32},{48,40},{56,48},{64,5... | collective-permute-start | bytes 1597448 | tf_op jit(solution)/shard_map/ppermute | solution.py:392
  15.4 23.4 %collective-permute-start = (f32[1040,128]{1,0:T(8,128)S(1)}, f32[1040,128]{1,0:T(8,128)S(1)}, u32[]{:S(2)}, u32[]{:S(2)}) collective-permute-start(f32[1040,128]{1,0:T(8,128)S(1)} %bitcast.7), channel_id=1, source_target_pairs={{0,8},{8,16},{16,24},{24,32},{32,40},{40,48},{48,56},{56,64},{64,7... | collective-permute-start | bytes 1597448 | tf_op jit(solution)/shard_map/ppermute | solution.py:392
  17.3 20.5 %collective-permute-start.6 = (f32[72,512]{1,0:T(8,128)}, f32[72,512]{1,0:T(8,128)S(1)}, u32[]{:S(2)}, u32[]{:S(2)}) collective-permute-start(f32[72,512]{1,0:T(8,128)} %get-tuple-element.12), channel_id=1, source_target_pairs={{0,4},{4,0},{1,5},{5,1},{2,6},{6,2},{3,7},{7,3},{8,12},{12,8},{9,1... | collective-permute-start | bytes 442376 | tf_op jit(solution)/shard_map/ppermute | solution.py:399
  19.3 22.1 %collective-permute-start.4 = (f32[1,128]{1,0:T(1,128)S(1)}, f32[1,128]{1,0:T(1,128)S(1)}, u32[]{:S(2)}, u32[]{:S(2)}) collective-permute-start(f32[1,128]{1,0:T(1,128)S(1)} %get-tuple-element.20), channel_id=1, source_target_pairs={{0,16},{8,24},{16,32},{24,40},{32,48},{40,56},{48,64},{56,72},{64,... | collective-permute-start | bytes 1544 | tf_op jit(solution)/shard_map/ppermute | solution.py:392
  22.2 19.2 %collective-permute-start.5 = (f32[2,128]{1,0:T(2,128)S(1)}, f32[2,128]{1,0:T(2,128)S(1)}, u32[]{:S(2)}, u32[]{:S(2)}) collective-permute-start(f32[2,128]{1,0:T(2,128)S(1)} %pad_maximum_fusion.2), channel_id=1, source_target_pairs={{0,496},{8,504},{16,0},{24,8},{32,16},{40,24},{48,32},{56,40},{64,... | collective-permute-start | bytes 3080 | tf_op jit(solution)/shard_map/ppermute | solution.py:392
  34.5 17.6 %collective-permute-start.3 = (f32[1040,128]{1,0:T(8,128)S(1)}, f32[1040,128]{1,0:T(8,128)S(1)}, u32[]{:S(2)}, u32[]{:S(2)}) collective-permute-start(f32[1040,128]{1,0:T(8,128)S(1)} %collective-permute-done.2.above1), channel_id=1, source_target_pairs={{0,504},{8,0},{16,8},{24,16},{32,24},{40,32},{48,40},{56,48},{64,5... | collective-permute-start | bytes 1597448 | tf_op jit(solution)/shard_map/ppermute | solution.py:392
  38.9 13.3 %collective-permute-start.1 = (f32[520,128]{1,0:T(8,128)S(1)}, f32[520,128]{1,0:T(8,128)S(1)}, u32[]{:S(2)}, u32[]{:S(2)}) collective-permute-start(f32[520,128]{1,0:T(8,128)S(1)} %slice.31), channel_id=1, source_target_pairs={{0,8},{8,16},{16,24},{24,32},{32,40},{40,48},{48,56},{56,64},{64,7... | collective-permute-start | bytes 798728 | tf_op jit(solution)/shard_map/ppermute | solution.py:392
  55.7 61.2 %all-to-all-start.1 = ((f32[64,4,8,128]{3,2,1,0:T(8,128)}), f32[64,4,8,128]{3,2,1,0:T(8,128)S(1)}, u32[]{:S(2)}, u32[]{:S(2)}) async-start(f32[64,4,8,128]{3,2,1,0:T(8,128)} %grid_tiles.1), calls=%async_computation.1 | async-start | bytes 2097152 | tf_op jit(solution)/shard_map/all_to_all | solution.py:415

commit v5 on v4

--- a/solution.py
+++ b/solution.py
@@ -272,11 +272,11 @@
     return jnp.exp(-2.0 * math.pi**2 * sigma**2 * folded**2)
 
 
-def circulant(sigma, basis):
+def circulant(sigma, basis, rows):
     length = basis.shape[0]
     return (
         lax.dot_general(
-            basis * response(sigma, length),
+            basis[0:rows] * response(sigma, length),
             basis,
             (((1,), (1,)), ((), ())),
             precision=highest,
@@ -288,14 +288,13 @@
 
 def tables_kernel(sigma, row_waves, column_waves, rows_out, columns_out):
     width = sigma[pl.program_id(0)]
-    high, low = split(circulant(width, row_waves[...]))
+    half = rows_out.shape[2]
+    high, low = split(circulant(width, row_waves[...], half))
     rows_out[0, 0] = high
     rows_out[0, 1] = low
-    high, low = split(circulant(width, column_waves[...]))
-    columns_out[0, 0:TX, 0:TX] = high
-    columns_out[0, 0:TX, TX:] = low
-    columns_out[0, TX:, 0:TX] = high
-    columns_out[0, TX:, TX:] = jnp.zeros_like(low)
+    high, low = split(circulant(width, column_waves[...], TX))
+    columns_out[0, :, 0:TX] = high
+    columns_out[0, :, TX:] = low
 
 
 def make_tables(sigma, length):
@@ -306,8 +305,8 @@
         tables_kernel,
         grid=(channels,),
         out_shape=(
-            jax.ShapeDtypeStruct((channels, 2, length, length), bf16),
-            jax.ShapeDtypeStruct((channels, 2 * TX, 2 * TX), bf16),
+            jax.ShapeDtypeStruct((channels, 2, length // 2, length), bf16),
+            jax.ShapeDtypeStruct((channels, TX, 2 * TX), bf16),
         ),
         in_specs=[
             whole(pltpu.SMEM),
@@ -315,8 +314,8 @@
             fixed((TX, 2 * TX)),
         ],
         out_specs=(
-            pl.BlockSpec((1, 2, length, length), lambda c: (c, 0, 0, 0)),
-            pl.BlockSpec((1, 2 * TX, 2 * TX), lambda c: (c, 0, 0)),
+            pl.BlockSpec((1, 2, length // 2, length), lambda c: (c, 0, 0, 0)),
+            pl.BlockSpec((1, TX, 2 * TX), lambda c: (c, 0, 0)),
         ),
         compiler_params=pltpu.CompilerParams(vmem_limit_bytes=60 << 20),
         cost_estimate=pl.CostEstimate(
@@ -330,16 +329,23 @@
     field, rows_in, columns_in, out, rows_table, columns_table, across, smoothed, here, done
 ):
     channels, length, _ = smoothed.shape
+    half = length // 2
     columns_copy = pltpu.make_async_copy(columns_in, columns_table, here.at[0])
     rows_copy = pltpu.make_async_copy(rows_in, rows_table, here.at[1])
     columns_copy.start()
     rows_copy.start()
-    columns_copy.wait()
     for c in range(channels):
         high, low = split(field[pl.ds(c, length, stride=channels), :])
-        both = jnp.dot(
-            jnp.concatenate([high, low], axis=1), columns_table[c], preferred_element_type=f32
+        across[c, :, 0:TX] = high
+        across[c, :, TX:] = low
+    columns_copy.wait()
+    none = jnp.zeros((TX, TX), bf16)
+    for c in range(channels):
+        table = columns_table[c]
+        table = jnp.concatenate(
+            [table, jnp.concatenate([table[:, 0:TX], none], axis=1)], axis=0
         )
+        both = jnp.dot(across[c], table, preferred_element_type=f32)
         high, low = split(both[:, 0:TX] + both[:, TX:])
         across[c, :, 0:TX] = high
         across[c, :, TX:] = low
@@ -348,9 +354,15 @@
     copies = []
     for number in range(GROUPS):
         for c in range(number * group, (number + 1) * group):
-            both = jnp.dot(rows_table[c, 0], across[c], preferred_element_type=f32)
-            rest = jnp.dot(rows_table[c, 1], across[c, :, 0:TX], preferred_element_type=f32)
-            smoothed[c] = both[:, 0:TX] + both[:, TX:] + rest
+            straight = across[c]
+            swapped = jnp.concatenate([straight[half:], straight[:half]], axis=0)
+            highs = jnp.concatenate([straight[:, 0:TX], swapped[:, 0:TX]], axis=1)
+            lows = jnp.concatenate([straight[:, TX:], swapped[:, TX:]], axis=1)
+            total = jnp.dot(rows_table[c, 0], highs, preferred_element_type=f32)
+            total = total + jnp.dot(rows_table[c, 0], lows, preferred_element_type=f32)
+            total = total + jnp.dot(rows_table[c, 1], highs, preferred_element_type=f32)
+            smoothed[c, 0:half, :] = total[:, 0:TX]
+            smoothed[c, half:, :] = total[:, TX:]
         part = pl.ds(number * group, group)
         copies.append(pltpu.make_async_copy(smoothed.at[part], out.at[part], done.at[number]))
         copies[-1].start()
@@ -359,7 +371,7 @@
 
 
 def smooth(field, rows_table, columns_table):
-    channels, _, length, _ = rows_table.shape
+    channels, _, _, length = rows_table.shape
     return pl.pallas_call(
         smooth_kernel,
         out_shape=jax.ShapeDtypeStruct((channels, length, TX), f32),

time: 121 us -> 120 us (level)
  the two profiles are of different devices: /device:TPU:32 before, /device:TPU:2 now
where the time goes in v5:
time: 120 us
  waiting for transfers between devices  43.1 us (36%)
  starting transfers between devices  41.3 us (34%)
  Pallas kernels  17.1 us (14%)
  blocking collectives  14.1 us (12%)
  other arithmetic  2.89 us (2%)
    all_to_all x1, waiting for transfers between devices, local(): lax.all_to_all(gridded, ('y', 'z'), split_axis=0, concat_axis=0, tiled=True)  41.4 us
    ppermute x6, starting transfers between devices, shift(): lax.ppermute(array, ('y', 'z'), [(i, (i + by) % chips) for i in range(chi...  33.1 us
    psum x1, blocking collectives, local(): sums = lax.psum(jnp.concatenate(parts, axis=0), 'chan')  8.72 us
    pallas_call x1, Pallas kernels, make_tables(): pl.pallas_call(tables_kernel, grid=(channels,), out_shape=(jax.ShapeDtype...  8.2 us
    all_to_all x1, starting transfers between devices, local(): lax.all_to_all(gridded, ('y', 'z'), split_axis=0, concat_axis=0, tiled=True)  6.28 us
    all_to_all x1, blocking collectives, local(): here = lax.all_to_all(unit, 'core', split_axis=0, concat_axis=0, tiled=True)  5.37 us
    pallas_call x1, Pallas kernels, grid_tiles(): pl.pallas_call(grid_kernel, out_shape=jax.ShapeDtypeStruct((HALF_CH // 8,...  3.5 us
    pallas_call x1, Pallas kernels, prepare(): pl.pallas_call(prepare_kernel, out_shape=(jax.ShapeDtypeStruct(unit, f32)...  2.78 us
  transfers between devices with their start and end apart: 8, of which 2 were waited for; matrix products, arithmetic and copies ran while one was open for 3% of the time, Pallas kernels for 7%

profile of v5, /device:TPU:2, one launch (start us, length us, event | category | flops | bytes accessed | tf_op | source)
XLA Modules:
  0.0 119.9 jit_solution(845017121942745339)
XLA Ops:
  0.0 2.8 %prepare.1 = (f32[2,520,128]{2,1,0:T(8,128)}, f32[72,512]{1,0:T(8,128)}) custom-call(s32[8]{0:T(128)} %counts_in.1, f32[128,1024]{1,0:T(8,128)} %spectra_in.1, s32[1,128]{1,0:T(1,128)} %bitcast.12, f32[19,1024]{1,0:T(8,128)} %feed_gain_in.1, s32[8,64]{1,0:T(8,128)} %send_list_in.1, f32[64,512]{1,0:T(8,128)} %bitcast.10, s32[1,512]{1,0:T(1,128)} %bitcast.11), custom_call_target="tpu_custom_call" | custom-call | tf_op jit(solution)/shard_map/prepare/pallas_call | solution.py:146
  2.8 0.0 copy-start.1
  2.8 5.4 %all_to_all.13 = f32[2,520,128]{2,1,0:T(8,128)S(1)} all-to-all(f32[2,520,128]{2,1,0:T(8,128)} %get-tuple-element.11), channel_id=1, replica_groups=mesh['y'=4,'z'=16,'core'=2,'chan'=4] {'core'}, dimensions={0} | all-to-all | bytes 1064960 | tf_op jit(solution)/shard_map/all_to_all | solution.py:410
  8.2 13.8 %collective-permute-start.2 = (f32[1040,128]{1,0:T(8,128)S(1)}, f32[1040,128]{1,0:T(8,128)S(1)}, u32[]{:S(2)}, u32[]{:S(2)}) collective-permute-start(f32[1040,128]{1,0:T(8,128)S(1)} %bitcast.6), channel_id=1, source_target_pairs={{0,504},{8,0},{16,8},{24,16},{32,24},{40,32},{48,40},{56,48},{64,5... | collective-permute-start | bytes 1597448 | tf_op jit(solution)/shard_map/ppermute | solution.py:404
  22.0 1.9 %collective-permute-start = (f32[1040,128]{1,0:T(8,128)S(1)}, f32[1040,128]{1,0:T(8,128)S(1)}, u32[]{:S(2)}, u32[]{:S(2)}) collective-permute-start(f32[1040,128]{1,0:T(8,128)S(1)} %bitcast.7), channel_id=1, source_target_pairs={{0,8},{8,16},{16,24},{24,32},{32,40},{40,48},{48,56},{56,64},{64,7... | collective-permute-start | bytes 1597448 | tf_op jit(solution)/shard_map/ppermute | solution.py:404
  23.9 0.0 copy-done.1
  24.0 1.9 %collective-permute-start.6 = (f32[72,512]{1,0:T(8,128)S(1)}, f32[72,512]{1,0:T(8,128)S(1)}, u32[]{:S(2)}, u32[]{:S(2)}) collective-permute-start(f32[72,512]{1,0:T(8,128)S(1)} %copy-done.1), channel_id=1, source_target_pairs={{0,4},{4,0},{1,5},{5,1},{2,6},{6,2},{3,7},{7,3},{8,12},{12,8},{9,1... | collective-permute-start | bytes 442376 | tf_op jit(solution)/shard_map/ppermute | solution.py:411
  25.9 1.9 %collective-permute-start.4 = (f32[1,128]{1,0:T(1,128)S(1)}, f32[1,128]{1,0:T(1,128)S(1)}, u32[]{:S(2)}, u32[]{:S(2)}) collective-permute-start(f32[1,128]{1,0:T(1,128)S(1)} %get-tuple-element.20), channel_id=1, source_target_pairs={{0,16},{8,24},{16,32},{24,40},{32,48},{40,56},{48,64},{56,72},{64,... | collective-permute-start | bytes 1544 | tf_op jit(solution)/shard_map/ppermute | solution.py:404
  27.8 8.1 %collective-permute-start.5 = (f32[2,128]{1,0:T(2,128)S(1)}, f32[2,128]{1,0:T(2,128)S(1)}, u32[]{:S(2)}, u32[]{:S(2)}) collective-permute-start(f32[2,128]{1,0:T(2,128)S(1)} %pad_maximum_fusion.2), channel_id=1, source_target_pairs={{0,496},{8,504},{16,0},{24,8},{32,16},{40,24},{48,32},{56,40},{64,... | collective-permute-start | bytes 3080 | tf_op jit(solution)/shard_map/ppermute | solution.py:404
  36.0 0.0 collective-permute-done.2.above1
  36.0 5.3 %collective-permute-start.3 = (f32[1040,128]{1,0:T(8,128)S(1)}, f32[1040,128]{1,0:T(8,128)S(1)}, u32[]{:S(2)}, u32[]{:S(2)}) collective-permute-start(f32[1040,128]{1,0:T(8,128)S(1)} %collective-permute-done.2.above1), channel_id=1, source_target_pairs={{0,504},{8,0},{16,8},{24,16},{32,24},{40,32},{48,40},{56,48},{64,5... | collective-permute-start | bytes 1597448 | tf_op jit(solution)/shard_map/ppermute | solution.py:404
  41.4 0.0 collective-permute-done.6
  41.4 0.0 collective-permute-done.below1
  41.4 1.9 %collective-permute-start.1 = (f32[520,128]{1,0:T(8,128)S(1)}, f32[520,128]{1,0:T(8,128)S(1)}, u32[]{:S(2)}, u32[]{:S(2)}) collective-permute-start(f32[520,128]{1,0:T(8,128)S(1)} %slice.31), channel_id=1, source_target_pairs={{0,8},{8,16},{16,24},{24,32},{32,40},{40,48},{48,56},{56,64},{64,7... | collective-permute-start | bytes 798728 | tf_op jit(solution)/shard_map/ppermute | solution.py:404
  43.4 0.0 collective-permute-done.4
  43.4 0.0 collective-permute-done.5
  43.4 0.1 concatenate.13
  43.5 8.7 %psum.7.sums = f32[9,128]{1,0:T(8,128)S(1)} all-reduce(f32[9,128]{1,0:T(8,128)S(1)} %concatenate.13), channel_id=1, replica_groups=mesh['y'=4,'z'=16,'core'=2,'chan'=4] {'chan'}, use_global_device_ids=true, to_apply=%region_0.0 | all-reduce | flops 1152 | bytes 9216 | tf_op jit(solution)/shard_map/psum | solution.py:418
  52.3 1.7 %collective-permute-done.1.below2 = f32[520,128]{1,0:T(8,128)S(1)} collective-permute-done((f32[520,128]{1,0:T(8,128)S(1)}, f32[520,128]{1,0:T(8,128)S(1)}, u32[]{:S(2)}, u32[]{:S(2)}) %collective-permute-start.1) | collective-permute-done | bytes 266272 | tf_op jit(solution)/shard_map/ppermute | solution.py:404
  54.0 0.0 collective-permute-done.3.above2
  54.0 3.5 %grid_tiles.1 = f32[64,4,8,128]{3,2,1,0:T(8,128)} custom-call(f32[520,128]{1,0:T(8,128)S(1)} %collective-permute-done.1.below2, f32[1040,128]{1,0:T(8,128)S(1)} %collective-permute-done.below1, f32[1040,128]{1,0:T(8,128)S(1)} %bitcast.9, f32[1040,128]{1,0:T(8,128)S(1)} %collective-permute-done.2.above1, f32[1040,128]{1,0:T(8,128)S(1)} %collective-permute-done.3.above2, ...), custom_call_target="tpu_custom_call" | custom-call | tf_op jit(solution)/shard_map/grid_tiles/pallas_call | solution.py:243
  57.5 6.3 %all-to-all-start.1 = ((f32[64,4,8,128]{3,2,1,0:T(8,128)}), f32[64,4,8,128]{3,2,1,0:T(8,128)S(1)}, u32[]{:S(2)}, u32[]{:S(2)}) async-start(f32[64,4,8,128]{3,2,1,0:T(8,128)} %grid_tiles.1), calls=%async_computation.1 | async-start | bytes 2097152 | tf_op jit(solution)/shard_map/all_to_all | solution.py:427
  63.8 0.3 fusion.14
  64.1 0.7 pad_maximum_fusion.1.column_waves
  64.7 1.0 fusion.6
  65.8 0.9 pad_maximum_fusion.row_waves
  66.7 8.2 %smoothing_tables.1 = (bf16[8,2,128,256]{3,2,1,0:T(8,128)(2,1)}, bf16[8,128,256]{2,1,0:T(8,128)(2,1)}) custom-call(f32[8]{0:T(128)} %sigma, f32[256,512]{1,0:T(8,128)} %pad_maximum_fusion.row_waves, f32[128,256]{1,0:T(8,128)} %pad_maximum_fusion.1.column_waves), custom_call_target="tpu_custom_call" | custom-call | flops 3221225472 | bytes 6291456 | tf_op jit(solution)/shard_map/smoothing_tables/pallas_call | solution.py:304
  74.9 41.4 %all-to-all-done.1 = f32[64,4,8,128]{3,2,1,0:T(8,128)S(1)} async-done(((f32[64,4,8,128]{3,2,1,0:T(8,128)}), f32[64,4,8,128]{3,2,1,0:T(8,128)S(1)}, u32[]{:S(2)}, u32[]{:S(2)}) %all-to-all-start.1) | async-done | bytes 1048608 | tf_op jit(solution)/shard_map/all_to_all | solution.py:427
  116.2 0.0 copy-start
  116.2 1.0 copy-done
  117.2 2.6 %smooth.1 = f32[8,256,128]{2,1,0:T(8,128)} custom-call(f32[2048,128]{1,0:T(8,128)S(1)} %bitcast.5, bf16[8,2,128,256]{3,2,1,0:T(8,128)(2,1)} %get-tuple-element.15.rows_in, bf16[8,128,256]{2,1,0:T(8,128)(2,1)S(1)} %copy-done), custom_call_target="tpu_custom_call" | custom-call | tf_op jit(solution)/shard_map/smooth/pallas_call | solution.py:375
  (6 shorter events, 0.1 us)
Async XLA Ops:
  2.8 21.2 %copy-start.1 = (f32[72,512]{1,0:T(8,128)S(1)}, f32[72,512]{1,0:T(8,128)}, u32[]{:S(2)}) copy-start(f32[72,512]{1,0:T(8,128)} %get-tuple-element.12) | copy-start | bytes 442372
  8.2 27.8 %collective-permute-start.2 = (f32[1040,128]{1,0:T(8,128)S(1)}, f32[1040,128]{1,0:T(8,128)S(1)}, u32[]{:S(2)}, u32[]{:S(2)}) collective-permute-start(f32[1040,128]{1,0:T(8,128)S(1)} %bitcast.6), channel_id=1, source_target_pairs={{0,504},{8,0},{16,8},{24,16},{32,24},{40,32},{48,40},{56,48},{64,5... | collective-permute-start | bytes 1597448 | tf_op jit(solution)/shard_map/ppermute | solution.py:404
  22.0 19.4 %collective-permute-start = (f32[1040,128]{1,0:T(8,128)S(1)}, f32[1040,128]{1,0:T(8,128)S(1)}, u32[]{:S(2)}, u32[]{:S(2)}) collective-permute-start(f32[1040,128]{1,0:T(8,128)S(1)} %bitcast.7), channel_id=1, source_target_pairs={{0,8},{8,16},{16,24},{24,32},{32,40},{40,48},{48,56},{56,64},{64,7... | collective-permute-start | bytes 1597448 | tf_op jit(solution)/shard_map/ppermute | solution.py:404
  24.0 17.4 %collective-permute-start.6 = (f32[72,512]{1,0:T(8,128)S(1)}, f32[72,512]{1,0:T(8,128)S(1)}, u32[]{:S(2)}, u32[]{:S(2)}) collective-permute-start(f32[72,512]{1,0:T(8,128)S(1)} %copy-done.1), channel_id=1, source_target_pairs={{0,4},{4,0},{1,5},{5,1},{2,6},{6,2},{3,7},{7,3},{8,12},{12,8},{9,1... | collective-permute-start | bytes 442376 | tf_op jit(solution)/shard_map/ppermute | solution.py:411
  25.9 17.5 %collective-permute-start.4 = (f32[1,128]{1,0:T(1,128)S(1)}, f32[1,128]{1,0:T(1,128)S(1)}, u32[]{:S(2)}, u32[]{:S(2)}) collective-permute-start(f32[1,128]{1,0:T(1,128)S(1)} %get-tuple-element.20), channel_id=1, source_target_pairs={{0,16},{8,24},{16,32},{24,40},{32,48},{40,56},{48,64},{56,72},{64,... | collective-permute-start | bytes 1544 | tf_op jit(solution)/shard_map/ppermute | solution.py:404
  27.8 15.6 %collective-permute-start.5 = (f32[2,128]{1,0:T(2,128)S(1)}, f32[2,128]{1,0:T(2,128)S(1)}, u32[]{:S(2)}, u32[]{:S(2)}) collective-permute-start(f32[2,128]{1,0:T(2,128)S(1)} %pad_maximum_fusion.2), channel_id=1, source_target_pairs={{0,496},{8,504},{16,0},{24,8},{32,16},{40,24},{48,32},{56,40},{64,... | collective-permute-start | bytes 3080 | tf_op jit(solution)/shard_map/ppermute | solution.py:404
  36.0 18.0 %collective-permute-start.3 = (f32[1040,128]{1,0:T(8,128)S(1)}, f32[1040,128]{1,0:T(8,128)S(1)}, u32[]{:S(2)}, u32[]{:S(2)}) collective-permute-start(f32[1040,128]{1,0:T(8,128)S(1)} %collective-permute-done.2.above1), channel_id=1, source_target_pairs={{0,504},{8,0},{16,8},{24,16},{32,24},{40,32},{48,40},{56,48},{64,5... | collective-permute-start | bytes 1597448 | tf_op jit(solution)/shard_map/ppermute | solution.py:404
  41.4 12.5 %collective-permute-start.1 = (f32[520,128]{1,0:T(8,128)S(1)}, f32[520,128]{1,0:T(8,128)S(1)}, u32[]{:S(2)}, u32[]{:S(2)}) collective-permute-start(f32[520,128]{1,0:T(8,128)S(1)} %slice.31), channel_id=1, source_target_pairs={{0,8},{8,16},{16,24},{24,32},{32,40},{40,48},{48,56},{56,64},{64,7... | collective-permute-start | bytes 798728 | tf_op jit(solution)/shard_map/ppermute | solution.py:404
  57.5 58.7 %all-to-all-start.1 = ((f32[64,4,8,128]{3,2,1,0:T(8,128)}), f32[64,4,8,128]{3,2,1,0:T(8,128)S(1)}, u32[]{:S(2)}, u32[]{:S(2)}) async-start(f32[64,4,8,128]{3,2,1,0:T(8,128)} %grid_tiles.1), calls=%async_computation.1 | async-start | bytes 2097152 | tf_op jit(solution)/shard_map/all_to_all | solution.py:427
  116.2 1.0 copy-start

commit v6 on v5

--- a/solution.py
+++ b/solution.py
@@ -23,7 +23,7 @@
 REACH = 9
 GROUPS = 8
 PARTS = 4
-VMEM_SMOOTH = 52
+VMEM_SMOOTH = 105
 VMEM_PREPARE = 56
 PIX = TY * TX
 
@@ -286,15 +286,15 @@
     )
 
 
-def tables_kernel(sigma, row_waves, column_waves, rows_out, columns_out):
+def tables_kernel(sigma, row_waves, column_waves, tables_out):
     width = sigma[pl.program_id(0)]
-    half = rows_out.shape[2]
+    half = row_waves.shape[0] // 2
     high, low = split(circulant(width, row_waves[...], half))
-    rows_out[0, 0] = high
-    rows_out[0, 1] = low
+    tables_out[0, 0:half] = high
+    tables_out[0, half : 2 * half] = low
     high, low = split(circulant(width, column_waves[...], TX))
-    columns_out[0, :, 0:TX] = high
-    columns_out[0, :, TX:] = low
+    tables_out[0, 2 * half :, 0:TX] = high
+    tables_out[0, 2 * half :, TX:] = low
 
 
 def make_tables(sigma, length):
@@ -304,19 +304,13 @@
     return pl.pallas_call(
         tables_kernel,
         grid=(channels,),
-        out_shape=(
-            jax.ShapeDtypeStruct((channels, 2, length // 2, length), bf16),
-            jax.ShapeDtypeStruct((channels, TX, 2 * TX), bf16),
-        ),
+        out_shape=jax.ShapeDtypeStruct((channels, length + TX, 2 * TX), bf16),
         in_specs=[
             whole(pltpu.SMEM),
             fixed((length, 2 * length)),
             fixed((TX, 2 * TX)),
         ],
-        out_specs=(
-            pl.BlockSpec((1, 2, length // 2, length), lambda c: (c, 0, 0, 0)),
-            pl.BlockSpec((1, TX, 2 * TX), lambda c: (c, 0, 0)),
-        ),
+        out_specs=pl.BlockSpec((1, length + TX, 2 * TX), lambda c: (c, 0, 0)),
         compiler_params=pltpu.CompilerParams(vmem_limit_bytes=60 << 20),
         cost_estimate=pl.CostEstimate(
             flops=2 * channels * 6 * 2 * length**3, bytes_accessed=6 << 20, transcendentals=0
@@ -325,13 +319,16 @@
     )(sigma, waves_rows, waves(TX))
 
 
-def smooth_kernel(
-    field, rows_in, columns_in, out, rows_table, columns_table, across, smoothed, here, done
-):
+def smooth_kernel(field, tables_in, out, tables, across, smoothed, here, done):
     channels, length, _ = smoothed.shape
     half = length // 2
-    columns_copy = pltpu.make_async_copy(columns_in, columns_table, here.at[0])
-    rows_copy = pltpu.make_async_copy(rows_in, rows_table, here.at[1])
+    rows_part, columns_part = pl.ds(0, length), pl.ds(length, TX)
+    columns_copy = pltpu.make_async_copy(
+        tables_in.at[:, columns_part], tables.at[:, columns_part], here.at[0]
+    )
+    rows_copy = pltpu.make_async_copy(
+        tables_in.at[:, rows_part], tables.at[:, rows_part], here.at[1]
+    )
     columns_copy.start()
     rows_copy.start()
     for c in range(channels):
@@ -341,7 +338,7 @@
     columns_copy.wait()
     none = jnp.zeros((TX, TX), bf16)
     for c in range(channels):
-        table = columns_table[c]
+        table = tables[c, length:, :]
         table = jnp.concatenate(
             [table, jnp.concatenate([table[:, 0:TX], none], axis=1)], axis=0
         )
@@ -358,9 +355,9 @@
             swapped = jnp.concatenate([straight[half:], straight[:half]], axis=0)
             highs = jnp.concatenate([straight[:, 0:TX], swapped[:, 0:TX]], axis=1)
             lows = jnp.concatenate([straight[:, TX:], swapped[:, TX:]], axis=1)
-            total = jnp.dot(rows_table[c, 0], highs, preferred_element_type=f32)
-            total = total + jnp.dot(rows_table[c, 0], lows, preferred_element_type=f32)
-            total = total + jnp.dot(rows_table[c, 1], highs, preferred_element_type=f32)
+            total = jnp.dot(tables[c, 0:half, :], highs, preferred_element_type=f32)
+            total = total + jnp.dot(tables[c, 0:half, :], lows, preferred_element_type=f32)
+            total = total + jnp.dot(tables[c, half:length, :], highs, preferred_element_type=f32)
             smoothed[c, 0:half, :] = total[:, 0:TX]
             smoothed[c, half:, :] = total[:, TX:]
         part = pl.ds(number * group, group)
@@ -370,24 +367,24 @@
         copy.wait()
 
 
-def smooth(field, rows_table, columns_table):
-    channels, _, _, length = rows_table.shape
+def smooth(field, tables):
+    channels, rows, _ = tables.shape
+    length = rows - TX
     return pl.pallas_call(
         smooth_kernel,
         out_shape=jax.ShapeDtypeStruct((channels, length, TX), f32),
-        in_specs=[whole(), whole(pltpu.HBM), whole(pltpu.HBM)],
+        in_specs=[whole(), whole(pltpu.HBM)],
         out_specs=whole(pltpu.HBM),
         scratch_shapes=[
-            VMEM(rows_table.shape, bf16),
-            VMEM(columns_table.shape, bf16),
+            VMEM(tables.shape, bf16),
             VMEM((channels, length, 2 * TX), bf16),
             VMEM((channels, length, TX), f32),
             pltpu.SemaphoreType.DMA((2,)),
             pltpu.SemaphoreType.DMA((GROUPS,)),
         ],
-        compiler_params=pltpu.CompilerParams(vmem_limit_bytes=VMEM_SMOOTH << 20),
+        compiler_params=pltpu.CompilerParams(vmem_limit_bytes=VMEM_SMOOTH << 19),
         name="smooth",
-    )(field, rows_table, columns_table)
+    )(field, tables)
 
 
 def sum_rows(block):
@@ -425,8 +422,8 @@
     )
     gridded, beam_width = lax.optimization_barrier((gridded, beam_width))
     relaid = lax.all_to_all(gridded, ("y", "z"), split_axis=0, concat_axis=0, tiled=True)
-    rows_table, columns_table = make_tables(beam_width, chips * CORES * TY)
-    return smooth(relaid.reshape(chips * CORES * TY * 8, TX), rows_table, columns_table)
+    tables = make_tables(beam_width, chips * CORES * TY)
+    return smooth(relaid.reshape(chips * CORES * TY * 8, TX), tables)
 
 
 def solution(mesh):

time: 120 us -> 120 us (level)
  the two profiles are of different devices: /device:TPU:2 before, /device:TPU:32 now
where the time goes in v6:
time: 120 us
  starting transfers between devices  42.3 us (35%)
  waiting for transfers between devices  40.1 us (33%)
  Pallas kernels  17.3 us (14%)
  blocking collectives  15.8 us (13%)
  other arithmetic  3.77 us (3%)
    all_to_all x1, waiting for transfers between devices, local(): lax.all_to_all(gridded, ('y', 'z'), split_axis=0, concat_axis=0, tiled=True)  40.1 us
    ppermute x6, starting transfers between devices, shift(): lax.ppermute(array, ('y', 'z'), [(i, (i + by) % chips) for i in range(chi...  30.3 us
    psum x1, blocking collectives, local(): sums = lax.psum(jnp.concatenate(parts, axis=0), 'chan')  10.6 us
    all_to_all x1, starting transfers between devices, local(): lax.all_to_all(gridded, ('y', 'z'), split_axis=0, concat_axis=0, tiled=True)  10.1 us
    pallas_call x1, Pallas kernels, make_tables(): pl.pallas_call(tables_kernel, grid=(channels,), out_shape=jax.ShapeDtypeS...  8.19 us
    all_to_all x1, blocking collectives, local(): here = lax.all_to_all(unit, 'core', split_axis=0, concat_axis=0, tiled=True)  5.24 us
    pallas_call x1, Pallas kernels, grid_tiles(): pl.pallas_call(grid_kernel, out_shape=jax.ShapeDtypeStruct((HALF_CH // 8,...  3.5 us
    pallas_call x1, Pallas kernels, smooth(): pl.pallas_call(smooth_kernel, out_shape=jax.ShapeDtypeStruct((channels, l...  2.85 us
  transfers between devices with their start and end apart: 8, of which 1 were waited for; matrix products, arithmetic and copies ran while one was open for 3% of the time, Pallas kernels for 7%

profile of v6, /device:TPU:32, one launch (start us, length us, event | category | flops | bytes accessed | tf_op | source)
XLA Modules:
  0.0 119.8 jit_solution(5458625170771822286)
XLA Ops:
  0.0 2.8 %prepare.1 = (f32[2,520,128]{2,1,0:T(8,128)}, f32[72,512]{1,0:T(8,128)}) custom-call(s32[8]{0:T(128)} %counts_in.1, f32[128,1024]{1,0:T(8,128)} %spectra_in.1, s32[1,128]{1,0:T(1,128)} %bitcast.12, f32[19,1024]{1,0:T(8,128)} %feed_gain_in.1, s32[8,64]{1,0:T(8,128)} %send_list_in.1, f32[64,512]{1,0:T(8,128)} %bitcast.10, s32[1,512]{1,0:T(1,128)} %bitcast.11), custom_call_target="tpu_custom_call" | custom-call | tf_op jit(solution)/shard_map/prepare/pallas_call | solution.py:146
  2.8 5.2 %all_to_all.13 = f32[2,520,128]{2,1,0:T(8,128)S(1)} all-to-all(f32[2,520,128]{2,1,0:T(8,128)} %get-tuple-element.9), channel_id=1, replica_groups=mesh['y'=4,'z'=16,'core'=2,'chan'=4] {'core'}, dimensions={0} | all-to-all | bytes 1064960 | tf_op jit(solution)/shard_map/all_to_all | solution.py:407
  8.0 7.4 %collective-permute-start.2 = (f32[1040,128]{1,0:T(8,128)S(1)}, f32[1040,128]{1,0:T(8,128)S(1)}, u32[]{:S(2)}, u32[]{:S(2)}) collective-permute-start(f32[1040,128]{1,0:T(8,128)S(1)} %bitcast.6), channel_id=1, source_target_pairs={{0,504},{8,0},{16,8},{24,16},{32,24},{40,32},{48,40},{56,48},{64,5... | collective-permute-start | bytes 1597448 | tf_op jit(solution)/shard_map/ppermute | solution.py:401
  15.4 1.9 %collective-permute-start = (f32[1040,128]{1,0:T(8,128)S(1)}, f32[1040,128]{1,0:T(8,128)S(1)}, u32[]{:S(2)}, u32[]{:S(2)}) collective-permute-start(f32[1040,128]{1,0:T(8,128)S(1)} %bitcast.7), channel_id=1, source_target_pairs={{0,8},{8,16},{16,24},{24,32},{32,40},{40,48},{48,56},{56,64},{64,7... | collective-permute-start | bytes 1597448 | tf_op jit(solution)/shard_map/ppermute | solution.py:401
  17.3 1.9 %collective-permute-start.6 = (f32[72,512]{1,0:T(8,128)}, f32[72,512]{1,0:T(8,128)S(1)}, u32[]{:S(2)}, u32[]{:S(2)}) collective-permute-start(f32[72,512]{1,0:T(8,128)} %get-tuple-element.10), channel_id=1, source_target_pairs={{0,4},{4,0},{1,5},{5,1},{2,6},{6,2},{3,7},{7,3},{8,12},{12,8},{9,1... | collective-permute-start | bytes 442376 | tf_op jit(solution)/shard_map/ppermute | solution.py:408
  19.3 2.9 %collective-permute-start.4 = (f32[1,128]{1,0:T(1,128)S(1)}, f32[1,128]{1,0:T(1,128)S(1)}, u32[]{:S(2)}, u32[]{:S(2)}) collective-permute-start(f32[1,128]{1,0:T(1,128)S(1)} %get-tuple-element.16), channel_id=1, source_target_pairs={{0,16},{8,24},{16,32},{24,40},{32,48},{40,56},{48,64},{56,72},{64,... | collective-permute-start | bytes 1544 | tf_op jit(solution)/shard_map/ppermute | solution.py:401
  22.2 12.2 %collective-permute-start.5 = (f32[2,128]{1,0:T(2,128)S(1)}, f32[2,128]{1,0:T(2,128)S(1)}, u32[]{:S(2)}, u32[]{:S(2)}) collective-permute-start(f32[2,128]{1,0:T(2,128)S(1)} %pad_maximum_fusion.2), channel_id=1, source_target_pairs={{0,496},{8,504},{16,0},{24,8},{32,16},{40,24},{48,32},{56,40},{64,... | collective-permute-start | bytes 3080 | tf_op jit(solution)/shard_map/ppermute | solution.py:401
  34.5 0.0 collective-permute-done.2.above1
  34.5 3.4 %collective-permute-start.3 = (f32[1040,128]{1,0:T(8,128)S(1)}, f32[1040,128]{1,0:T(8,128)S(1)}, u32[]{:S(2)}, u32[]{:S(2)}) collective-permute-start(f32[1040,128]{1,0:T(8,128)S(1)} %collective-permute-done.2.above1), channel_id=1, source_target_pairs={{0,504},{8,0},{16,8},{24,16},{32,24},{40,32},{48,40},{56,48},{64,5... | collective-permute-start | bytes 1597448 | tf_op jit(solution)/shard_map/ppermute | solution.py:401
  37.9 0.0 collective-permute-done.6
  37.9 0.9 broadcast_select_fusion
  38.8 0.0 collective-permute-done.below1
  38.9 2.5 %collective-permute-start.1 = (f32[520,128]{1,0:T(8,128)S(1)}, f32[520,128]{1,0:T(8,128)S(1)}, u32[]{:S(2)}, u32[]{:S(2)}) collective-permute-start(f32[520,128]{1,0:T(8,128)S(1)} %slice.31), channel_id=1, source_target_pairs={{0,8},{8,16},{16,24},{24,32},{32,40},{40,48},{48,56},{56,64},{64,7... | collective-permute-start | bytes 798728 | tf_op jit(solution)/shard_map/ppermute | solution.py:401
  41.4 0.0 collective-permute-done.4
  41.4 0.0 collective-permute-done.5
  41.4 0.1 concatenate.13
  41.5 10.6 %psum.7.sums = f32[9,128]{1,0:T(8,128)S(1)} all-reduce(f32[9,128]{1,0:T(8,128)S(1)} %concatenate.13), channel_id=1, replica_groups=mesh['y'=4,'z'=16,'core'=2,'chan'=4] {'chan'}, use_global_device_ids=true, to_apply=%region_0.0 | all-reduce | flops 1152 | bytes 9216 | tf_op jit(solution)/shard_map/psum | solution.py:415
  52.1 0.0 collective-permute-done.1.below2
  52.1 0.0 collective-permute-done.3.above2
  52.1 3.5 %grid_tiles.1 = f32[64,4,8,128]{3,2,1,0:T(8,128)} custom-call(f32[520,128]{1,0:T(8,128)S(1)} %collective-permute-done.1.below2, f32[1040,128]{1,0:T(8,128)S(1)} %collective-permute-done.below1, f32[1040,128]{1,0:T(8,128)S(1)} %bitcast.9, f32[1040,128]{1,0:T(8,128)S(1)} %collective-permute-done.2.above1, f32[1040,128]{1,0:T(8,128)S(1)} %collective-permute-done.3.above2, ...), custom_call_target="tpu_custom_call" | custom-call | tf_op jit(solution)/shard_map/grid_tiles/pallas_call | solution.py:243
  55.7 10.1 %all-to-all-start.1 = ((f32[64,4,8,128]{3,2,1,0:T(8,128)}), f32[64,4,8,128]{3,2,1,0:T(8,128)S(1)}, u32[]{:S(2)}, u32[]{:S(2)}) async-start(f32[64,4,8,128]{3,2,1,0:T(8,128)} %grid_tiles.1), calls=%async_computation.1 | async-start | bytes 2097152 | tf_op jit(solution)/shard_map/all_to_all | solution.py:424
  65.7 0.3 fusion.14
  66.0 0.7 pad_maximum_fusion.1.column_waves
  66.7 1.0 fusion.6
  67.7 0.9 pad_maximum_fusion.row_waves
  68.6 8.2 %smoothing_tables.1.tables_in = bf16[8,384,256]{2,1,0:T(8,128)(2,1)} custom-call(f32[8]{0:T(128)} %sigma, f32[256,512]{1,0:T(8,128)} %pad_maximum_fusion.row_waves, f32[128,256]{1,0:T(8,128)} %pad_maximum_fusion.1.column_waves), custom_call_target="tpu_custom_call" | custom-call | flops 3221225472 | bytes 6291456 | tf_op jit(solution)/shard_map/smoothing_tables/pallas_call | solution.py:304
  76.8 40.1 %all-to-all-done.1 = f32[64,4,8,128]{3,2,1,0:T(8,128)S(1)} async-done(((f32[64,4,8,128]{3,2,1,0:T(8,128)}), f32[64,4,8,128]{3,2,1,0:T(8,128)S(1)}, u32[]{:S(2)}, u32[]{:S(2)}) %all-to-all-start.1) | async-done | bytes 1048608 | tf_op jit(solution)/shard_map/all_to_all | solution.py:424
  116.9 2.9 %smooth.1 = f32[8,256,128]{2,1,0:T(8,128)} custom-call(f32[2048,128]{1,0:T(8,128)S(1)} %bitcast.5, bf16[8,384,256]{2,1,0:T(8,128)(2,1)} %smoothing_tables.1.tables_in), custom_call_target="tpu_custom_call" | custom-call | tf_op jit(solution)/shard_map/smooth/pallas_call | solution.py:373
  (5 shorter events, 0.0 us)
Async XLA Ops:
  8.0 26.5 %collective-permute-start.2 = (f32[1040,128]{1,0:T(8,128)S(1)}, f32[1040,128]{1,0:T(8,128)S(1)}, u32[]{:S(2)}, u32[]{:S(2)}) collective-permute-start(f32[1040,128]{1,0:T(8,128)S(1)} %bitcast.6), channel_id=1, source_target_pairs={{0,504},{8,0},{16,8},{24,16},{32,24},{40,32},{48,40},{56,48},{64,5... | collective-permute-start | bytes 1597448 | tf_op jit(solution)/shard_map/ppermute | solution.py:401
  15.4 23.4 %collective-permute-start = (f32[1040,128]{1,0:T(8,128)S(1)}, f32[1040,128]{1,0:T(8,128)S(1)}, u32[]{:S(2)}, u32[]{:S(2)}) collective-permute-start(f32[1040,128]{1,0:T(8,128)S(1)} %bitcast.7), channel_id=1, source_target_pairs={{0,8},{8,16},{16,24},{24,32},{32,40},{40,48},{48,56},{56,64},{64,7... | collective-permute-start | bytes 1597448 | tf_op jit(solution)/shard_map/ppermute | solution.py:401
  17.3 20.5 %collective-permute-start.6 = (f32[72,512]{1,0:T(8,128)}, f32[72,512]{1,0:T(8,128)S(1)}, u32[]{:S(2)}, u32[]{:S(2)}) collective-permute-start(f32[72,512]{1,0:T(8,128)} %get-tuple-element.10), channel_id=1, source_target_pairs={{0,4},{4,0},{1,5},{5,1},{2,6},{6,2},{3,7},{7,3},{8,12},{12,8},{9,1... | collective-permute-start | bytes 442376 | tf_op jit(solution)/shard_map/ppermute | solution.py:408
  19.3 22.1 %collective-permute-start.4 = (f32[1,128]{1,0:T(1,128)S(1)}, f32[1,128]{1,0:T(1,128)S(1)}, u32[]{:S(2)}, u32[]{:S(2)}) collective-permute-start(f32[1,128]{1,0:T(1,128)S(1)} %get-tuple-element.16), channel_id=1, source_target_pairs={{0,16},{8,24},{16,32},{24,40},{32,48},{40,56},{48,64},{56,72},{64,... | collective-permute-start | bytes 1544 | tf_op jit(solution)/shard_map/ppermute | solution.py:401
  22.2 19.2 %collective-permute-start.5 = (f32[2,128]{1,0:T(2,128)S(1)}, f32[2,128]{1,0:T(2,128)S(1)}, u32[]{:S(2)}, u32[]{:S(2)}) collective-permute-start(f32[2,128]{1,0:T(2,128)S(1)} %pad_maximum_fusion.2), channel_id=1, source_target_pairs={{0,496},{8,504},{16,0},{24,8},{32,16},{40,24},{48,32},{56,40},{64,... | collective-permute-start | bytes 3080 | tf_op jit(solution)/shard_map/ppermute | solution.py:401
  34.5 17.6 %collective-permute-start.3 = (f32[1040,128]{1,0:T(8,128)S(1)}, f32[1040,128]{1,0:T(8,128)S(1)}, u32[]{:S(2)}, u32[]{:S(2)}) collective-permute-start(f32[1040,128]{1,0:T(8,128)S(1)} %collective-permute-done.2.above1), channel_id=1, source_target_pairs={{0,504},{8,0},{16,8},{24,16},{32,24},{40,32},{48,40},{56,48},{64,5... | collective-permute-start | bytes 1597448 | tf_op jit(solution)/shard_map/ppermute | solution.py:401
  38.9 13.3 %collective-permute-start.1 = (f32[520,128]{1,0:T(8,128)S(1)}, f32[520,128]{1,0:T(8,128)S(1)}, u32[]{:S(2)}, u32[]{:S(2)}) collective-permute-start(f32[520,128]{1,0:T(8,128)S(1)} %slice.31), channel_id=1, source_target_pairs={{0,8},{8,16},{16,24},{24,32},{32,40},{40,48},{48,56},{56,64},{64,7... | collective-permute-start | bytes 798728 | tf_op jit(solution)/shard_map/ppermute | solution.py:401
  55.7 61.2 %all-to-all-start.1 = ((f32[64,4,8,128]{3,2,1,0:T(8,128)}), f32[64,4,8,128]{3,2,1,0:T(8,128)S(1)}, u32[]{:S(2)}, u32[]{:S(2)}) async-start(f32[64,4,8,128]{3,2,1,0:T(8,128)} %grid_tiles.1), calls=%async_computation.1 | async-start | bytes 2097152 | tf_op jit(solution)/shard_map/all_to_all | solution.py:424

commit v7 on v6

--- a/solution.py
+++ b/solution.py
@@ -175,10 +175,11 @@
 
 
 def grid_kernel(
-    below2, below1, here, above1, above2, sums, packed_even, packed_odd, out,
+    below2, below1, here, above1, above2, sums, packed_own, packed_other, out,
     left_high, left_low, right, dense, tiles, done,
 ):
-    for tile, pack in enumerate((packed_even, packed_odd)):
+    core = lax.axis_index("core")
+    for tile, pack in ((core, packed_own), (1 - core, packed_other)):
         weight = pack[0:KB, :]
         block = pack[KB : KB + 1, :]
         for number in range(PIX // KB):
@@ -237,7 +238,7 @@
             )
 
 
-def grid_tiles(units, sums, packed_even, packed_odd):
+def grid_tiles(units, sums, packed_own, packed_other):
     slots = BAND * CAP
     depth = REACH * SLAB
     return pl.pallas_call(
@@ -255,7 +256,7 @@
         ],
         compiler_params=pltpu.CompilerParams(vmem_limit_bytes=32 << 20),
         name="grid_tiles",
-    )(*units, sums, packed_even, packed_odd)
+    )(*units, sums, packed_own, packed_other)
 
 
 def waves(length):
@@ -413,12 +414,11 @@
     below2 = shift(below1[UNIT:], 1)
     parts = [part_below2] + [sum_rows(block) for block in (below1, here, above1)] + [part_above2]
     sums = lax.psum(jnp.concatenate(parts, axis=0), "chan")
-    even = lax.axis_index("core") == 0
     gridded = grid_tiles(
         (below2, below1, here, above1, above2),
         sums,
-        jnp.where(even, packed, packed_other),
-        jnp.where(even, packed_other, packed),
+        packed,
+        packed_other,
     )
     gridded, beam_width = lax.optimization_barrier((gridded, beam_width))
     relaid = lax.all_to_all(gridded, ("y", "z"), split_axis=0, concat_axis=0, tiled=True)

time: 120 us -> 129 us (1.075)
  waiting for transfers between devices: 40.1 us -> 45.7 us
  starting transfers between devices: 42.3 us -> 45.8 us
    ppermute x6, waiting for transfers between devices: 0.02 us -> 6.78 us  [shift(): lax.ppermute(array, ('y', 'z'), [(i, (i + by) % chips) for i in range(chi...]
    all_to_all x1, starting transfers between devices: 10.1 us -> 12.1 us  [local(): lax.all_to_all(gridded, ('y', 'z'), split_axis=0, concat_axis=0, tiled=True)]
    ppermute x6, starting transfers between devices: 30.3 us -> 31.8 us  [shift(): lax.ppermute(array, ('y', 'z'), [(i, (i + by) % chips) for i in range(chi...]
  transfers between devices with their start and end apart: 8 -> 8, of which waited for: 1 -> 2; matrix products, arithmetic and copies ran while one was open for 3% -> 2% of each run, Pallas kernels for 7% -> 6%
where the time goes in v7:
time: 129 us; the launch traced here: 128 us
  starting transfers between devices  45.8 us (36%)
  waiting for transfers between devices  45.7 us (35%)
  Pallas kernels  17.5 us (14%)
  blocking collectives  16 us (12%)
  other arithmetic  2.84 us (2%)
    all_to_all x1, waiting for transfers between devices, local(): lax.all_to_all(gridded, ('y', 'z'), split_axis=0, concat_axis=0, tiled=True)  38.9 us
    ppermute x6, starting transfers between devices, shift(): lax.ppermute(array, ('y', 'z'), [(i, (i + by) % chips) for i in range(chi...  31.8 us
    all_to_all x1, starting transfers between devices, local(): lax.all_to_all(gridded, ('y', 'z'), split_axis=0, concat_axis=0, tiled=True)  12.1 us
    psum x1, blocking collectives, local(): sums = lax.psum(jnp.concatenate(parts, axis=0), 'chan')  10.6 us
    pallas_call x1, Pallas kernels, make_tables(): pl.pallas_call(tables_kernel, grid=(channels,), out_shape=jax.ShapeDtypeS...  8.19 us
    ppermute x6, waiting for transfers between devices, shift(): lax.ppermute(array, ('y', 'z'), [(i, (i + by) % chips) for i in range(chi...  6.78 us
    all_to_all x1, blocking collectives, local(): here = lax.all_to_all(unit, 'core', split_axis=0, concat_axis=0, tiled=True)  5.37 us
    pallas_call x1, Pallas kernels, grid_tiles(): pl.pallas_call(grid_kernel, out_shape=jax.ShapeDtypeStruct((HALF_CH // 8,...  3.67 us
  transfers between devices with their start and end apart: 8, of which 2 were waited for; matrix products, arithmetic and copies ran while one was open for 2% of the time, Pallas kernels for 6%

profile of v7, /device:TPU:32, one launch (start us, length us, event | category | flops | bytes accessed | tf_op | source)
XLA Modules:
  0.0 128.1 jit_solution(11466594207525137244)
XLA Ops:
  0.0 2.8 %prepare.1 = (f32[2,520,128]{2,1,0:T(8,128)}, f32[72,512]{1,0:T(8,128)}) custom-call(s32[8]{0:T(128)} %counts_in.1, f32[128,1024]{1,0:T(8,128)} %spectra_in.1, s32[1,128]{1,0:T(1,128)} %bitcast.12, f32[19,1024]{1,0:T(8,128)} %feed_gain_in.1, s32[8,64]{1,0:T(8,128)} %send_list_in.1, f32[64,512]{1,0:T(8,128)} %bitcast.10, s32[1,512]{1,0:T(1,128)} %bitcast.11), custom_call_target="tpu_custom_call" | custom-call | tf_op jit(solution)/shard_map/prepare/pallas_call | solution.py:146
  2.8 0.0 copy-start
  2.8 5.4 %all_to_all.13 = f32[2,520,128]{2,1,0:T(8,128)S(1)} all-to-all(f32[2,520,128]{2,1,0:T(8,128)} %get-tuple-element.9), channel_id=1, replica_groups=mesh['y'=4,'z'=16,'core'=2,'chan'=4] {'core'}, dimensions={0} | all-to-all | bytes 1064960 | tf_op jit(solution)/shard_map/all_to_all | solution.py:408
  8.2 7.4 %collective-permute-start.2 = (f32[1040,128]{1,0:T(8,128)S(1)}, f32[1040,128]{1,0:T(8,128)S(1)}, u32[]{:S(2)}, u32[]{:S(2)}) collective-permute-start(f32[1040,128]{1,0:T(8,128)S(1)} %bitcast.6), channel_id=1, source_target_pairs={{0,504},{8,0},{16,8},{24,16},{32,24},{40,32},{48,40},{56,48},{64,5... | collective-permute-start | bytes 1597448 | tf_op jit(solution)/shard_map/ppermute | solution.py:402
  15.6 1.9 %collective-permute-start = (f32[1040,128]{1,0:T(8,128)S(1)}, f32[1040,128]{1,0:T(8,128)S(1)}, u32[]{:S(2)}, u32[]{:S(2)}) collective-permute-start(f32[1040,128]{1,0:T(8,128)S(1)} %bitcast.7), channel_id=1, source_target_pairs={{0,8},{8,16},{16,24},{24,32},{32,40},{40,48},{48,56},{56,64},{64,7... | collective-permute-start | bytes 1597448 | tf_op jit(solution)/shard_map/ppermute | solution.py:402
  17.5 2.9 %collective-permute-start.4 = (f32[1,128]{1,0:T(1,128)S(1)}, f32[1,128]{1,0:T(1,128)S(1)}, u32[]{:S(2)}, u32[]{:S(2)}) collective-permute-start(f32[1,128]{1,0:T(1,128)S(1)} %get-tuple-element.16), channel_id=1, source_target_pairs={{0,16},{8,24},{16,32},{24,40},{32,48},{40,56},{48,64},{56,72},{64,... | collective-permute-start | bytes 1544 | tf_op jit(solution)/shard_map/ppermute | solution.py:402
  20.4 6.8 %collective-permute-done.2.above1 = f32[1040,128]{1,0:T(8,128)S(1)} collective-permute-done((f32[1040,128]{1,0:T(8,128)S(1)}, f32[1040,128]{1,0:T(8,128)S(1)}, u32[]{:S(2)}, u32[]{:S(2)}) %collective-permute-start.2) | collective-permute-done | bytes 532512 | tf_op jit(solution)/shard_map/ppermute | solution.py:402
  27.2 8.5 %collective-permute-start.3 = (f32[1040,128]{1,0:T(8,128)S(1)}, f32[1040,128]{1,0:T(8,128)S(1)}, u32[]{:S(2)}, u32[]{:S(2)}) collective-permute-start(f32[1040,128]{1,0:T(8,128)S(1)} %collective-permute-done.2.above1), channel_id=1, source_target_pairs={{0,504},{8,0},{16,8},{24,16},{32,24},{40,32},{48,40},{56,48},{64,5... | collective-permute-start | bytes 1597448 | tf_op jit(solution)/shard_map/ppermute | solution.py:402
  35.7 7.2 %collective-permute-start.5 = (f32[2,128]{1,0:T(2,128)S(1)}, f32[2,128]{1,0:T(2,128)S(1)}, u32[]{:S(2)}, u32[]{:S(2)}) collective-permute-start(f32[2,128]{1,0:T(2,128)S(1)} %pad_maximum_fusion.2), channel_id=1, source_target_pairs={{0,496},{8,504},{16,0},{24,8},{32,16},{40,24},{48,32},{56,40},{64,... | collective-permute-start | bytes 3080 | tf_op jit(solution)/shard_map/ppermute | solution.py:402
  42.8 1.9 %collective-permute-start.6 = (f32[72,512]{1,0:T(8,128)}, f32[72,512]{1,0:T(8,128)S(1)}, u32[]{:S(2)}, u32[]{:S(2)}) collective-permute-start(f32[72,512]{1,0:T(8,128)} %get-tuple-element.10.packed_own), channel_id=1, source_target_pairs={{0,4},{4,0},{1,5},{5,1},{2,6},{6,2},{3,7},{7,3},{8,12},{12,8},{9,1... | collective-permute-start | bytes 442376 | tf_op jit(solution)/shard_map/ppermute | solution.py:409
  44.8 0.0 collective-permute-done.below1
  44.8 3.9 %collective-permute-start.1 = (f32[520,128]{1,0:T(8,128)S(1)}, f32[520,128]{1,0:T(8,128)S(1)}, u32[]{:S(2)}, u32[]{:S(2)}) collective-permute-start(f32[520,128]{1,0:T(8,128)S(1)} %slice.31), channel_id=1, source_target_pairs={{0,8},{8,16},{16,24},{24,32},{32,40},{40,48},{48,56},{56,64},{64,7... | collective-permute-start | bytes 798728 | tf_op jit(solution)/shard_map/ppermute | solution.py:402
  48.8 0.0 collective-permute-done.4
  48.8 0.0 collective-permute-done.5
  48.8 0.1 concatenate.13
  48.9 10.6 %psum.7.sums = f32[9,128]{1,0:T(8,128)S(1)} all-reduce(f32[9,128]{1,0:T(8,128)S(1)} %concatenate.13), channel_id=1, replica_groups=mesh['y'=4,'z'=16,'core'=2,'chan'=4] {'chan'}, use_global_device_ids=true, to_apply=%region_0.0 | all-reduce | flops 1152 | bytes 9216 | tf_op jit(solution)/shard_map/psum | solution.py:416
  59.5 0.0 collective-permute-done.6.packed_other
  59.5 0.0 collective-permute-done.1.below2
  59.5 0.0 collective-permute-done.3.above2
  59.6 0.0 copy-done
  59.6 3.7 %grid_tiles.1 = f32[64,4,8,128]{3,2,1,0:T(8,128)} custom-call(f32[520,128]{1,0:T(8,128)S(1)} %collective-permute-done.1.below2, f32[1040,128]{1,0:T(8,128)S(1)} %collective-permute-done.below1, f32[1040,128]{1,0:T(8,128)S(1)} %bitcast.9, f32[1040,128]{1,0:T(8,128)S(1)} %collective-permute-done.2.above1, f32[1040,128]{1,0:T(8,128)S(1)} %collective-permute-done.3.above2, ...), custom_call_target="tpu_custom_call" | custom-call | tf_op jit(solution)/shard_map/grid_tiles/pallas_call | solution.py:244
  63.2 12.1 %all-to-all-start.1 = ((f32[64,4,8,128]{3,2,1,0:T(8,128)}), f32[64,4,8,128]{3,2,1,0:T(8,128)S(1)}, u32[]{:S(2)}, u32[]{:S(2)}) async-start(f32[64,4,8,128]{3,2,1,0:T(8,128)} %grid_tiles.1), calls=%async_computation.1 | async-start | bytes 2097152 | tf_op jit(solution)/shard_map/all_to_all | solution.py:424
  75.3 0.3 fusion.14
  75.6 0.7 pad_maximum_fusion.1.column_waves
  76.3 1.0 fusion.6
  77.3 0.9 pad_maximum_fusion.row_waves
  78.2 8.2 %smoothing_tables.1.tables_in = bf16[8,384,256]{2,1,0:T(8,128)(2,1)} custom-call(f32[8]{0:T(128)} %sigma, f32[256,512]{1,0:T(8,128)} %pad_maximum_fusion.row_waves, f32[128,256]{1,0:T(8,128)} %pad_maximum_fusion.1.column_waves), custom_call_target="tpu_custom_call" | custom-call | flops 3221225472 | bytes 6291456 | tf_op jit(solution)/shard_map/smoothing_tables/pallas_call | solution.py:305
  86.4 38.9 %all-to-all-done.1 = f32[64,4,8,128]{3,2,1,0:T(8,128)S(1)} async-done(((f32[64,4,8,128]{3,2,1,0:T(8,128)}), f32[64,4,8,128]{3,2,1,0:T(8,128)S(1)}, u32[]{:S(2)}, u32[]{:S(2)}) %all-to-all-start.1) | async-done | bytes 1048608 | tf_op jit(solution)/shard_map/all_to_all | solution.py:424
  125.2 2.9 %smooth.1 = f32[8,256,128]{2,1,0:T(8,128)} custom-call(f32[2048,128]{1,0:T(8,128)S(1)} %bitcast.5, bf16[8,384,256]{2,1,0:T(8,128)(2,1)} %smoothing_tables.1.tables_in), custom_call_target="tpu_custom_call" | custom-call | tf_op jit(solution)/shard_map/smooth/pallas_call | solution.py:374
  (5 shorter events, 0.0 us)
Async XLA Ops:
  2.8 56.8 %copy-start = (f32[72,512]{1,0:T(8,128)S(1)}, f32[72,512]{1,0:T(8,128)}, u32[]{:S(2)}) copy-start(f32[72,512]{1,0:T(8,128)} %get-tuple-element.10.packed_own) | copy-start | bytes 442372
  8.2 19.0 %collective-permute-start.2 = (f32[1040,128]{1,0:T(8,128)S(1)}, f32[1040,128]{1,0:T(8,128)S(1)}, u32[]{:S(2)}, u32[]{:S(2)}) collective-permute-start(f32[1040,128]{1,0:T(8,128)S(1)} %bitcast.6), channel_id=1, source_target_pairs={{0,504},{8,0},{16,8},{24,16},{32,24},{40,32},{48,40},{56,48},{64,5... | collective-permute-start | bytes 1597448 | tf_op jit(solution)/shard_map/ppermute | solution.py:402
  15.6 29.2 %collective-permute-start = (f32[1040,128]{1,0:T(8,128)S(1)}, f32[1040,128]{1,0:T(8,128)S(1)}, u32[]{:S(2)}, u32[]{:S(2)}) collective-permute-start(f32[1040,128]{1,0:T(8,128)S(1)} %bitcast.7), channel_id=1, source_target_pairs={{0,8},{8,16},{16,24},{24,32},{32,40},{40,48},{48,56},{56,64},{64,7... | collective-permute-start | bytes 1597448 | tf_op jit(solution)/shard_map/ppermute | solution.py:402
  17.5 31.3 %collective-permute-start.4 = (f32[1,128]{1,0:T(1,128)S(1)}, f32[1,128]{1,0:T(1,128)S(1)}, u32[]{:S(2)}, u32[]{:S(2)}) collective-permute-start(f32[1,128]{1,0:T(1,128)S(1)} %get-tuple-element.16), channel_id=1, source_target_pairs={{0,16},{8,24},{16,32},{24,40},{32,48},{40,56},{48,64},{56,72},{64,... | collective-permute-start | bytes 1544 | tf_op jit(solution)/shard_map/ppermute | solution.py:402
  27.2 32.4 %collective-permute-start.3 = (f32[1040,128]{1,0:T(8,128)S(1)}, f32[1040,128]{1,0:T(8,128)S(1)}, u32[]{:S(2)}, u32[]{:S(2)}) collective-permute-start(f32[1040,128]{1,0:T(8,128)S(1)} %collective-permute-done.2.above1), channel_id=1, source_target_pairs={{0,504},{8,0},{16,8},{24,16},{32,24},{40,32},{48,40},{56,48},{64,5... | collective-permute-start | bytes 1597448 | tf_op jit(solution)/shard_map/ppermute | solution.py:402
  35.7 13.1 %collective-permute-start.5 = (f32[2,128]{1,0:T(2,128)S(1)}, f32[2,128]{1,0:T(2,128)S(1)}, u32[]{:S(2)}, u32[]{:S(2)}) collective-permute-start(f32[2,128]{1,0:T(2,128)S(1)} %pad_maximum_fusion.2), channel_id=1, source_target_pairs={{0,496},{8,504},{16,0},{24,8},{32,16},{40,24},{48,32},{56,40},{64,... | collective-permute-start | bytes 3080 | tf_op jit(solution)/shard_map/ppermute | solution.py:402
  42.8 16.7 %collective-permute-start.6 = (f32[72,512]{1,0:T(8,128)}, f32[72,512]{1,0:T(8,128)S(1)}, u32[]{:S(2)}, u32[]{:S(2)}) collective-permute-start(f32[72,512]{1,0:T(8,128)} %get-tuple-element.10.packed_own), channel_id=1, source_target_pairs={{0,4},{4,0},{1,5},{5,1},{2,6},{6,2},{3,7},{7,3},{8,12},{12,8},{9,1... | collective-permute-start | bytes 442376 | tf_op jit(solution)/shard_map/ppermute | solution.py:409
  44.8 14.7 %collective-permute-start.1 = (f32[520,128]{1,0:T(8,128)S(1)}, f32[520,128]{1,0:T(8,128)S(1)}, u32[]{:S(2)}, u32[]{:S(2)}) collective-permute-start(f32[520,128]{1,0:T(8,128)S(1)} %slice.31), channel_id=1, source_target_pairs={{0,8},{8,16},{16,24},{24,32},{32,40},{40,48},{48,56},{56,64},{64,7... | collective-permute-start | bytes 798728 | tf_op jit(solution)/shard_map/ppermute | solution.py:402
  63.2 62.0 %all-to-all-start.1 = ((f32[64,4,8,128]{3,2,1,0:T(8,128)}), f32[64,4,8,128]{3,2,1,0:T(8,128)S(1)}, u32[]{:S(2)}, u32[]{:S(2)}) async-start(f32[64,4,8,128]{3,2,1,0:T(8,128)} %grid_tiles.1), calls=%async_computation.1 | async-start | bytes 2097152 | tf_op jit(solution)/shard_map/all_to_all | solution.py:424
